TPU v7x, 32 devices: a whole 2x2x4 slice. The times are simulated.
32 devices in a mesh: ctx: 8 (over z, x), fsdp: 4 (over y, core).
Axes of the slice: x: 2, y: 2, z: 4, core: 2. Of those that a mesh axis runs over, the one named last changes fastest.
Arguments:
- inputs: bfloat16 [5120, 2304], P(('ctx', 'fsdp')), may hold values from -6 to 6
- cotangent: bfloat16 [5120, 2304], P(('ctx', 'fsdp')), may hold values from -6 to 6
- w_query: bfloat16 [2304, 2048], P(('ctx', 'fsdp')), may hold values from -0.25 to 0.25
- w_key: bfloat16 [2304, 1024], P(('ctx', 'fsdp')), may hold values from -0.125 to 0.125
- w_value: bfloat16 [2304, 1024], P(('ctx', 'fsdp')), may hold values from -0.125 to 0.125
- w_out_t: bfloat16 [2304, 2048], P(('ctx', 'fsdp')), may hold values from -0.125 to 0.125
- w_gate: bfloat16 [2304, 9216], P(('ctx', 'fsdp')), may hold values from -0.125 to 0.125
- w_up: bfloat16 [2304, 9216], P(('ctx', 'fsdp')), may hold values from -0.125 to 0.125
- w_down_t: bfloat16 [2304, 9216], P(('ctx', 'fsdp')), may hold values from -0.0625 to 0.0625
- gain_attn_in: bfloat16 [2304], P(('ctx', 'fsdp')), may hold values from 0.25 to 1.75
- gain_attn_out: bfloat16 [2304], P(('ctx', 'fsdp')), may hold values from 0.25 to 1.75
- gain_mlp_in: bfloat16 [2304], P(('ctx', 'fsdp')), may hold values from 0.25 to 1.75
- gain_mlp_out: bfloat16 [2304], P(('ctx', 'fsdp')), may hold values from 0.25 to 1.75
Outputs:
- output: bfloat16 [5120, 2304], P(('ctx', 'fsdp'))
- input_grad: bfloat16 [5120, 2304], P(('ctx', 'fsdp'))
- grad_query: float32 [2304, 2048], P(('ctx', 'fsdp'))
- grad_key: float32 [2304, 1024], P(('ctx', 'fsdp'))
- grad_value: float32 [2304, 1024], P(('ctx', 'fsdp'))
- grad_out_t: float32 [2304, 2048], P(('ctx', 'fsdp'))
- grad_gate: float32 [2304, 9216], P(('ctx', 'fsdp'))
- grad_up: float32 [2304, 9216], P(('ctx', 'fsdp'))
- grad_down_t: float32 [2304, 9216], P(('ctx', 'fsdp'))
- grad_gain_attn_in: float32 [2304], P(('ctx', 'fsdp'))
- grad_gain_attn_out: float32 [2304], P(('ctx', 'fsdp'))
- grad_gain_mlp_in: float32 [2304], P(('ctx', 'fsdp'))
- grad_gain_mlp_out: float32 [2304], P(('ctx', 'fsdp'))
All inputs are finite; a program needn't handle non-finite values.
Results may differ from a plain program's by a relative error of at most 0.023.
Values may be sent and summed in bfloat16 or wider, within the bound.
No kernel may reach another device: no remote copies, remote signals or barrier semaphores. Data moves between devices by JAX's collectives and lax.ppermute only.
A program may use at most 320 MiB of HBM per device.

v0:
```python
import jax
import jax.numpy as jnp
from jax import lax
from jax.sharding import PartitionSpec as P

HEADS = 8
KV_HEADS = 4
HEAD = 256
WINDOW = 4096
CAP = 10


epsilon = 1e-06
masked_value = -1e30


def shifted(value, axis, steps):
    count = lax.axis_size(axis)
    first, last = (max(0, -steps), min(count, count - steps))
    return lax.ppermute(value, axis, [(source, source + steps) for source in range(first, last)])


def normed(values, weights):
    scaling = lax.rsqrt(jnp.mean(values * values, axis=-1, keepdims=True) + epsilon)
    return values * scaling * weights


def rotary_tables(positions, head_width):
    halfway = head_width // 2
    frequency = 10000.0 ** (-jnp.arange(halfway, dtype=jnp.float32) * 2.0 / head_width)
    angles = positions.astype(jnp.float32)[:, None] * frequency[None, :]
    return (jnp.cos(angles)[:, None, :], jnp.sin(angles)[:, None, :])


def rotate(values, cosine, sine_value):
    halfway = values.shape[-1] // 2
    leading = values[..., :halfway]
    trailing = values[..., halfway:]
    return jnp.concatenate(
        [leading * cosine - trailing * sine_value, trailing * cosine + leading * sine_value],
        axis=-1,
    )


def rotate_back(grads_in, cosine, sine_value):
    halfway = grads_in.shape[-1] // 2
    leading = grads_in[..., :halfway]
    trailing = grads_in[..., halfway:]
    return jnp.concatenate(
        [leading * cosine + trailing * sine_value, trailing * cosine - leading * sine_value],
        axis=-1,
    )


def contract_last(left_side, right_side):
    return lax.dot_general(
        left_side, right_side, (((1,), (1,)), ((), ())), preferred_element_type=jnp.float32
    )


def column_term(left_side, right_side):
    return lax.dot_general(
        left_side, right_side, (((0,), (0,)), ((), ())), preferred_element_type=jnp.float32
    )


def gelu_tanh(values):
    return jax.nn.gelu(values, approximate=True)


def split_columns(summed, widths):
    pieces = []
    offset_now = 0
    for width_now in widths:
        pieces.append(summed[:, offset_now : offset_now + width_now])
        offset_now = offset_now + width_now
    return pieces


def window_pass(own_pair, reach_blocks):
    window_list = [own_pair]
    for hop_index in range(reach_blocks):
        window_list.insert(0, shifted(window_list[0], "ctx", 1))
    return jnp.stack(window_list, axis=1)


def window_return(d_window, reach_blocks):
    carried = d_window[:, 0]
    for hop_index in range(1, reach_blocks + 1):
        carried = (
            shifted(carried.astype(jnp.bfloat16), "ctx", -1).astype(carried.dtype)
            + d_window[:, hop_index]
        )
    return carried


def scores_of(query_head, key_head, allowed):
    raw_scores = jnp.einsum(
        "rgd,kd->grk", query_head, key_head, preferred_element_type=jnp.float32
    ) * HEAD ** (-0.5)
    capped = CAP * jnp.tanh(raw_scores / CAP)
    masked = jnp.where(allowed[None], capped, masked_value)
    return (capped, masked)


def attention_forward(query_heads, keys_heads, values_heads, allowed):

    def forward_head(entries):
        query_head, key_head, value_head = entries
        capped, masked = scores_of(query_head, key_head, allowed)
        highest = jnp.max(masked, axis=-1, keepdims=True)
        totals = jnp.sum(jnp.exp(masked - highest), axis=-1, keepdims=True)
        log_total = highest + jnp.log(totals)
        soft_b = jnp.exp(masked - log_total).astype(jnp.bfloat16)
        head_out = jnp.einsum("grk,kd->rgd", soft_b, value_head, preferred_element_type=jnp.float32)
        return (head_out, log_total)

    return lax.map(forward_head, (query_heads, keys_heads, values_heads))


def attention_backward(query_heads, keys_heads, values_heads, log_totals, d_heads, allowed):

    def backward_head(entries):
        query_head, key_head, value_head, log_total, d_head = entries
        capped, masked = scores_of(query_head, key_head, allowed)
        soft_f = jnp.exp(masked - log_total)
        d_prob = jnp.einsum("rgd,kd->grk", d_head, value_head, preferred_element_type=jnp.float32)
        inner = jnp.sum(soft_f * d_prob, axis=-1, keepdims=True)
        tanh_part = capped / CAP
        d_raw_b = (soft_f * (d_prob - inner) * (1.0 - tanh_part * tanh_part)).astype(jnp.bfloat16)
        d_query_head = jnp.einsum(
            "grk,kd->rgd", d_raw_b, key_head, preferred_element_type=jnp.float32
        ) * HEAD ** (-0.5)
        d_key_head = jnp.einsum(
            "grk,rgd->kd", d_raw_b, query_head, preferred_element_type=jnp.float32
        ) * HEAD ** (-0.5)
        d_value_head = jnp.einsum(
            "grk,rgd->kd", soft_f.astype(jnp.bfloat16), d_head, preferred_element_type=jnp.float32
        )
        return (d_query_head, d_key_head, d_value_head)

    return lax.map(backward_head, (query_heads, keys_heads, values_heads, log_totals, d_heads))


def body(
    inputs,
    cotangent,
    w_query,
    w_key,
    w_value,
    w_out_t,
    w_gate,
    w_up,
    w_down_t,
    gain_attn_in,
    gain_attn_out,
    gain_mlp_in,
    gain_mlp_out,
):
    tok_rows = inputs.shape[0]
    members = lax.axis_size("fsdp")
    block_len = tok_rows * members
    reach_blocks = (WINDOW + block_len - 2) // block_len
    span_len = (reach_blocks + 1) * block_len
    group_size = HEADS // KV_HEADS
    ctx_place = lax.axis_index("ctx")
    key_pos = (ctx_place - reach_blocks) * block_len + jnp.arange(span_len, dtype=jnp.int32)
    source = inputs.astype(jnp.float32)
    grad_top = cotangent.astype(jnp.float32)
    gain_tiles = jnp.tile(
        jnp.stack([gain_attn_in, gain_attn_out, gain_mlp_in, gain_mlp_out], axis=1), (1, members)
    )
    swapped = (
        lax.all_to_all(w_query, "fsdp", split_axis=1, concat_axis=0, tiled=True),
        lax.all_to_all(w_key, "fsdp", split_axis=1, concat_axis=0, tiled=True),
        lax.all_to_all(w_value, "fsdp", split_axis=1, concat_axis=0, tiled=True),
        lax.all_to_all(w_out_t, "fsdp", split_axis=1, concat_axis=0, tiled=True),
        lax.all_to_all(w_gate, "fsdp", split_axis=1, concat_axis=0, tiled=True),
        lax.all_to_all(w_up, "fsdp", split_axis=1, concat_axis=0, tiled=True),
        lax.all_to_all(w_down_t, "fsdp", split_axis=1, concat_axis=0, tiled=True),
        lax.all_to_all(gain_tiles, "fsdp", split_axis=1, concat_axis=0, tiled=True),
    )
    gathered = (
        lax.all_gather(swapped[0], "ctx", axis=0, tiled=True),
        lax.all_gather(swapped[1], "ctx", axis=0, tiled=True),
        lax.all_gather(swapped[2], "ctx", axis=0, tiled=True),
        lax.all_gather(swapped[3], "ctx", axis=0, tiled=True),
        lax.all_gather(swapped[4], "ctx", axis=0, tiled=True),
        lax.all_gather(swapped[5], "ctx", axis=0, tiled=True),
        lax.all_gather(swapped[6], "ctx", axis=0, tiled=True),
        lax.all_gather(swapped[7], "ctx", axis=0, tiled=True),
    )
    gain_table = gathered[7].astype(jnp.float32)
    gain_list = [gain_table[:, 0], gain_table[:, 1], gain_table[:, 2], gain_table[:, 3]]
    here_pos = ctx_place * block_len + jnp.arange(block_len, dtype=jnp.int32)

    def widen(values):
        return lax.all_gather(values, "fsdp", axis=0, tiled=True)

    def narrow(values):
        return lax.psum_scatter(values, "fsdp", scatter_dimension=0, tiled=True)

    query_w, key_w, value_w, out_w, gate_w, up_w, down_w = gathered[:7]
    here_rows = here_pos.shape[0]
    q_here = query_w.shape[1] // HEAD
    kv_here = key_w.shape[1] // HEAD
    kv_cols = kv_here * HEAD
    allowed = (
        (key_pos[None, :] <= here_pos[:, None])
        & (here_pos[:, None] - key_pos[None, :] < WINDOW)
        & (key_pos[None, :] >= 0)
    )
    cosine, sine_value = rotary_tables(here_pos, HEAD)
    attn_in, attn_in_pull = jax.vjp(normed, source, gain_list[0])
    attn_in_b = widen(attn_in.astype(jnp.bfloat16))
    query_raw = jnp.dot(attn_in_b, query_w, preferred_element_type=jnp.float32).reshape(
        here_rows, q_here, HEAD
    )
    query_b = rotate(query_raw, cosine, sine_value).astype(jnp.bfloat16)
    key_raw = jnp.dot(attn_in_b, key_w, preferred_element_type=jnp.float32).reshape(
        here_rows, kv_here, HEAD
    )
    key_b = rotate(key_raw, cosine, sine_value).astype(jnp.bfloat16).reshape(here_rows, kv_cols)
    value_b = jnp.dot(attn_in_b, value_w, preferred_element_type=jnp.float32).astype(jnp.bfloat16)
    own_pair = jnp.stack([key_b, value_b])
    window_parts = window_pass(own_pair, reach_blocks)
    kv_window = window_parts.reshape(2, span_len, kv_cols)
    keys_heads = kv_window[0].reshape(span_len, kv_here, HEAD).transpose(1, 0, 2)
    values_heads = kv_window[1].reshape(span_len, kv_here, HEAD).transpose(1, 0, 2)
    query_heads = query_b.reshape(here_rows, kv_here, group_size, HEAD).transpose(1, 0, 2, 3)
    head_outs, log_totals = attention_forward(query_heads, keys_heads, values_heads, allowed)
    attended_b = (
        head_outs.transpose(1, 0, 2, 3).reshape(here_rows, q_here * HEAD).astype(jnp.bfloat16)
    )
    projected = narrow(contract_last(attended_b, out_w))
    post_attn, post_attn_pull = jax.vjp(normed, projected, gain_list[1])
    hidden = source + post_attn
    mlp_in, mlp_in_pull = jax.vjp(normed, hidden, gain_list[2])
    mlp_in_b = widen(mlp_in.astype(jnp.bfloat16))
    gate_b = jnp.dot(mlp_in_b, gate_w, preferred_element_type=jnp.float32).astype(jnp.bfloat16)
    up_b = jnp.dot(mlp_in_b, up_w, preferred_element_type=jnp.float32).astype(jnp.bfloat16)
    up_f = up_b.astype(jnp.float32)
    activated, activated_pull = jax.vjp(gelu_tanh, gate_b.astype(jnp.float32))
    mixed_b = (activated * up_f).astype(jnp.bfloat16)
    reduced = narrow(contract_last(mixed_b, down_w))
    post_mlp, post_mlp_pull = jax.vjp(normed, reduced, gain_list[3])
    output = (hidden + post_mlp).astype(jnp.bfloat16)
    d_reduced, grad_gain_mlp_out = post_mlp_pull(grad_top)
    d_reduced_b = widen(d_reduced.astype(jnp.bfloat16))
    d_mixed = jnp.dot(d_reduced_b, down_w, preferred_element_type=jnp.float32)
    (d_gate,) = activated_pull(d_mixed * up_f)
    d_gate_b = d_gate.astype(jnp.bfloat16)
    d_up_b = (d_mixed * activated).astype(jnp.bfloat16)
    d_mlp_in = narrow(contract_last(d_gate_b, gate_w) + contract_last(d_up_b, up_w))
    d_hid, grad_gain_mlp_in = mlp_in_pull(d_mlp_in)
    d_hidden = grad_top + d_hid
    d_projected, grad_gain_attn_out = post_attn_pull(d_hidden)
    d_projected_b = widen(d_projected.astype(jnp.bfloat16))
    d_attended_b = jnp.dot(d_projected_b, out_w, preferred_element_type=jnp.float32).astype(
        jnp.bfloat16
    )
    d_att_heads = d_attended_b.reshape(here_rows, kv_here, group_size, HEAD).transpose(1, 0, 2, 3)
    d_query_heads, d_key_heads, d_value_heads = attention_backward(
        query_heads, keys_heads, values_heads, log_totals, d_att_heads, allowed
    )
    d_window = jnp.stack(
        [
            d_key_heads.transpose(1, 0, 2).reshape(span_len, kv_cols),
            d_value_heads.transpose(1, 0, 2).reshape(span_len, kv_cols),
        ]
    ).reshape(2, reach_blocks + 1, block_len, kv_cols)
    own_grads = window_return(d_window, reach_blocks)
    d_key_b = (
        rotate_back(own_grads[0].reshape(here_rows, kv_here, HEAD), cosine, sine_value)
        .reshape(here_rows, kv_cols)
        .astype(jnp.bfloat16)
    )
    d_value_b = own_grads[1].astype(jnp.bfloat16)
    d_query_b = (
        rotate_back(
            d_query_heads.transpose(1, 0, 2, 3).reshape(here_rows, q_here, HEAD), cosine, sine_value
        )
        .reshape(here_rows, q_here * HEAD)
        .astype(jnp.bfloat16)
    )
    d_attn_in = narrow(
        contract_last(d_query_b, query_w)
        + contract_last(d_key_b, key_w)
        + contract_last(d_value_b, value_w)
    )
    d_source, grad_gain_attn_in = attn_in_pull(d_attn_in)
    input_grad = (d_hidden + d_source).astype(jnp.bfloat16)
    attn_summed = lax.psum_scatter(
        jnp.concatenate(
            [
                column_term(attn_in_b, d_query_b),
                column_term(attn_in_b, d_key_b),
                column_term(attn_in_b, d_value_b),
                column_term(d_projected_b, attended_b),
            ],
            axis=1,
        ).astype(jnp.bfloat16),
        "ctx",
        scatter_dimension=0,
        tiled=True,
    ).astype(jnp.float32)
    gate_summed = lax.psum_scatter(
        column_term(mlp_in_b, d_gate_b).astype(jnp.bfloat16), "ctx", scatter_dimension=0, tiled=True
    ).astype(jnp.float32)
    up_summed = lax.psum_scatter(
        column_term(mlp_in_b, d_up_b).astype(jnp.bfloat16), "ctx", scatter_dimension=0, tiled=True
    ).astype(jnp.float32)
    down_summed = lax.psum_scatter(
        column_term(d_reduced_b, mixed_b).astype(jnp.bfloat16),
        "ctx",
        scatter_dimension=0,
        tiled=True,
    ).astype(jnp.float32)
    parts = split_columns(attn_summed, [q_here * HEAD, kv_cols, kv_cols, q_here * HEAD])
    pieces = (
        lax.all_to_all(
            parts[0].astype(jnp.bfloat16), "fsdp", split_axis=0, concat_axis=1, tiled=True
        ).astype(jnp.float32),
        lax.all_to_all(
            parts[1].astype(jnp.bfloat16), "fsdp", split_axis=0, concat_axis=1, tiled=True
        ).astype(jnp.float32),
        lax.all_to_all(
            parts[2].astype(jnp.bfloat16), "fsdp", split_axis=0, concat_axis=1, tiled=True
        ).astype(jnp.float32),
        lax.all_to_all(
            parts[3].astype(jnp.bfloat16), "fsdp", split_axis=0, concat_axis=1, tiled=True
        ).astype(jnp.float32),
        lax.all_to_all(
            gate_summed.astype(jnp.bfloat16), "fsdp", split_axis=0, concat_axis=1, tiled=True
        ).astype(gate_summed.dtype),
        lax.all_to_all(
            up_summed.astype(jnp.bfloat16), "fsdp", split_axis=0, concat_axis=1, tiled=True
        ).astype(up_summed.dtype),
        lax.all_to_all(
            down_summed.astype(jnp.bfloat16), "fsdp", split_axis=0, concat_axis=1, tiled=True
        ).astype(down_summed.dtype),
    )
    gain_grads = (
        lax.psum_scatter(grad_gain_attn_in, ("ctx", "fsdp"), scatter_dimension=0, tiled=True),
        lax.psum_scatter(grad_gain_attn_out, ("ctx", "fsdp"), scatter_dimension=0, tiled=True),
        lax.psum_scatter(grad_gain_mlp_in, ("ctx", "fsdp"), scatter_dimension=0, tiled=True),
        lax.psum_scatter(grad_gain_mlp_out, ("ctx", "fsdp"), scatter_dimension=0, tiled=True),
    )
    return (
        output,
        input_grad,
        pieces[0],
        pieces[1],
        pieces[2],
        pieces[3],
        pieces[4],
        pieces[5],
        pieces[6],
        gain_grads[0],
        gain_grads[1],
        gain_grads[2],
        gain_grads[3],
    )


def solution(mesh):
    placed = (
        P(("ctx", "fsdp"), None),
        P(("ctx", "fsdp"), None),
        P(("ctx", "fsdp"), None),
        P(("ctx", "fsdp"), None),
        P(("ctx", "fsdp"), None),
        P(("ctx", "fsdp"), None),
        P(("ctx", "fsdp"), None),
        P(("ctx", "fsdp"), None),
        P(("ctx", "fsdp"), None),
        P(("ctx", "fsdp")),
        P(("ctx", "fsdp")),
        P(("ctx", "fsdp")),
        P(("ctx", "fsdp")),
    )
    return jax.shard_map(
        body,
        mesh=mesh,
        in_specs=placed,
        out_specs=(
            P(("ctx", "fsdp"), None),
            P(("ctx", "fsdp"), None),
            P(("ctx", "fsdp"), None),
            P(("ctx", "fsdp"), None),
            P(("ctx", "fsdp"), None),
            P(("ctx", "fsdp"), None),
            P(("ctx", "fsdp"), None),
            P(("ctx", "fsdp"), None),
            P(("ctx", "fsdp"), None),
            P(("ctx", "fsdp")),
            P(("ctx", "fsdp")),
            P(("ctx", "fsdp")),
            P(("ctx", "fsdp")),
        ),
        check_vma=False,
    )
```

profile of v0, /device:TPU:0, one launch (start us, length us, event | category | flops | bytes accessed | tf_op | source)
XLA Modules:
  0.0 2001.8 jit_solution(8969384026109587184)
XLA Ops:
  25.6 31.0 %all-gather = bf16[8,288,4]{1,2,0:T(4,128)(2,1)S(1)} all-gather(bf16[1,288,4]{1,2,0:T(4,128)(2,1)S(1)} %reshape.451), channel_id=1, replica_groups=mesh['ctx'=8,'fsdp'=4] {'ctx'}, dimensions={0}, use_global_device_ids=true | all-gather | bytes 20736 | tf_op jit(solution)/shard_map/all_gather | solution.py:191
  68.3 19.3 all-gather.13.cloned.1.call-done
  92.5 38.4 %all-gather.17.cloned.1.call-done = bf16[2304,256]{1,0:T(8,128)(2,1)} async-done(((bf16[288,256]{1,0:T(8,128)(2,1)}), bf16[2304,256]{1,0:T(8,128)(2,1)}) %all-gather.17.cloned.1.call-update) | async-done | bytes 1179664 | tf_op jit(solution)/shard_map/all_gather | solution.py:186
  153.8 15.1 collective-permute-done.1
  168.8 11.6 collective-permute-start.2
  180.5 24.3 %collective-permute-done.2 = bf16[2,640,256]{1,2,0:T(8,128)(2,1)S(1)} collective-permute-done((bf16[2,640,256]{1,2,0:T(8,128)(2,1)S(1)}, bf16[2,640,256]{1,2,0:T(8,128)(2,1)S(1)}, u32[]{:S(2)}, u32[]{:S(2)}) %collective-permute-start.2) | collective-permute-done | bytes 655392 | tf_op jit(solution)/shard_map/ppermute | solution.py:20
  210.6 12.1 collective-permute-done.3
  288.0 14.2 fusion.6
  302.2 12.7 exponential_reduce_fusion
  314.9 13.8 fusion.40
  336.4 21.6 %all_to_all.243 = bf16[72,4,2304]{2,0,1:T(8,128)(2,1)} all-to-all(bf16[72,4,2304]{2,0,1:T(8,128)(2,1)S(1)} %bitcast.288), channel_id=1, replica_groups=mesh['ctx'=8,'fsdp'=4] {'fsdp'}, dimensions={1} | all-to-all | bytes 2654208 | tf_op jit(solution)/shard_map/all_to_all | solution.py:178
  358.4 42.2 %reduce-scatter.11.cloned.1.call-done = f32[160,2304]{1,0:T(8,128)} async-done(((f32[640,2304]{1,0:T(8,128)}), f32[160,2304]{1,0:T(8,128)}) %reduce-scatter.11.cloned.1.call-update) | async-done | bytes 1474576 | tf_op jit(solution)/shard_map/reduce_scatter | solution.py:201
  406.5 20.7 %all_to_all.244 = bf16[72,4,2304]{2,0,1:T(8,128)(2,1)} all-to-all(bf16[72,4,2304]{2,0,1:T(8,128)(2,1)S(1)} %bitcast.289), channel_id=1, replica_groups=mesh['ctx'=8,'fsdp'=4] {'fsdp'}, dimensions={1} | all-to-all | bytes 2654208 | tf_op jit(solution)/shard_map/all_to_all | solution.py:179
  427.4 20.7 %all_to_all.245 = bf16[72,4,2304]{2,0,1:T(8,128)(2,1)} all-to-all(bf16[72,4,2304]{2,0,1:T(8,128)(2,1)S(1)} %bitcast.290), channel_id=1, replica_groups=mesh['ctx'=8,'fsdp'=4] {'fsdp'}, dimensions={1} | all-to-all | bytes 2654208 | tf_op jit(solution)/shard_map/all_to_all | solution.py:180
  448.2 107.3 %all-gather.25.cloned.1.call-done = bf16[2304,2304]{1,0:T(8,128)(2,1)} async-done(((bf16[288,2304]{1,0:T(8,128)(2,1)}), bf16[2304,2304]{1,0:T(8,128)(2,1)}) %all-gather.25.cloned.1.call-update) | async-done | bytes 10616848 | tf_op jit(solution)/shard_map/all_gather | solution.py:188
  555.5 27.9 %all-gather.23.cloned.1.call-done = bf16[640,2304]{1,0:T(8,128)(2,1)} async-done(((bf16[160,2304]{1,0:T(8,128)(2,1)}), bf16[640,2304]{1,0:T(8,128)(2,1)}) %all-gather.23.cloned.1.call-update) | async-done | bytes 2949136 | tf_op jit(solution)/shard_map/all_gather | solution.py:198
  583.4 12.8 convolution_convert_fusion.4
  596.1 142.1 %all-gather.27.cloned.1.call-done = bf16[2304,2304]{1,0:T(8,128)(2,1)} async-done(((bf16[288,2304]{1,0:T(8,128)(2,1)}), bf16[2304,2304]{1,0:T(8,128)(2,1)}) %all-gather.27.cloned.1.call-update) | async-done | bytes 10616848 | tf_op jit(solution)/shard_map/all_gather | solution.py:189
  738.3 12.8 convolution_convert_fusion.3
  751.1 140.1 %all-gather.29.cloned.1.call-done = bf16[2304,2304]{1,0:T(8,128)(2,1)} async-done(((bf16[288,2304]{1,0:T(8,128)(2,1)}), bf16[2304,2304]{1,0:T(8,128)(2,1)}) %all-gather.29.cloned.1.call-update) | async-done | bytes 10616848 | tf_op jit(solution)/shard_map/all_gather | solution.py:190
  891.2 15.3 fusion.113
  906.6 54.0 %reduce-scatter.13.cloned.1.call-done = f32[160,2304]{1,0:T(8,128)} async-done(((f32[640,2304]{1,0:T(8,128)}), f32[160,2304]{1,0:T(8,128)}) %reduce-scatter.13.cloned.1.call-update) | async-done | bytes 1474576 | tf_op jit(solution)/shard_map/reduce_scatter | solution.py:201
  967.3 27.4 %all-gather.31.cloned.1.call-done = bf16[640,2304]{1,0:T(8,128)(2,1)} async-done(((bf16[160,2304]{1,0:T(8,128)(2,1)}), bf16[640,2304]{1,0:T(8,128)(2,1)}) %all-gather.31.cloned.1.call-update) | async-done | bytes 2949136 | tf_op jit(solution)/shard_map/all_gather | solution.py:198
  994.6 17.8 fusion.19
  1012.4 13.3 fusion.121
  1025.7 16.8 convolution_add_fusion
  1042.6 55.9 %reduce-scatter.15.cloned.1.call-done = f32[160,2304]{1,0:T(8,128)} async-done(((f32[640,2304]{1,0:T(8,128)}), f32[160,2304]{1,0:T(8,128)}) %reduce-scatter.15.cloned.1.call-update) | async-done | bytes 1474576 | tf_op jit(solution)/shard_map/reduce_scatter | solution.py:201
  1105.3 15.4 convolution_convert_fusion.1
  1122.6 15.2 convolution_convert_fusion
  1139.6 12.5 convolution_convert_fusion.2
  1157.4 16.8 fusion.2
  1178.9 10.8 fusion.122
  1189.8 44.5 %fusion.3 = bf16[2,640,5120]{1,2,0:T(8,128)(2,1)} fusion(f32[5120,640,2]{1,0,2:T(8,128)} %fusion.122, f32[5120,640,2]{1,0,2:T(8,128)} %get-tuple-element.104, f32[2,640]{1,0:T(2,128)S(1)} %copy-done.60, pred[640,5120]{0,1:T(8,128)(4,1)} %fusion.10), kind=kOutput, calls=%fused_computation.5 | output fusion | flops 98310400 | bytes 68817920 | tf_op jit(solution)/shard_map/while/body/eval_jaxpr/sub | solution.py:130
  1234.3 13.7 fusion.15
  1262.1 26.5 %collective-permute-done.7 = bf16[2,640,256]{1,2,0:T(8,128)(2,1)S(1)} collective-permute-done((bf16[2,640,256]{1,2,0:T(8,128)(2,1)S(1)}, bf16[2,640,256]{1,2,0:T(8,128)(2,1)S(1)}, u32[]{:S(2)}, u32[]{:S(2)}) %collective-permute-start.7) | collective-permute-done | bytes 655392 | tf_op jit(solution)/shard_map/ppermute | solution.py:20
  1290.1 24.7 %collective-permute-done.8 = bf16[2,640,256]{1,2,0:T(8,128)(2,1)S(1)} collective-permute-done((bf16[2,640,256]{1,2,0:T(8,128)(2,1)S(1)}, bf16[2,640,256]{1,2,0:T(8,128)(2,1)S(1)}, u32[]{:S(2)}, u32[]{:S(2)}) %collective-permute-start.8) | collective-permute-done | bytes 655392 | tf_op jit(solution)/shard_map/ppermute | solution.py:20
  1316.2 38.0 %collective-permute-done.9 = bf16[2,640,256]{1,2,0:T(8,128)(2,1)S(1)} collective-permute-done((bf16[2,640,256]{1,2,0:T(8,128)(2,1)S(1)}, bf16[2,640,256]{1,2,0:T(8,128)(2,1)S(1)}, u32[]{:S(2)}, u32[]{:S(2)}) %collective-permute-start.9) | collective-permute-done | bytes 655392 | tf_op jit(solution)/shard_map/ppermute | solution.py:20
  1355.7 30.0 %collective-permute-done.10 = bf16[2,640,256]{1,2,0:T(8,128)(2,1)S(1)} collective-permute-done((bf16[2,640,256]{1,2,0:T(8,128)(2,1)S(1)}, bf16[2,640,256]{1,2,0:T(8,128)(2,1)S(1)}, u32[]{:S(2)}, u32[]{:S(2)}) %collective-permute-start.10) | collective-permute-done | bytes 655392 | tf_op jit(solution)/shard_map/ppermute | solution.py:20
  1387.2 40.3 %collective-permute-done.11 = bf16[2,640,256]{1,2,0:T(8,128)(2,1)S(1)} collective-permute-done((bf16[2,640,256]{1,2,0:T(8,128)(2,1)S(1)}, bf16[2,640,256]{1,2,0:T(8,128)(2,1)S(1)}, u32[]{:S(2)}, u32[]{:S(2)}) %collective-permute-start.11) | collective-permute-done | bytes 655392 | tf_op jit(solution)/shard_map/ppermute | solution.py:20
  1437.9 19.9 collective-permute-done.12
  1465.4 27.6 %collective-permute-done.13 = bf16[2,640,256]{1,2,0:T(8,128)(2,1)S(1)} collective-permute-done((bf16[2,640,256]{1,2,0:T(8,128)(2,1)}, bf16[2,640,256]{1,2,0:T(8,128)(2,1)S(1)}, u32[]{:S(2)}, u32[]{:S(2)}) %collective-permute-start.13) | collective-permute-done | bytes 655392 | tf_op jit(solution)/shard_map/ppermute | solution.py:20
  1510.0 14.0 pad_maximum_fusion
  1538.0 43.9 %reduce-scatter.23.cloned.1.call-done = bf16[288,2304]{1,0:T(8,128)(2,1)} async-done(((bf16[2304,2304]{1,0:T(8,128)(2,1)}), bf16[288,2304]{1,0:T(8,128)(2,1)}) %reduce-scatter.23.cloned.1.call-update) | async-done | bytes 1327120 | tf_op jit(solution)/shard_map/reduce_scatter | solution.py:313
  1585.5 179.4 %reduce-scatter.19.cloned.1.call-done = bf16[288,2304]{1,0:T(8,128)(2,1)} async-done(((bf16[2304,2304]{1,0:T(8,128)(2,1)}), bf16[288,2304]{1,0:T(8,128)(2,1)}) %reduce-scatter.19.cloned.1.call-update) | async-done | bytes 1327120 | tf_op jit(solution)/shard_map/reduce_scatter | solution.py:307
  1773.0 13.7 all-to-all-done.12
  1790.3 31.8 %reduce-scatter.17.cloned.1.call-done = f32[160,2304]{1,0:T(8,128)} async-done(((f32[640,2304]{1,0:T(8,128)}), f32[160,2304]{1,0:T(8,128)}) %reduce-scatter.17.cloned.1.call-update) | async-done | bytes 1474576 | tf_op jit(solution)/shard_map/reduce_scatter | solution.py:201
  1824.1 42.9 %all-reduce.4 = (f32[2304]{0:T(1024)S(1)}, f32[2304]{0:T(1024)S(1)}, f32[2304]{0:T(1024)S(1)}, f32[2304]{0:T(1024)S(1)}) all-reduce(f32[2304]{0:T(1024)S(1)} %get-tuple-element.70, f32[2304]{0:T(1024)S(1)} %copy-done.54, f32[2304]{0:T(1024)S(1)} %copy-done.53, ...), channel_id=10, replica_groups=mesh['ctx'=8,'fsdp'=4] {'ctx','fsdp'}, use_global_device_ids=true, to_apply=%region_20.21.clone | all-reduce | flops 9216 | bytes 73728
  1872.2 84.2 %reduce-scatter.25.cloned.1.call-done = bf16[288,1536]{1,0:T(8,128)(2,1)} async-done(((bf16[2304,1536]{1,0:T(8,128)(2,1)}), bf16[288,1536]{1,0:T(8,128)(2,1)}) %reduce-scatter.25.cloned.1.call-update) | async-done | bytes 884752 | tf_op jit(solution)/shard_map/reduce_scatter | solution.py:293
  (347 shorter events, 299.1 us)
Async XLA Ops:
  7.2 61.1 %all-gather.15.cloned.1.call-start = ((), (), s32[]{:S(2)}) async-start(), calls=%async_computation.24 | async-start | bytes 1327104 | tf_op jit(solution)/shard_map/all_gather | solution.py:185
  18.5 7.0 all-to-all-start
  21.7 65.9 %all-gather.13.cloned.1.call-start = ((), (), s32[]{:S(2)}) async-start(), calls=%async_computation.23 | async-start | bytes 3686400 | tf_op jit(solution)/shard_map/all_gather | solution.py:198
  60.2 70.7 %all-gather.17.cloned.1.call-start = ((), (), s32[]{:S(2)}) async-start(), calls=%async_computation.25 | async-start | bytes 1327104 | tf_op jit(solution)/shard_map/all_gather | solution.py:186
  68.2 195.5 %all-gather.19.cloned.1.call-start = ((), (), s32[]{:S(2)}) async-start(), calls=%async_computation.26 | async-start | bytes 2654208 | tf_op jit(solution)/shard_map/all_gather | solution.py:184
  68.3 184.3 %copy-start.71 = (f32[128]{0:T(128)}, f32[128]{0:T(128)S(1)}, u32[]{:S(2)}) copy-start(f32[128]{0:T(128)S(1)} %multiply_power_fusion) | copy-start | bytes 1540
  68.3 184.3 %copy-start.50 = (f32[640]{0:T(1024)}, f32[640]{0:T(1024)S(1)}, u32[]{:S(2)}) copy-start(f32[640]{0:T(1024)S(1)} %fusion.97) | copy-start | bytes 7684
  134.2 15.2 collective-permute-start
  149.3 97.4 %copy-start.30 = (bf16[2,640,256]{1,2,0:T(8,128)(2,1)}, bf16[2,640,256]{1,2,0:T(8,128)(2,1)S(1)}, u32[]{:S(2)}) copy-start(bf16[2,640,256]{1,2,0:T(8,128)(2,1)S(1)} %collective-permute-done) | copy-start | bytes 1966084
  149.3 19.5 collective-permute-start.1
  168.8 99.6 %copy-start.32 = (bf16[2,640,256]{1,2,0:T(8,128)(2,1)}, bf16[2,640,256]{1,2,0:T(8,128)(2,1)S(1)}, u32[]{:S(2)}) copy-start(bf16[2,640,256]{1,2,0:T(8,128)(2,1)S(1)} %collective-permute-done.1) | copy-start | bytes 1966084
  168.8 35.9 %collective-permute-start.2 = (bf16[2,640,256]{1,2,0:T(8,128)(2,1)S(1)}, bf16[2,640,256]{1,2,0:T(8,128)(2,1)S(1)}, u32[]{:S(2)}, u32[]{:S(2)}) collective-permute-start(bf16[2,640,256]{1,2,0:T(8,128)(2,1)S(1)} %collective-permute-done.1), channel_id=1, source_target_pairs={{0,4},{4,8},{8,12},{12,16},{16,20},{20,24},{24,28},{1,5},{5,9},{9,... | collective-permute-start | bytes 1966088 | tf_op jit(solution)/shard_map/ppermute | solution.py:20
  204.7 18.0 collective-permute-start.3
  222.7 17.9 collective-permute-start.4
  231.2 22.6 %all-to-all-start.4 = ((bf16[72,4,512]{2,0,1:T(8,128)(2,1)}), bf16[72,4,512]{2,0,1:T(8,128)(2,1)S(1)}, u32[]{:S(2)}, u32[]{:S(2)}) async-start(bf16[72,4,512]{2,0,1:T(8,128)(2,1)} %bitcast.276), calls=%async_computation.4 | async-start | bytes 589824 | tf_op jit(solution)/shard_map/all_to_all | solution.py:177
  234.7 94.1 %all-gather.21.cloned.1.call-start = ((), (), s32[]{:S(2)}) async-start(), calls=%async_computation.27 | async-start | bytes 2654208 | tf_op jit(solution)/shard_map/all_gather | solution.py:187
  240.6 16.6 collective-permute-start.5
  254.6 146.0 %reduce-scatter.11.cloned.1.call-start = ((), (), s32[]{:S(2)}) async-start(), calls=%async_computation.28 | async-start | bytes 7372800 | tf_op jit(solution)/shard_map/reduce_scatter | solution.py:201
  257.2 18.9 collective-permute-start.6
  335.0 220.5 %all-gather.25.cloned.1.call-start = ((), (), s32[]{:S(2)}) async-start(), calls=%async_computation.30 | async-start | bytes 11943936 | tf_op jit(solution)/shard_map/all_gather | solution.py:188
  358.0 225.4 %all-gather.23.cloned.1.call-start = ((), (), s32[]{:S(2)}) async-start(), calls=%async_computation.29 | async-start | bytes 3686400 | tf_op jit(solution)/shard_map/all_gather | solution.py:198
  406.3 331.9 %all-gather.27.cloned.1.call-start = ((), (), s32[]{:S(2)}) async-start(), calls=%async_computation.31 | async-start | bytes 11943936 | tf_op jit(solution)/shard_map/all_gather | solution.py:189
  427.3 463.9 %all-gather.29.cloned.1.call-start = ((), (), s32[]{:S(2)}) async-start(), calls=%async_computation.32 | async-start | bytes 11943936 | tf_op jit(solution)/shard_map/all_gather | solution.py:190
  448.1 512.5 %reduce-scatter.13.cloned.1.call-start = ((), (), s32[]{:S(2)}) async-start(), calls=%async_computation.33 | async-start | bytes 7372800 | tf_op jit(solution)/shard_map/reduce_scatter | solution.py:201
  906.5 88.1 %all-gather.31.cloned.1.call-start = ((), (), s32[]{:S(2)}) async-start(), calls=%async_computation.34 | async-start | bytes 3686400 | tf_op jit(solution)/shard_map/all_gather | solution.py:198
  967.0 131.4 %reduce-scatter.15.cloned.1.call-start = ((), (), s32[]{:S(2)}) async-start(), calls=%async_computation.35 | async-start | bytes 7372800 | tf_op jit(solution)/shard_map/reduce_scatter | solution.py:201
  1042.6 131.6 %all-gather.33.cloned.1.call-start = ((), (), s32[]{:S(2)}) async-start(), calls=%async_computation.36 | async-start | bytes 3686400 | tf_op jit(solution)/shard_map/all_gather | solution.py:198
  1105.1 429.4 %reduce-scatter.21.cloned.1.call-start = ((), (), s32[]{:S(2)}) async-start(), calls=%async_computation.39 | async-start | bytes 11943936 | tf_op jit(solution)/shard_map/reduce_scatter | solution.py:310
  1120.8 461.1 %reduce-scatter.23.cloned.1.call-start = ((), (), s32[]{:S(2)}) async-start(), calls=%async_computation.40 | async-start | bytes 11943936 | tf_op jit(solution)/shard_map/reduce_scatter | solution.py:313
  1137.8 627.1 %reduce-scatter.19.cloned.1.call-start = ((), (), s32[]{:S(2)}) async-start(), calls=%async_computation.38 | async-start | bytes 11943936 | tf_op jit(solution)/shard_map/reduce_scatter | solution.py:307
  1152.2 670.0 %reduce-scatter.17.cloned.1.call-start = ((), (), s32[]{:S(2)}) async-start(), calls=%async_computation.37 | async-start | bytes 7372800 | tf_op jit(solution)/shard_map/reduce_scatter | solution.py:201
  1260.7 197.1 %copy-start.1 = (f32[1,8,640,256]{2,3,0,1:T(8,128)}, f32[1,8,640,256]{2,3,0,1:T(8,128)S(1)}, u32[]{:S(2)}) copy-start(f32[1,8,640,256]{2,3,0,1:T(8,128)S(1)} %convolution_bitcast_fusion.1) | copy-start | bytes 15728644
  1260.8 27.8 %collective-permute-start.7 = (bf16[2,640,256]{1,2,0:T(8,128)(2,1)S(1)}, bf16[2,640,256]{1,2,0:T(8,128)(2,1)S(1)}, u32[]{:S(2)}, u32[]{:S(2)}) collective-permute-start(bf16[2,640,256]{1,2,0:T(8,128)(2,1)S(1)} %fusion.72), channel_id=1, source_target_pairs={{4,0},{8,4},{12,8},{16,12},{20,16},{24,20},{28,24},{5,1},{9,5},{13... | collective-permute-start | bytes 1966088 | tf_op jit(solution)/shard_map/ppermute | solution.py:20
  1288.8 26.0 %collective-permute-start.8 = (bf16[2,640,256]{1,2,0:T(8,128)(2,1)S(1)}, bf16[2,640,256]{1,2,0:T(8,128)(2,1)S(1)}, u32[]{:S(2)}, u32[]{:S(2)}) collective-permute-start(bf16[2,640,256]{1,2,0:T(8,128)(2,1)S(1)} %fusion.52), channel_id=1, source_target_pairs={{4,0},{8,4},{12,8},{16,12},{20,16},{24,20},{28,24},{5,1},{9,5},{13... | collective-permute-start | bytes 1966088 | tf_op jit(solution)/shard_map/ppermute | solution.py:20
  1314.9 39.3 %collective-permute-start.9 = (bf16[2,640,256]{1,2,0:T(8,128)(2,1)S(1)}, bf16[2,640,256]{1,2,0:T(8,128)(2,1)S(1)}, u32[]{:S(2)}, u32[]{:S(2)}) collective-permute-start(bf16[2,640,256]{1,2,0:T(8,128)(2,1)S(1)} %fusion.56), channel_id=1, source_target_pairs={{4,0},{8,4},{12,8},{16,12},{20,16},{24,20},{28,24},{5,1},{9,5},{13... | collective-permute-start | bytes 1966088 | tf_op jit(solution)/shard_map/ppermute | solution.py:20
  1354.4 31.3 %collective-permute-start.10 = (bf16[2,640,256]{1,2,0:T(8,128)(2,1)S(1)}, bf16[2,640,256]{1,2,0:T(8,128)(2,1)S(1)}, u32[]{:S(2)}, u32[]{:S(2)}) collective-permute-start(bf16[2,640,256]{1,2,0:T(8,128)(2,1)S(1)} %fusion.60), channel_id=1, source_target_pairs={{4,0},{8,4},{12,8},{16,12},{20,16},{24,20},{28,24},{5,1},{9,5},{13... | collective-permute-start | bytes 1966088 | tf_op jit(solution)/shard_map/ppermute | solution.py:20
  1385.9 41.6 %collective-permute-start.11 = (bf16[2,640,256]{1,2,0:T(8,128)(2,1)S(1)}, bf16[2,640,256]{1,2,0:T(8,128)(2,1)S(1)}, u32[]{:S(2)}, u32[]{:S(2)}) collective-permute-start(bf16[2,640,256]{1,2,0:T(8,128)(2,1)S(1)} %fusion.64), channel_id=1, source_target_pairs={{4,0},{8,4},{12,8},{16,12},{20,16},{24,20},{28,24},{5,1},{9,5},{13... | collective-permute-start | bytes 1966088 | tf_op jit(solution)/shard_map/ppermute | solution.py:20
  1427.6 30.2 %collective-permute-start.12 = (bf16[2,640,256]{1,2,0:T(8,128)(2,1)S(1)}, bf16[2,640,256]{1,2,0:T(8,128)(2,1)}, u32[]{:S(2)}, u32[]{:S(2)}) collective-permute-start(bf16[2,640,256]{1,2,0:T(8,128)(2,1)S(1)} %fusion.68), channel_id=1, source_target_pairs={{4,0},{8,4},{12,8},{16,12},{20,16},{24,20},{28,24},{5,1},{9,5},{13... | collective-permute-start | bytes 1966088 | tf_op jit(solution)/shard_map/ppermute | solution.py:20
  1459.9 33.1 %collective-permute-start.13 = (bf16[2,640,256]{1,2,0:T(8,128)(2,1)}, bf16[2,640,256]{1,2,0:T(8,128)(2,1)S(1)}, u32[]{:S(2)}, u32[]{:S(2)}) collective-permute-start(bf16[2,640,256]{1,2,0:T(8,128)(2,1)} %fusion.46), channel_id=1, source_target_pairs={{4,0},{8,4},{12,8},{16,12},{20,16},{24,20},{28,24},{5,1},{9,5},{13... | collective-permute-start | bytes 1966088 | tf_op jit(solution)/shard_map/ppermute | solution.py:20
  1500.5 455.8 %reduce-scatter.25.cloned.1.call-start = ((), (), s32[]{:S(2)}) async-start(), calls=%async_computation.41 | async-start | bytes 7962624 | tf_op jit(solution)/shard_map/reduce_scatter | solution.py:293
  1534.5 47.4 %all-to-all-start.13 = ((bf16[4,72,2304]{2,1,0:T(8,128)(2,1)}), bf16[4,72,2304]{2,1,0:T(8,128)(2,1)S(1)}, u32[]{:S(2)}, u32[]{:S(2)}) async-start(bf16[4,72,2304]{2,1,0:T(8,128)(2,1)} %bitcast.304), calls=%async_computation.19 | async-start | bytes 2654208 | tf_op jit(solution)/shard_map/all_to_all | solution.py:336
  1581.9 183.0 %all-to-all-start.14 = ((bf16[4,72,2304]{2,1,0:T(8,128)(2,1)}), bf16[4,72,2304]{2,1,0:T(8,128)(2,1)S(1)}, u32[]{:S(2)}, u32[]{:S(2)}) async-start(bf16[4,72,2304]{2,1,0:T(8,128)(2,1)} %bitcast.303), calls=%async_computation.21 | async-start | bytes 2654208 | tf_op jit(solution)/shard_map/all_to_all | solution.py:339
  1764.8 21.8 %all-to-all-start.12 = ((bf16[4,72,2304]{2,1,0:T(8,128)(2,1)}), bf16[4,72,2304]{2,1,0:T(8,128)(2,1)}, u32[]{:S(2)}, u32[]{:S(2)}) async-start(bf16[4,72,2304]{2,1,0:T(8,128)(2,1)} %bitcast.302), calls=%async_computation.17 | async-start | bytes 2654208 | tf_op jit(solution)/shard_map/all_to_all | solution.py:333
  1788.6 80.9 %copy-start.9 = (f32[160,2304]{1,0:T(8,128)S(1)}, f32[160,2304]{1,0:T(8,128)}, u32[]{:S(2)}) copy-start(f32[160,2304]{1,0:T(8,128)} %copy-done.8) | copy-start | bytes 4423684
  1958.1 8.1 all-to-all-start.10
  1966.2 8.1 all-to-all-start.9
  1974.3 9.8 all-to-all-start.11
  1984.1 9.8 all-to-all-start.8
  (72 other events, 1580.4 us)
Sparse Core Ops, SparseCore 0:
  17.3 41.7 all-gather.14
  61.2 26.3 all-gather.12
  89.9 41.0 all-gather.16
  146.3 66.0 all-gather.18
  254.7 59.0 all-gather.20
  335.1 65.4 reduce-scatter.10
  403.0 152.4 all-gather.24
  557.7 25.5 all-gather.22
  585.8 152.4 all-gather.26
  740.5 150.6 all-gather.28
  906.6 53.9 reduce-scatter.12
  967.2 27.4 all-gather.30
  1042.7 55.7 reduce-scatter.14
  1105.2 27.3 all-gather.32
  1136.5 197.7 reduce-scatter.20
  1337.7 244.1 reduce-scatter.22
  1585.8 179.0 reduce-scatter.18
  1767.3 54.8 reduce-scatter.16
  1826.3 130.0 reduce-scatter.24
where the time goes:
time: 2010 us; the launch traced here: 2000 us
  waiting for transfers between devices  1300 us (65%)
  matrix products  238 us (12%)
  blocking collectives  163 us (8%)
  other arithmetic  136 us (7%)
  starting transfers between devices  86.8 us (4%)
  local copies, waits for them, and re-layouts  58.3 us (3%)
    ppermute x14, waiting for transfers between devices, shifted(): lax.ppermute(value, axis, [(source, source + steps) for source in range(f...  276 us
    reduce_scatter x4, waiting for transfers between devices, narrow(): return lax.psum_scatter(values, 'fsdp', scatter_dimension=0, tiled=True)  184 us
    reduce_scatter x1, waiting for transfers between devices, body(): lax.psum_scatter(column_term(mlp_in_b, d_gate_b).astype(jnp.bfloat16), 'c...  179 us
    all_gather x1, waiting for transfers between devices, body(): lax.all_gather(swapped[5], 'ctx', axis=0, tiled=True)  142 us
    all_gather x1, waiting for transfers between devices, body(): lax.all_gather(swapped[6], 'ctx', axis=0, tiled=True)  140 us
    all_gather x1, waiting for transfers between devices, body(): lax.all_gather(swapped[4], 'ctx', axis=0, tiled=True)  107 us
    reduce_scatter x1, waiting for transfers between devices, body(): lax.psum_scatter(jnp.concatenate([column_term(attn_in_b, d_query_b), colu...  84.2 us
    all_gather x4, waiting for transfers between devices, widen(): return lax.all_gather(values, 'fsdp', axis=0, tiled=True)  74.5 us
  transfers between devices with their start and end apart: 42, of which 34 were waited for; matrix products, arithmetic and copies ran while one was open for 17% of the time, Pallas kernels for 0%

commit v1 on v0

v1 whole, which is shorter than its diff:
```python
import jax
import jax.numpy as jnp
from jax import lax
from jax.experimental import pallas as pl
from jax.experimental.pallas import tpu as pltpu
from jax.sharding import Mesh
from jax.sharding import PartitionSpec as P

HEADS = 8
KV_HEADS = 4
HEAD = 256
WINDOW = 4096
CAP = 10.0
EPS = 1e-06
SCALE = HEAD**-0.5
BLOCK = 256

RING = 4
AXES = ("z", "b", "y", "c")
GROUP = ("z", "c")
COPIES = ("b", "y")

bf16 = jnp.bfloat16
f32 = jnp.float32


def swapped(value, axis):
    return lax.ppermute(value, axis, [(0, 1), (1, 0)])


def rotated(value, axis, steps):
    count = lax.axis_size(axis)
    return lax.ppermute(value, axis, [(i, (i + steps) % count) for i in range(count)])


def join(*values):
    return lax.optimization_barrier(values)


def dot_nn(left, right):
    return lax.dot_general(left, right, (((1,), (0,)), ((), ())), preferred_element_type=f32)


def dot_nt(left, right):
    return lax.dot_general(left, right, (((1,), (1,)), ((), ())), preferred_element_type=f32)


def dot_tn(left, right):
    return lax.dot_general(left, right, (((0,), (0,)), ((), ())), preferred_element_type=f32)


def moved(values, first, second):
    rest = values.shape[1] // (first * second)
    starts = [(i * second + j) * rest for j in range(second) for i in range(first)]
    return jnp.concatenate([values[:, s : s + rest] for s in starts], axis=1)


def copies_first(values, normed=False):
    rows, width = values.shape
    copies = lax.axis_size("b") * lax.axis_size("y")

    def kernel(in_ref, out_ref, *normed_refs):
        here = moved(in_ref[...].astype(f32), RING, copies)
        out_ref[...] = here.astype(out_ref.dtype)
        if normed:
            inverse = lax.rsqrt(jnp.mean(here * here, axis=1, keepdims=True) + EPS)
            normed_refs[0][...] = (here * inverse).astype(bf16)
            normed_refs[1][...] = inverse

    out_shape = [jax.ShapeDtypeStruct((rows, width), values.dtype)]
    if normed:
        out_shape.append(jax.ShapeDtypeStruct((rows, width), bf16))
        out_shape.append(jax.ShapeDtypeStruct((rows, 1), f32))
    result = pl.pallas_call(
        kernel,
        out_shape=out_shape,
        compiler_params=pltpu.CompilerParams(vmem_limit_bytes=24 << 20),
        cost_estimate=pl.CostEstimate(
            flops=rows * width, bytes_accessed=8 * rows * width, transcendentals=0
        ),
        name="copies_first",
    )(values)
    return result if normed else result[0]


def copies_back(values):
    rows, width = values.shape
    copies = lax.axis_size("b") * lax.axis_size("y")

    def kernel(in_ref, out_ref):
        out_ref[...] = moved(in_ref[...].astype(f32), copies, RING).astype(out_ref.dtype)

    return pl.pallas_call(
        kernel,
        out_shape=jax.ShapeDtypeStruct((rows, width), values.dtype),
        compiler_params=pltpu.CompilerParams(vmem_limit_bytes=24 << 20),
        cost_estimate=pl.CostEstimate(
            flops=rows * width, bytes_accessed=8 * rows * width, transcendentals=0
        ),
        name="copies_back",
    )(values)


def gather_tokens(own, work=None, beside=(None, None, None)):
    half = own.shape[0] // 2
    up, down = own[:half], own[half:]
    chunks, results = [jnp.concatenate([own, swapped(own, "c")], axis=0)], []
    beside = list(beside)
    for step in range(RING):
        results.append(work(step, chunks[step]) if work else ())
        if step == RING - 1:
            return chunks, results, beside
        up, down = rotated(up, "z", 1), rotated(down, "z", -1)
        extra = beside[step] or ()
        if results[step] or extra:
            up, down, results[step], beside[step] = join(up, down, results[step], extra)
        both = jnp.concatenate([up, down], axis=0)
        chunks.append(jnp.concatenate([both, swapped(both, "c")], axis=0))


def relative_places():
    place = None
    for axis in AXES:
        count = lax.axis_size(axis)
        at = (lax.axis_index(axis) - jnp.arange(count, dtype=jnp.int32)) % count
        place = at if place is None else (place[:, None] * count + at[None, :]).reshape(-1)
    return place


def gather_small(value):
    for axis in AXES[::-1]:
        parts = [value] + [rotated(value, axis, k) for k in range(1, lax.axis_size(axis))]
        value = jnp.concatenate(parts, axis=0)
    place = relative_places()
    chosen = place[None, :] == jnp.arange(place.shape[0], dtype=jnp.int32)[:, None]
    return dot_nn(chosen.astype(value.dtype), value)


def scatter_small(value):
    place = relative_places()
    chosen = place[:, None] == jnp.arange(place.shape[0], dtype=jnp.int32)[None, :]
    value = jnp.dot(
        chosen.astype(f32), value, precision=lax.Precision.HIGHEST, preferred_element_type=f32
    )
    for axis in AXES:
        count = lax.axis_size(axis)
        parts = value.reshape(count, -1, value.shape[1])
        total = parts[0]
        for k in range(1, count):
            total = total + rotated(parts[k], axis, -k)
        value = total
    return value[0]


def scatter_tokens(chunks, beside=(None, None, None)):
    rows = chunks[0].shape[0] // 2
    half = rows // 2
    carried = None
    beside = list(beside)
    for step in range(RING):
        chunk = chunks[(step + 1) % RING]
        here = chunk[:rows].astype(f32) + swapped(chunk[rows:], "c").astype(f32)
        if carried is not None:
            here = here + carried.astype(f32)
        if step == RING - 1:
            return here, beside
        sent = here.astype(bf16)
        up, down = rotated(sent[:half], "z", 1), rotated(sent[half:], "z", -1)
        if beside[step] is not None:
            up, down, *beside[step] = join(up, down, *beside[step])
        carried = jnp.concatenate([up, down], axis=0)


def ring_pieces(values, tok):
    half = tok // 2
    return values.reshape(RING, 2, 2, half, values.shape[-1])


def by_block(values, tok):
    parts = ring_pieces(values, tok)
    order = [0] + list(range(RING - 1, 0, -1))
    blocks = [jnp.stack([parts[i, :, 0], parts[order[i], :, 1]], axis=1) for i in range(RING)]
    return jnp.concatenate([block.reshape(2 * tok, -1) for block in blocks], axis=0)


def exchange(blocks):
    return lax.all_to_all(blocks, GROUP, split_axis=0, concat_axis=0, tiled=True)


def gather_rows(blocks):
    parts, rows, cols = blocks.shape
    return lax.all_gather(blocks.reshape(parts * rows, cols), COPIES, axis=0, tiled=True)


def scatter_rows(grad):
    total = lax.psum_scatter(grad, COPIES, scatter_dimension=0, tiled=True)
    return total.reshape(8, -1, grad.shape[1])


def split_cols(weight):
    rows, cols = weight.shape
    return weight.reshape(rows, 8, cols // 8).transpose(1, 0, 2)


def join_cols(blocks):
    parts, rows, cols = blocks.shape
    return blocks.transpose(1, 0, 2).reshape(rows, parts * cols)


def attention_forward(q, kv, meta, q_pos, k_pos, q_block):
    tokens = q.shape[0]
    keys = kv.shape[1]
    steps = tokens // q_block
    key_steps = keys // BLOCK

    def kernel(meta_ref, q_ref, kv_ref, q_pos_ref, k_pos_ref, o_ref, lse_ref, acc_ref, sum_ref):
        i = pl.program_id(0)
        core = meta_ref[0]
        q_low, q_high = meta_ref[1 + 2 * i], meta_ref[2 + 2 * i]
        acc_ref[...] = jnp.zeros_like(acc_ref)
        sum_ref[...] = jnp.zeros_like(sum_ref)

        def step(j, carry):
            k_low = meta_ref[1 + 2 * steps + 2 * j]
            k_high = meta_ref[2 + 2 * steps + 2 * j]

            @pl.when((q_high >= k_low) & (q_low - k_high < WINDOW))
            def _():
                place = pl.ds(pl.multiple_of(j * BLOCK, BLOCK), BLOCK)
                key = kv_ref[core, place, :]
                value = kv_ref[1 - core, place, :]
                scores = dot_nt(q_ref[...], key)
                turned = jnp.tanh(scores * (SCALE / CAP))
                away = q_pos_ref[...] - k_pos_ref[j]
                weight = jnp.where((away >= 0) & (away < WINDOW), jnp.exp(turned * CAP), 0.0)
                sum_ref[...] += jnp.sum(weight, axis=1, keepdims=True)
                acc_ref[...] += dot_nn(weight.astype(bf16), value)

            return carry

        lax.fori_loop(0, key_steps, step, 0)
        total = sum_ref[...]
        o_ref[...] = acc_ref[...] / total
        lse_ref[...] = jnp.log(total)

    return pl.pallas_call(
        kernel,
        grid=(steps,),
        in_specs=[
            pl.BlockSpec(memory_space=pltpu.SMEM),
            pl.BlockSpec((q_block, HEAD), lambda i: (i, 0)),
            pl.BlockSpec(memory_space=pltpu.VMEM),
            pl.BlockSpec((q_block, 1), lambda i: (i, 0)),
            pl.BlockSpec(memory_space=pltpu.VMEM),
        ],
        out_specs=[
            pl.BlockSpec((q_block, HEAD), lambda i: (i, 0)),
            pl.BlockSpec((q_block, 1), lambda i: (i, 0)),
        ],
        out_shape=[
            jax.ShapeDtypeStruct((tokens, HEAD), f32),
            jax.ShapeDtypeStruct((tokens, 1), f32),
        ],
        scratch_shapes=[pltpu.VMEM((q_block, HEAD), f32), pltpu.VMEM((q_block, 1), f32)],
        compiler_params=pltpu.CompilerParams(vmem_limit_bytes=2 * kv.size + (12 << 20)),
        cost_estimate=pl.CostEstimate(
            flops=4 * tokens * keys * HEAD,
            bytes_accessed=2 * kv.size + 8 * tokens * HEAD,
            transcendentals=2 * tokens * keys,
        ),
        name="attention_forward",
    )(meta, q, kv, q_pos, k_pos)


def attention_backward(q, d_out, kv, meta, lse, delta, q_pos, k_pos):
    tokens = q.shape[0]
    keys = kv.shape[1]
    steps = tokens // BLOCK
    key_steps = keys // BLOCK

    def kernel(
        meta_ref, q_ref, d_ref, kv_ref, lse_ref, delta_ref, q_pos_ref, k_pos_ref,
        dq_ref, dkv_ref, key_acc, value_acc,
    ):
        j = pl.program_id(0)
        core = meta_ref[0]
        k_low = meta_ref[1 + 2 * steps + 2 * j]
        k_high = meta_ref[2 + 2 * steps + 2 * j]

        @pl.when(j == 0)
        def _():
            dq_ref[...] = jnp.zeros_like(dq_ref)

        key_acc[...] = jnp.zeros_like(key_acc)
        value_acc[...] = jnp.zeros_like(value_acc)
        for i in range(steps):
            q_low, q_high = meta_ref[1 + 2 * i], meta_ref[2 + 2 * i]

            @pl.when((q_high >= k_low) & (q_low - k_high < WINDOW))
            def _(i=i):
                place = pl.ds(i * BLOCK, BLOCK)
                key = kv_ref[core]
                value = kv_ref[1 - core]
                query = q_ref[place, :]
                d_here = d_ref[place, :]
                turned = jnp.tanh(dot_nt(key, query) * (SCALE / CAP))
                away = q_pos_ref[:, place] - k_pos_ref[...]
                soft = jnp.where(
                    (away >= 0) & (away < WINDOW),
                    jnp.exp(turned * CAP - lse_ref[:, place]),
                    0.0,
                )
                d_prob = dot_nt(value, d_here)
                d_raw = soft * (d_prob - delta_ref[:, place]) * (1.0 - turned * turned)
                d_raw = d_raw.astype(bf16)
                value_acc[...] += dot_nn(soft.astype(bf16), d_here)
                key_acc[...] += dot_nn(d_raw, query)
                dq_ref[place, :] += dot_tn(d_raw, key)

        dkv_ref[core] = (key_acc[...] * SCALE).astype(bf16)
        dkv_ref[1 - core] = value_acc[...].astype(bf16)

        @pl.when(j == key_steps - 1)
        def _():
            dq_ref[...] = dq_ref[...] * SCALE

    whole = pl.BlockSpec(memory_space=pltpu.VMEM)
    return pl.pallas_call(
        kernel,
        grid=(key_steps,),
        in_specs=[
            pl.BlockSpec(memory_space=pltpu.SMEM),
            whole,
            whole,
            pl.BlockSpec((2, BLOCK, HEAD), lambda j: (0, j, 0)),
            whole,
            whole,
            whole,
            pl.BlockSpec((BLOCK, 1), lambda j: (j, 0)),
        ],
        out_specs=[whole, pl.BlockSpec((2, BLOCK, HEAD), lambda j: (0, j, 0))],
        out_shape=[
            jax.ShapeDtypeStruct((tokens, HEAD), f32),
            jax.ShapeDtypeStruct((2, keys, HEAD), bf16),
        ],
        scratch_shapes=[pltpu.VMEM((BLOCK, HEAD), f32), pltpu.VMEM((BLOCK, HEAD), f32)],
        compiler_params=pltpu.CompilerParams(vmem_limit_bytes=24 << 20),
        cost_estimate=pl.CostEstimate(
            flops=10 * tokens * keys * HEAD,
            bytes_accessed=4 * kv.size + 8 * tokens * HEAD,
            transcendentals=2 * tokens * keys,
        ),
        name="attention_backward",
    )(meta, q, d_out, kv, lse, delta, q_pos, k_pos)


def turn(values, cosine, sine):
    half = HEAD // 2
    parts = []
    for first in range(0, values.shape[1], HEAD):
        i = first // HEAD
        a = values[:, first : first + half]
        b = values[:, first + half : first + HEAD]
        parts += [a * cosine[i] - b * sine[i], b * cosine[i] + a * sine[i]]
    return jnp.concatenate(parts, axis=1)


def mean(values):
    return jnp.mean(values, axis=1, keepdims=True)


def gelu_parts(u):
    k = 0.7978845608028654
    t = jnp.tanh(k * (u + 0.044715 * u * u * u))
    value = 0.5 * u * (1.0 + t)
    slope = 0.5 * (1.0 + t) + 0.5 * u * (1.0 - t * t) * k * (1.0 + 3 * 0.044715 * u * u)
    return value, slope


def body(
    inputs,
    cotangent,
    w_query,
    w_key,
    w_value,
    w_out_t,
    w_gate,
    w_up,
    w_down_t,
    gain_attn_in,
    gain_attn_out,
    gain_mlp_in,
    gain_mlp_out,
):
    tok, width = inputs.shape
    rows = w_query.shape[0]
    count_b, count_y = lax.axis_size("b"), lax.axis_size("y")
    z, b, y, c = [lax.axis_index(name) for name in AXES]

    g_attn = gain_attn_in.astype(f32)[:, None]
    g_mlp = gain_mlp_in.astype(f32)[:, None]

    def scaled(weight, gain):
        return (weight.astype(f32) * gain).astype(bf16)

    pairs = jnp.stack(
        [w_key.reshape(rows, KV_HEADS, HEAD), w_value.reshape(rows, KV_HEADS, HEAD)], axis=2
    ).reshape(rows, 8, HEAD)
    qkv_pack = jnp.concatenate([w_query.reshape(rows, 8, HEAD), pairs], axis=2)
    qkv_pack = (qkv_pack.astype(f32) * g_attn[:, :, None]).astype(bf16).transpose(1, 0, 2)
    x, normed_x, r1 = copies_first(inputs, normed=True)
    x = x.astype(f32)
    out_pack = split_cols(w_out_t)
    gate_pack = split_cols(scaled(w_gate, g_mlp))
    up_pack = split_cols(scaled(w_up, g_mlp))
    down_pack = split_cols(w_down_t)
    qkv_w = gather_rows(exchange(qkv_pack))
    gains = jnp.concatenate([gain_attn_out, gain_mlp_out])[None]
    gains = gather_small(gains)
    x1, _, ((out_pack,), _, _) = gather_tokens(normed_x, None, ((out_pack,), None, None))
    out_mine = exchange(out_pack)
    x1[3], out_mine, gate_pack, gains = join(x1[3], out_mine, gate_pack, gains)
    out_w = gather_rows(out_mine)
    gate_mine = exchange(gate_pack)
    qkv = jnp.concatenate([dot_nn(part, qkv_w) for part in x1], axis=0)
    g_attn_out = moved(gains[:, :rows].reshape(1, width), RING, count_b * count_y)
    g_mlp_out = moved(gains[:, rows:].reshape(1, width), RING, count_b * count_y)

    def positions(places_b, places_y, places_c):
        blocks = (z - jnp.arange(RING, dtype=jnp.int32)) % RING
        place = (blocks * count_b + places_b[:, None, None]) * count_y + places_y[:, None]
        place = place[..., None] * 2 + places_c
        place = place[..., None] * tok + jnp.arange(tok, dtype=jnp.int32)
        return place.reshape(-1)

    cores = jnp.arange(2, dtype=jnp.int32)
    q_pos = positions(b[None], y[None], c ^ cores)
    k_pos = positions(
        (b - jnp.arange(count_b, dtype=jnp.int32)) % count_b,
        (y - jnp.arange(count_y, dtype=jnp.int32)) % count_y,
        cores,
    )

    def by_core(values):
        parts = values.reshape(RING, 2, tok, HEAD)
        return jnp.where(c == 0, parts, parts[:, ::-1]).reshape(values.shape)

    def bounds(places, block):
        blocks = places.reshape(-1, block)
        return jnp.stack([jnp.min(blocks, axis=1), jnp.max(blocks, axis=1)], axis=1).reshape(-1)

    q_block = 2 * tok
    core_id = c.astype(jnp.int32)[None]
    meta_forward = jnp.concatenate([core_id, bounds(q_pos, q_block), bounds(k_pos, BLOCK)])
    meta_backward = jnp.concatenate([core_id, bounds(q_pos, BLOCK), bounds(k_pos, BLOCK)])
    frequency = 10000.0 ** (-jnp.arange(HEAD // 2, dtype=f32) * 2.0 / HEAD)
    angles = q_pos.astype(f32)[:, None] * frequency[None, :]
    cos_q, sin_q = jnp.cos(angles), jnp.sin(angles)
    cos_kv, sin_kv = jnp.where(c == 0, cos_q, 1.0), jnp.where(c == 0, sin_q, 0.0)

    qkv = turn(by_block(qkv, tok), (cos_q, cos_kv), (sin_q, sin_kv)).astype(bf16)
    q = qkv[:, :HEAD]
    own_kv = by_core(qkv[:, HEAD:])
    kv_parts = []
    for k in range(count_b):
        here = rotated(own_kv, "b", k) if k else own_kv
        if k == 1:
            here, gate_mine, up_pack = join(here, gate_mine, up_pack)
            up_mine = exchange(up_pack)
        for j in range(count_y):
            kv_parts.append(rotated(here, "y", j) if j else here)
    kv_mine = jnp.concatenate(kv_parts, axis=0)
    kv_mine, gate_mine, up_mine, down_pack = join(kv_mine, gate_mine, up_mine, down_pack)
    gate_w = gather_rows(gate_mine)
    kv = jnp.stack([kv_mine, swapped(kv_mine, "c")])
    down_mine = exchange(down_pack)
    up_w = gather_rows(up_mine)
    keys = kv.shape[1]
    attended, lse = attention_forward(
        q, kv, meta_forward, q_pos[:, None], k_pos.reshape(-1, 1, BLOCK), q_block
    )
    attended, down_mine = join(attended, down_mine)
    down_w = gather_rows(down_mine)
    attended_b = by_block(attended.astype(bf16), tok)
    size = 2 * tok

    def cut(values):
        return [values[i * size : (i + 1) * size] for i in range(RING)]

    projected, _ = scatter_tokens([dot_nt(part, out_w).astype(bf16) for part in cut(attended_b)])
    r2 = lax.rsqrt(mean(projected * projected) + EPS)
    hidden = x + projected * r2 * g_attn_out

    r3 = lax.rsqrt(mean(hidden * hidden) + EPS)
    def mlp_forward(i, part):
        gate = dot_nn(part, gate_w).astype(bf16)
        up = dot_nn(part, up_w).astype(bf16)
        return gate, up, (gelu_parts(gate.astype(f32))[0] * up.astype(f32)).astype(bf16)

    x2, mlp, _ = gather_tokens((hidden * r3).astype(bf16), mlp_forward)
    gate, up, mixed = zip(*mlp)
    reduced, _ = scatter_tokens([dot_nt(part, down_w).astype(bf16) for part in mixed])
    r4 = lax.rsqrt(mean(reduced * reduced) + EPS)

    top = copies_first(cotangent).astype(f32)
    lifted = top * g_mlp_out
    d_reduced = r4 * lifted - reduced * (r4 * r4 * r4 * mean(lifted * reduced))
    def mlp_backward(i, part):
        d_mixed = dot_nn(part, down_w)
        gelu, slope = gelu_parts(gate[i].astype(f32))
        d_gate = (d_mixed * up[i].astype(f32) * slope).astype(bf16)
        d_up = (d_mixed * gelu).astype(bf16)
        return d_gate, d_up, (dot_nt(d_gate, gate_w) + dot_nt(d_up, up_w)).astype(bf16)

    x3, mlp, _ = gather_tokens(d_reduced.astype(bf16), mlp_backward)
    d_gate, d_up, dn3 = zip(*mlp)
    x2 = jnp.concatenate(x2, axis=0)
    x3 = jnp.concatenate(x3, axis=0)
    down_part = dot_tn(x3, jnp.concatenate(mixed, axis=0)).astype(bf16)
    gate_part = dot_tn(x2, jnp.concatenate(d_gate, axis=0)).astype(bf16)
    up_part = dot_tn(x2, jnp.concatenate(d_up, axis=0)).astype(bf16)
    dn3, parts = scatter_tokens(dn3, ((down_part,), (gate_part,), (up_part,)))
    down_rows, gate_rows, up_rows = [scatter_rows(part[0]) for part in parts]
    d_hidden = top + r3 * dn3 - hidden * (r3 * r3 * r3 * mean(dn3 * hidden))
    lifted = d_hidden * g_attn_out
    d_projected = r2 * lifted - projected * (r2 * r2 * r2 * mean(lifted * projected))
    d_projected, d_hidden, reduced = join(d_projected.astype(bf16), d_hidden, reduced)
    output = copies_back((hidden + reduced * r4 * g_mlp_out).astype(bf16))
    d_gain_mlp_out = jnp.sum(top * reduced * r4, axis=0, keepdims=True)
    d_gain_attn_out = jnp.sum(d_hidden * projected * r2, axis=0, keepdims=True)
    d_gains = jnp.concatenate(
        [
            moved(d_gain_attn_out, count_b * count_y, RING).reshape(-1, rows),
            moved(d_gain_mlp_out, count_b * count_y, RING).reshape(-1, rows),
        ],
        axis=1,
    )
    d_gains = scatter_small(d_gains)
    x4, d_attended, ((output,), _, _) = gather_tokens(
        d_projected, lambda i, part: (dot_nn(part, out_w).astype(bf16),), ((output,), None, None)
    )
    d_attended = by_block(jnp.concatenate([part[0] for part in d_attended], axis=0), tok)
    out_part = dot_tn(jnp.concatenate(x4, axis=0), attended_b).astype(bf16)
    delta = jnp.sum(d_attended.astype(f32) * attended, axis=1)
    delta, down_rows, out_part, d_gains = join(delta, down_rows, out_part, d_gains)
    out_rows = scatter_rows(out_part)
    down_sum = exchange(down_rows)
    d_query, d_kv = attention_backward(
        q,
        d_attended,
        kv,
        meta_backward,
        lse.reshape(1, -1),
        delta[None],
        q_pos[None],
        k_pos[:, None],
    )
    d_query, d_kv, down_sum, gate_rows, up_rows = join(
        d_query, d_kv, down_sum, gate_rows, up_rows
    )
    gate_sum = exchange(gate_rows)
    d_mine = (d_kv[0].astype(f32) + swapped(d_kv[1], "c").astype(f32)).astype(bf16)
    d_parts = d_mine.reshape(count_b, count_y, keys // (count_b * count_y), HEAD)
    d_own = None
    for k in list(range(1, count_b)) + [0]:
        piece = d_parts[k, 0].astype(f32)
        for j in range(1, count_y):
            piece = piece + rotated(d_parts[k, j], "y", -j).astype(f32)
        if k == 1:
            piece, gate_sum, up_rows = join(piece, gate_sum, up_rows)
            up_sum = exchange(up_rows)
        if k:
            piece = rotated(piece.astype(bf16), "b", -k).astype(f32)
        d_own = piece if d_own is None else d_own + piece
    d_own, up_sum, out_rows = join(d_own, up_sum, out_rows)
    out_sum = exchange(out_rows)
    d_q = turn(d_query, (cos_q,), (-sin_q,)).astype(bf16)
    d_k = turn(by_core(d_own), (cos_kv,), (-sin_kv,)).astype(bf16)
    d_qkv = by_block(jnp.concatenate([d_q, d_k], axis=1), tok)
    qkv_part = dot_tn(jnp.concatenate(x1, axis=0), d_qkv).astype(bf16)
    d_qkv, qkv_part = join(d_qkv, qkv_part)
    qkv_rows = scatter_rows(qkv_part)
    dn1, ((out_sum,), _, _) = scatter_tokens(
        [dot_nt(part, qkv_w).astype(bf16) for part in cut(d_qkv)], ((out_sum,), None, None)
    )
    qkv_sum = exchange(qkv_rows)
    down_sum, gate_sum, up_sum, out_sum, qkv_sum = [
        part.astype(f32) for part in (down_sum, gate_sum, up_sum, out_sum, qkv_sum)
    ]
    d_source = r1 * dn1 - x * (r1 * r1 * r1 * mean(dn1 * x))
    input_grad = copies_back((d_hidden + d_source).astype(bf16))

    q_sum = join_cols(qkv_sum[:, :, :HEAD])
    kv_sum = qkv_sum[:, :, HEAD:].reshape(KV_HEADS, 2, rows, HEAD)
    k_sum, v_sum = join_cols(kv_sum[:, 0]), join_cols(kv_sum[:, 1])
    gate_sum, up_sum = join_cols(gate_sum), join_cols(up_sum)

    def row_term(weight, grad):
        return jnp.sum(weight.astype(f32) * grad, axis=1)

    d_gain_attn_in = (
        row_term(w_query, q_sum) + row_term(w_key, k_sum) + row_term(w_value, v_sum)
    )
    d_gain_mlp_in = row_term(w_gate, gate_sum) + row_term(w_up, up_sum)
    return (
        output,
        input_grad,
        q_sum * g_attn,
        k_sum * g_attn,
        v_sum * g_attn,
        join_cols(out_sum),
        gate_sum * g_mlp,
        up_sum * g_mlp,
        join_cols(down_sum),
        d_gain_attn_in,
        d_gains[:rows],
        d_gain_mlp_in,
        d_gains[rows:],
    )


def solution(mesh):
    ctx, fsdp = mesh.devices.shape
    laid = Mesh(mesh.devices.reshape(RING, ctx // RING, fsdp // 2, 2), AXES)
    rows = P(AXES, None)
    line = P(AXES)
    return jax.shard_map(
        body,
        mesh=laid,
        in_specs=(rows,) * 9 + (line,) * 4,
        out_specs=(rows,) * 9 + (line,) * 4,
        check_vma=False,
    )
```

time: 2010 us -> 974 us (0.48)
  waiting for transfers between devices: 1300 us -> 356 us
  blocking collectives: 163 us -> 0 us
  starting transfers between devices: 86.8 us -> 186 us
  matrix products: 238 us -> 157 us
  Pallas kernels: 0 us -> 68.7 us
  other arithmetic: 136 us -> 82.6 us
  local copies, waits for them, and re-layouts: 58.3 us -> 89.9 us
    reduce_scatter x8 -> x5, waiting for transfers between devices: 491 us -> 0.02 us  [scatter_rows(): total = lax.psum_scatter(grad, COPIES, scatter_dimension=0, tiled=True)]
    all_gather x11 -> x5, waiting for transfers between devices: 503 us -> 15.5 us  [gather_rows(): lax.all_gather(blocks.reshape(parts * rows, cols), COPIES, axis=0, tiled=...]
    all_to_all x6 -> x0, blocking collectives: 89.3 us -> none  [the longest x1 21.6 us: body(): lax.all_to_all(w_gate, 'fsdp', split_axis=1, concat_axis=0, tiled=True)]
    ppermute x14 -> x100, starting transfers between devices: 52.8 us -> 142 us  [the longest x66 136 us: rotated(): lax.ppermute(value, axis, [(i, (i + steps) % count) for i in range(count)])]
    dot_general x27 -> x47, matrix products: 238 us -> 157 us  [the longest x21 60.1 us: dot_nn(): lax.dot_general(left, right, (((1,), (0,)), ((), ())), preferred_element_...]
    pallas_call x0 -> x6, Pallas kernels: none -> 68.7 us  [the longest x1 42.6 us: attention_backward(): pl.pallas_call(kernel, grid=(key_steps,), in_specs=[pl.BlockSpec(memory_s...]
    sub x1 -> x0, other arithmetic: 44.5 us -> none  [backward_head(): d_prob - inner]
    unnamed x1 -> x0, blocking collectives: 42.9 us -> none
  transfers between devices with their start and end apart: 42 -> 120, of which waited for: 34 -> 63; matrix products, arithmetic and copies ran while one was open for 17% -> 29% of each run, Pallas kernels for 0% -> 7%
where the time goes in v1:
time: 974 us; the launch traced here: 958 us
  waiting for transfers between devices  356 us (37%)
  starting transfers between devices  186 us (19%)
  matrix products  157 us (16%)
  local copies, waits for them, and re-layouts  89.9 us (9%)
  other arithmetic  82.6 us (8%)
  Pallas kernels  68.7 us (7%)
  between operations  17.7 us (2%)
    ppermute x66, waiting for transfers between devices, rotated(): lax.ppermute(value, axis, [(i, (i + steps) % count) for i in range(count)])  264 us
    ppermute x66, starting transfers between devices, rotated(): lax.ppermute(value, axis, [(i, (i + steps) % count) for i in range(count)])  136 us
    all_to_all x10, waiting for transfers between devices, exchange(): lax.all_to_all(blocks, GROUP, split_axis=0, concat_axis=0, tiled=True)  61.8 us
    dot_general x21, matrix products, dot_nn(): lax.dot_general(left, right, (((1,), (0,)), ((), ())), preferred_element_...  60.1 us
    dot_general x20, matrix products, dot_nt(): lax.dot_general(left, right, (((1,), (1,)), ((), ())), preferred_element_...  55.2 us
    unnamed x356, local copies, waits for them, and re-layouts  50.2 us
    all_to_all x10, starting transfers between devices, exchange(): lax.all_to_all(blocks, GROUP, split_axis=0, concat_axis=0, tiled=True)  42.8 us
    pallas_call x1, Pallas kernels, attention_backward(): pl.pallas_call(kernel, grid=(key_steps,), in_specs=[pl.BlockSpec(memory_s...  42.6 us
  transfers between devices with their start and end apart: 120, of which 63 were waited for; matrix products, arithmetic and copies ran while one was open for 29% of the time, Pallas kernels for 7%

profile of v1, /device:TPU:0, one launch (start us, length us, event | category | flops | bytes accessed | tf_op | source)
XLA Modules:
  0.0 957.7 jit_solution(4184752021623338454)
XLA Ops:
  24.6 21.1 %all-to-all-done = bf16[8,72,512]{2,1,0:T(8,128)(2,1)S(1)} async-done(((bf16[8,72,512]{2,1,0:T(8,128)(2,1)}), bf16[8,72,512]{2,1,0:T(8,128)(2,1)S(1)}, u32[]{:S(2)}, u32[]{:S(2)}) %all-to-all-start) | async-done | bytes 589856 | tf_op jit(solution)/shard_map/all_to_all | solution.py:187
  62.5 5.3 collective-permute-done.5
  75.9 9.7 %collective-permute-done.13 = bf16[8,144]{1,0:T(8,128)(2,1)S(1)} collective-permute-done((bf16[8,144]{1,0:T(8,128)(2,1)S(1)}, bf16[8,144]{1,0:T(8,128)(2,1)S(1)}, u32[]{:S(2)}, u32[]{:S(2)}) %collective-permute-start.13) | collective-permute-done | bytes 2336 | tf_op jit(solution)/shard_map/ppermute | solution.py:33
  127.0 15.8 %all-to-all-done.2 = bf16[8,72,1152]{2,1,0:T(8,128)(2,1)} async-done(((bf16[8,72,1152]{2,1,0:T(8,128)(2,1)}), bf16[8,72,1152]{2,1,0:T(8,128)(2,1)}, u32[]{:S(2)}, u32[]{:S(2)}) %all-to-all-start.2) | async-done | bytes 1327136 | tf_op jit(solution)/shard_map/all_to_all | solution.py:187
  153.0 17.3 %collective-permute-done.16 = bf16[1280,256]{1,0:T(8,128)(2,1)S(1)} collective-permute-done((bf16[1280,256]{1,0:T(8,128)(2,1)}, bf16[1280,256]{1,0:T(8,128)(2,1)S(1)}, u32[]{:S(2)}, u32[]{:S(2)}) %collective-permute-start.16) | collective-permute-done | bytes 655392 | tf_op jit(solution)/shard_map/ppermute | solution.py:33
  170.3 20.0 %collective-permute-done.18 = bf16[1280,256]{1,0:T(8,128)(2,1)S(1)} collective-permute-done((bf16[1280,256]{1,0:T(8,128)(2,1)}, bf16[1280,256]{1,0:T(8,128)(2,1)S(1)}, u32[]{:S(2)}, u32[]{:S(2)}) %collective-permute-start.18) | collective-permute-done | bytes 655392 | tf_op jit(solution)/shard_map/ppermute | solution.py:33
  206.2 22.7 %attention_forward.1 = (f32[1280,256]{1,0:T(8,128)S(1)}, f32[1280,1]{1,0:T(8,128)S(1)}) custom-call(s32[49]{0:T(128)S(1)} %pad_add_fusion.3.meta_ref, bf16[1280,256]{1,0:T(8,128)(2,1)S(1)} %pad_maximum_fusion.28.q_ref, bf16[2,5120,256]{2,1,0:T(8,128)(2,1)S(1)} %pad_maximum_fusion.kv_ref, s32[1280,1]{1,0:T(8,128)S(1)} %add.733.q_pos_ref, ...), custom_call_target="tpu_custom_call" | custom-call | flops 6710886400 | bytes 7864320 | tf_op jit(solution)/shard_map/attention_forward/pallas_call | solution.py:246
  246.0 8.6 collective-permute-done.24
  254.6 5.3 collective-permute-done.25
  265.8 7.9 collective-permute-done.26
  273.7 5.2 collective-permute-done.27
  284.4 9.2 collective-permute-done.28
  293.7 6.1 collective-permute-done.29
  308.3 5.4 convolution_convert_fusion.23
  313.7 7.3 all-gather.10.cloned.1.call-done
  321.0 6.1 fusion.79
  329.7 12.0 %collective-permute-start.35 = (bf16[80,2304]{1,0:T(8,128)(2,1)S(1)}, bf16[80,2304]{1,0:T(8,128)(2,1)S(1)}, u32[]{:S(2)}, u32[]{:S(2)}) collective-permute-start(bf16[80,2304]{1,0:T(8,128)(2,1)S(1)} %collective-permute-done.31), channel_id=1, source_target_pairs={{0,24},{8,0},{16,8},{24,16},{1,25},{9,1},{17,9},{25,17},{2,26},{10... | collective-permute-start | bytes 1105928 | tf_op jit(solution)/shard_map/ppermute | solution.py:33
  363.9 6.4 collective-permute-done.38
  376.6 8.1 all-gather.14.cloned.1.call-done
  389.6 5.9 multiply_convert_fusion.1
  405.3 6.8 collective-permute-done.44
  412.1 6.7 collective-permute-done.45
  426.0 6.4 collective-permute-done.46
  432.4 5.6 collective-permute-done.47
  443.8 9.0 collective-permute-done.48
  463.9 5.3 fusion.61
  524.9 9.7 %convolution_convert_fusion.2 = bf16[2304,1152]{1,0:T(8,128)(2,1)} fusion(bf16[1280,2304]{1,0:T(8,128)(2,1)S(1)} %constant_dynamic-update-slice_fusion.9, bf16[320,1152]{1,0:T(8,128)(2,1)S(1)} %copy-done.133, bf16[320,1152]{1,0:T(8,128)(2,1)S(1)} %copy-done.131, bf16[320,1152]{1,0:T(8,128)(2,1)S(1)} %copy-done.129, bf16[320,1152]{1,0:T(8,128)(2,1)S(1)} %copy-done.127), kind=kOutput, calls=%fused_computation.2 | convolution fusion | flops 6809223168 | bytes 14155776 | tf_op jit(solution)/shard_map/dot_general | solution.py:49
  548.9 6.2 multiply_convert_fusion
  556.0 11.6 %convolution_convert_fusion.1 = bf16[2304,1152]{1,0:T(8,128)(2,1)} fusion(bf16[1280,2304]{1,0:T(8,128)(2,1)} %get-tuple-element.272, bf16[320,1152]{1,0:T(8,128)(2,1)S(1)} %get-tuple-element.241, bf16[320,1152]{1,0:T(8,128)(2,1)S(1)} %copy-done.122, bf16[320,1152]{1,0:T(8,128)(2,1)S(1)} %copy-done.120, bf16[320,1152]{1,0:T(8,128)(2,1)S(1)} %copy-done.118), kind=kOutput, calls=%fused_computation.1 | convolution fusion | flops 6809223168 | bytes 14155776 | tf_op jit(solution)/shard_map/dot_general | solution.py:49
  568.1 5.1 fusion.301
  586.6 9.8 %convolution_convert_fusion = bf16[2304,1152]{1,0:T(8,128)(2,1)} fusion(bf16[1280,2304]{1,0:T(8,128)(2,1)S(1)} %bitcast.388, bf16[320,1152]{1,0:T(8,128)(2,1)S(1)} %copy-done.116, bf16[320,1152]{1,0:T(8,128)(2,1)S(1)} %copy-done.114, bf16[320,1152]{1,0:T(8,128)(2,1)S(1)} %copy-done.112, bf16[320,1152]{1,0:T(8,128)(2,1)S(1)} %copy-done.110), kind=kOutput, calls=%fused_computation | convolution fusion | flops 6809223168 | bytes 14155776 | tf_op jit(solution)/shard_map/dot_general | solution.py:49
  596.4 5.2 collective-permute-done.69
  634.8 8.3 collective-permute-done.70
  643.1 5.5 collective-permute-done.71
  655.5 6.5 collective-permute-done.73
  662.0 5.7 collective-permute-done.74
  674.3 6.6 collective-permute-done.76
  681.0 6.0 collective-permute-done.77
  708.1 42.6 %attention_backward.1 = (f32[1280,256]{1,0:T(8,128)S(1)}, bf16[2,5120,256]{2,1,0:T(8,128)(2,1)S(1)}) custom-call(s32[51]{0:T(128)S(1)} %pad_add_fusion.4.meta_ref, bf16[1280,256]{1,0:T(8,128)(2,1)S(1)} %copy-done.14, bf16[1280,256]{1,0:T(8,128)(2,1)S(1)} %pad_maximum_fusion.31.d_ref, bf16[2,5120,256]{2,1,0:T(8,128)(2,1)S(1)} %copy-done.3, ...), custom_call_target="tpu_custom_call" | custom-call | flops 16777216000 | bytes 13107200 | tf_op jit(solution)/shard_map/attention_backward/pallas_call | solution.py:328
  776.4 11.8 %collective-permute-done.87 = bf16[1280,256]{1,0:T(8,128)(2,1)} collective-permute-done((bf16[1280,256]{1,0:T(8,128)(2,1)S(1)}, bf16[1280,256]{1,0:T(8,128)(2,1)}, u32[]{:S(2)}, u32[]{:S(2)}) %collective-permute-start.87) | collective-permute-done | bytes 655392 | tf_op jit(solution)/shard_map/ppermute | solution.py:33
  790.3 7.1 all-to-all-done.6
  810.5 6.6 collective-permute-start.88
  820.9 5.6 collective-permute-done.89
  826.5 5.6 collective-permute-done.88
  840.3 7.7 convolution_convert_fusion.3
  878.8 6.7 collective-permute-done.95
  900.8 5.8 collective-permute-done.97
  935.2 11.1 %all-to-all-done.9 = bf16[8,72,512]{2,1,0:T(8,128)(2,1)S(1)} async-done(((bf16[8,72,512]{2,1,0:T(8,128)(2,1)}), bf16[8,72,512]{2,1,0:T(8,128)(2,1)S(1)}, u32[]{:S(2)}, u32[]{:S(2)}) %all-to-all-start.9) | async-done | bytes 589856 | tf_op jit(solution)/shard_map/all_to_all | solution.py:187
  (849 shorter events, 497.8 us)
Async XLA Ops:
  7.9 44.9 %collective-permute-start.10 = (bf16[1,144]{1,0:T(2,128)(2,1)S(1)}, bf16[1,144]{1,0:T(2,128)(2,1)S(1)}, u32[]{:S(2)}, u32[]{:S(2)}) collective-permute-start(bf16[1,144]{1,0:T(2,128)(2,1)S(1)} %broadcast_in_dim.17), channel_id=1, source_target_pairs={{0,1},{1,0},{2,3},{3,2},{4,5},{5,4},{6,7},{7,6},{8,9},{9,8},{10,11... | collective-permute-start | bytes 872 | tf_op jit(solution)/shard_map/ppermute | solution.py:33
  11.1 37.7 %collective-permute-start.1 = (bf16[80,2304]{1,0:T(8,128)(2,1)}, bf16[80,2304]{1,0:T(8,128)(2,1)}, u32[]{:S(2)}, u32[]{:S(2)}) collective-permute-start(bf16[80,2304]{1,0:T(8,128)(2,1)} %get-tuple-element.299), channel_id=1, source_target_pairs={{0,8},{8,16},{16,24},{24,0},{1,9},{9,17},{17,25},{25,1},{2,10},{10... | collective-permute-start | bytes 1105928 | tf_op jit(solution)/shard_map/ppermute | solution.py:33
  13.7 35.2 %collective-permute-start.2 = (bf16[80,2304]{1,0:T(8,128)(2,1)}, bf16[80,2304]{1,0:T(8,128)(2,1)}, u32[]{:S(2)}, u32[]{:S(2)}) collective-permute-start(bf16[80,2304]{1,0:T(8,128)(2,1)} %get-tuple-element.298), channel_id=1, source_target_pairs={{0,24},{8,0},{16,8},{24,16},{1,25},{9,1},{17,9},{25,17},{2,26},{10... | collective-permute-start | bytes 1105928 | tf_op jit(solution)/shard_map/ppermute | solution.py:33
  17.6 28.2 %all-to-all-start = ((bf16[8,72,512]{2,1,0:T(8,128)(2,1)}), bf16[8,72,512]{2,1,0:T(8,128)(2,1)S(1)}, u32[]{:S(2)}, u32[]{:S(2)}) async-start(bf16[8,72,512]{2,1,0:T(8,128)(2,1)} %copy.161), calls=%async_computation | async-start | bytes 1179648 | tf_op jit(solution)/shard_map/all_to_all | solution.py:187
  21.1 89.1 %all-gather.6.cloned.1.call-start = ((), (), s32[]{:S(2)}) async-start(), calls=%async_computation.15 | async-start | bytes 2949120 | tf_op jit(solution)/shard_map/all_gather | solution.py:192
  49.0 18.8 %collective-permute-start.5 = (bf16[80,2304]{1,0:T(8,128)(2,1)}, bf16[80,2304]{1,0:T(8,128)(2,1)}, u32[]{:S(2)}, u32[]{:S(2)}) collective-permute-start(bf16[80,2304]{1,0:T(8,128)(2,1)} %collective-permute-done.2), channel_id=1, source_target_pairs={{0,24},{8,0},{16,8},{24,16},{1,25},{9,1},{17,9},{25,17},{2,26},{10... | collective-permute-start | bytes 1105928 | tf_op jit(solution)/shard_map/ppermute | solution.py:33
  62.5 23.1 %collective-permute-start.7 = (bf16[80,2304]{1,0:T(8,128)(2,1)S(1)}, bf16[80,2304]{1,0:T(8,128)(2,1)}, u32[]{:S(2)}, u32[]{:S(2)}) collective-permute-start(bf16[80,2304]{1,0:T(8,128)(2,1)S(1)} %collective-permute-done.4), channel_id=1, source_target_pairs={{0,8},{8,16},{16,24},{24,0},{1,9},{9,17},{17,25},{25,1},{2,10},{10... | collective-permute-start | bytes 1105928 | tf_op jit(solution)/shard_map/ppermute | solution.py:33
  85.6 31.8 %collective-permute-start = (bf16[160,2304]{1,0:T(8,128)(2,1)S(1)}, bf16[160,2304]{1,0:T(8,128)(2,1)}, u32[]{:S(2)}, u32[]{:S(2)}) collective-permute-start(bf16[160,2304]{1,0:T(8,128)(2,1)S(1)} %get-tuple-element.108), channel_id=1, source_target_pairs={{0,1},{1,0},{2,3},{3,2},{4,5},{5,4},{6,7},{7,6},{8,9},{9,8},{10,11... | collective-permute-start | bytes 2211848 | tf_op jit(solution)/shard_map/ppermute | solution.py:28
  105.9 36.9 %all-to-all-start.2 = ((bf16[8,72,1152]{2,1,0:T(8,128)(2,1)}), bf16[8,72,1152]{2,1,0:T(8,128)(2,1)}, u32[]{:S(2)}, u32[]{:S(2)}) async-start(bf16[8,72,1152]{2,1,0:T(8,128)(2,1)} %copy.171), calls=%async_computation.2 | async-start | bytes 2654208 | tf_op jit(solution)/shard_map/all_to_all | solution.py:187
  143.9 49.0 %all-to-all-start.3 = ((bf16[8,72,1152]{2,1,0:T(8,128)(2,1)}), bf16[8,72,1152]{2,1,0:T(8,128)(2,1)S(1)}, u32[]{:S(2)}, u32[]{:S(2)}) async-start(bf16[8,72,1152]{2,1,0:T(8,128)(2,1)} %copy.172), calls=%async_computation.3 | async-start | bytes 2654208 | tf_op jit(solution)/shard_map/all_to_all | solution.py:187
  148.5 85.4 %all-gather.8.cloned.1.call-start = ((), (), s32[]{:S(2)}) async-start(), calls=%async_computation.16 | async-start | bytes 1474560 | tf_op jit(solution)/shard_map/all_gather | solution.py:192
  149.3 159.0 %all-gather.12.cloned.1.call-start = ((), (), s32[]{:S(2)}) async-start(), calls=%async_computation.18 | async-start | bytes 6635520 | tf_op jit(solution)/shard_map/all_gather | solution.py:192
  149.3 21.0 %collective-permute-start.16 = (bf16[1280,256]{1,0:T(8,128)(2,1)}, bf16[1280,256]{1,0:T(8,128)(2,1)S(1)}, u32[]{:S(2)}, u32[]{:S(2)}) collective-permute-start(bf16[1280,256]{1,0:T(8,128)(2,1)} %bitcast.24), channel_id=1, source_target_pairs={{0,2},{2,0},{1,3},{3,1},{4,6},{6,4},{5,7},{7,5},{8,10},{10,8},{9,1... | collective-permute-start | bytes 1966088 | tf_op jit(solution)/shard_map/ppermute | solution.py:33
  150.9 39.3 %collective-permute-start.18 = (bf16[1280,256]{1,0:T(8,128)(2,1)}, bf16[1280,256]{1,0:T(8,128)(2,1)S(1)}, u32[]{:S(2)}, u32[]{:S(2)}) collective-permute-start(bf16[1280,256]{1,0:T(8,128)(2,1)} %collective-permute-done.17), channel_id=1, source_target_pairs={{0,2},{2,0},{1,3},{3,1},{4,6},{6,4},{5,7},{7,5},{8,10},{10,8},{9,1... | collective-permute-start | bytes 1966088 | tf_op jit(solution)/shard_map/ppermute | solution.py:33
  195.4 37.6 %all-to-all-start.4 = ((bf16[8,72,1152]{2,1,0:T(8,128)(2,1)}), bf16[8,72,1152]{2,1,0:T(8,128)(2,1)}, u32[]{:S(2)}, u32[]{:S(2)}) async-start(bf16[8,72,1152]{2,1,0:T(8,128)(2,1)} %copy.174), calls=%async_computation.4 | async-start | bytes 2654208 | tf_op jit(solution)/shard_map/all_to_all | solution.py:187
  200.4 120.6 %all-gather.10.cloned.1.call-start = ((), (), s32[]{:S(2)}) async-start(), calls=%async_computation.17 | async-start | bytes 6635520 | tf_op jit(solution)/shard_map/all_gather | solution.py:192
  237.4 147.3 %all-gather.14.cloned.1.call-start = ((), (), s32[]{:S(2)}) async-start(), calls=%async_computation.19 | async-start | bytes 6635520 | tf_op jit(solution)/shard_map/all_gather | solution.py:192
  245.9 19.9 %collective-permute-start.21 = (bf16[160,2304]{1,0:T(8,128)(2,1)S(1)}, bf16[160,2304]{1,0:T(8,128)(2,1)S(1)}, u32[]{:S(2)}, u32[]{:S(2)}) collective-permute-start(bf16[160,2304]{1,0:T(8,128)(2,1)S(1)} %slice.817), channel_id=1, source_target_pairs={{0,1},{1,0},{2,3},{3,2},{4,5},{5,4},{6,7},{7,6},{8,9},{9,8},{10,11... | collective-permute-start | bytes 2211848 | tf_op jit(solution)/shard_map/ppermute | solution.py:28
  265.8 18.6 %collective-permute-start.20 = (bf16[160,2304]{1,0:T(8,128)(2,1)}, bf16[160,2304]{1,0:T(8,128)(2,1)S(1)}, u32[]{:S(2)}, u32[]{:S(2)}) collective-permute-start(bf16[160,2304]{1,0:T(8,128)(2,1)} %slice.813), channel_id=1, source_target_pairs={{0,1},{1,0},{2,3},{3,2},{4,5},{5,4},{6,7},{7,6},{8,9},{9,8},{10,11... | collective-permute-start | bytes 2211848 | tf_op jit(solution)/shard_map/ppermute | solution.py:28
  304.3 391.1 %reduce-scatter.6.cloned.1.call-start = ((), (), s32[]{:S(2)}) async-start(), calls=%async_computation.20 | async-start | bytes 6635520 | tf_op jit(solution)/shard_map/reduce_scatter | solution.py:196
  304.4 22.8 %collective-permute-start.30 = (bf16[80,2304]{1,0:T(8,128)(2,1)S(1)}, bf16[80,2304]{1,0:T(8,128)(2,1)S(1)}, u32[]{:S(2)}, u32[]{:S(2)}) collective-permute-start(bf16[80,2304]{1,0:T(8,128)(2,1)S(1)} %get-tuple-element.291), channel_id=1, source_target_pairs={{0,8},{8,16},{16,24},{24,0},{1,9},{9,17},{17,25},{25,1},{2,10},{10... | collective-permute-start | bytes 1105928 | tf_op jit(solution)/shard_map/ppermute | solution.py:33
  305.0 22.2 %collective-permute-start.31 = (bf16[80,2304]{1,0:T(8,128)(2,1)S(1)}, bf16[80,2304]{1,0:T(8,128)(2,1)S(1)}, u32[]{:S(2)}, u32[]{:S(2)}) collective-permute-start(bf16[80,2304]{1,0:T(8,128)(2,1)S(1)} %get-tuple-element.290), channel_id=1, source_target_pairs={{0,24},{8,0},{16,8},{24,16},{1,25},{9,1},{17,9},{25,17},{2,26},{10... | collective-permute-start | bytes 1105928 | tf_op jit(solution)/shard_map/ppermute | solution.py:33
  328.2 21.4 %collective-permute-start.34 = (bf16[80,2304]{1,0:T(8,128)(2,1)S(1)}, bf16[80,2304]{1,0:T(8,128)(2,1)S(1)}, u32[]{:S(2)}, u32[]{:S(2)}) collective-permute-start(bf16[80,2304]{1,0:T(8,128)(2,1)S(1)} %collective-permute-done.30), channel_id=1, source_target_pairs={{0,8},{8,16},{16,24},{24,0},{1,9},{9,17},{17,25},{25,1},{2,10},{10... | collective-permute-start | bytes 1105928 | tf_op jit(solution)/shard_map/ppermute | solution.py:33
  329.7 20.4 %collective-permute-start.35 = (bf16[80,2304]{1,0:T(8,128)(2,1)S(1)}, bf16[80,2304]{1,0:T(8,128)(2,1)S(1)}, u32[]{:S(2)}, u32[]{:S(2)}) collective-permute-start(bf16[80,2304]{1,0:T(8,128)(2,1)S(1)} %collective-permute-done.31), channel_id=1, source_target_pairs={{0,24},{8,0},{16,8},{24,16},{1,25},{9,1},{17,9},{25,17},{2,26},{10... | collective-permute-start | bytes 1105928 | tf_op jit(solution)/shard_map/ppermute | solution.py:33
  405.2 20.9 %collective-permute-start.41 = (bf16[160,2304]{1,0:T(8,128)(2,1)S(1)}, bf16[160,2304]{1,0:T(8,128)(2,1)S(1)}, u32[]{:S(2)}, u32[]{:S(2)}) collective-permute-start(bf16[160,2304]{1,0:T(8,128)(2,1)S(1)} %slice.853), channel_id=1, source_target_pairs={{0,1},{1,0},{2,3},{3,2},{4,5},{5,4},{6,7},{7,6},{8,9},{9,8},{10,11... | collective-permute-start | bytes 2211848 | tf_op jit(solution)/shard_map/ppermute | solution.py:28
  461.9 18.6 %collective-permute-start.51 = (bf16[80,2304]{1,0:T(8,128)(2,1)S(1)}, bf16[80,2304]{1,0:T(8,128)(2,1)S(1)}, u32[]{:S(2)}, u32[]{:S(2)}) collective-permute-start(bf16[80,2304]{1,0:T(8,128)(2,1)S(1)} %get-tuple-element.282), channel_id=1, source_target_pairs={{0,24},{8,0},{16,8},{24,16},{1,25},{9,1},{17,9},{25,17},{2,26},{10... | collective-permute-start | bytes 1105928 | tf_op jit(solution)/shard_map/ppermute | solution.py:33
  519.8 19.2 %collective-permute-start.65 = (bf16[80,2304]{1,0:T(8,128)(2,1)}, bf16[80,2304]{1,0:T(8,128)(2,1)}, u32[]{:S(2)}, u32[]{:S(2)}) collective-permute-start(bf16[80,2304]{1,0:T(8,128)(2,1)} %get-tuple-element.280), channel_id=1, source_target_pairs={{0,24},{8,0},{16,8},{24,16},{1,25},{9,1},{17,9},{25,17},{2,26},{10... | collective-permute-start | bytes 1105928 | tf_op jit(solution)/shard_map/ppermute | solution.py:33
  539.1 215.0 %reduce-scatter.8.cloned.1.call-start = ((), (), s32[]{:S(2)}) async-start(), calls=%async_computation.21 | async-start | bytes 6635520 | tf_op jit(solution)/shard_map/reduce_scatter | solution.py:196
  545.0 22.6 %collective-permute-start.66 = (bf16[80,2304]{1,0:T(8,128)(2,1)}, bf16[80,2304]{1,0:T(8,128)(2,1)S(1)}, u32[]{:S(2)}, u32[]{:S(2)}) collective-permute-start(bf16[80,2304]{1,0:T(8,128)(2,1)} %get-tuple-element.279), channel_id=1, source_target_pairs={{0,8},{8,16},{16,24},{24,0},{1,9},{9,17},{17,25},{25,1},{2,10},{10... | collective-permute-start | bytes 1105928 | tf_op jit(solution)/shard_map/ppermute | solution.py:33
  546.4 21.3 %collective-permute-start.67 = (bf16[80,2304]{1,0:T(8,128)(2,1)}, bf16[80,2304]{1,0:T(8,128)(2,1)}, u32[]{:S(2)}, u32[]{:S(2)}) collective-permute-start(bf16[80,2304]{1,0:T(8,128)(2,1)} %get-tuple-element.278), channel_id=1, source_target_pairs={{0,24},{8,0},{16,8},{24,16},{1,25},{9,1},{17,9},{25,17},{2,26},{10... | collective-permute-start | bytes 1105928 | tf_op jit(solution)/shard_map/ppermute | solution.py:33
  567.7 186.4 %reduce-scatter.10.cloned.1.call-start = ((), (), s32[]{:S(2)}) async-start(), calls=%async_computation.22 | async-start | bytes 6635520 | tf_op jit(solution)/shard_map/reduce_scatter | solution.py:196
  579.1 22.5 %collective-permute-start.53 = (bf16[160,2304]{1,0:T(8,128)(2,1)}, bf16[160,2304]{1,0:T(8,128)(2,1)}, u32[]{:S(2)}, u32[]{:S(2)}) collective-permute-start(bf16[160,2304]{1,0:T(8,128)(2,1)} %slice.691), channel_id=1, source_target_pairs={{0,1},{1,0},{2,3},{3,2},{4,5},{5,4},{6,7},{7,6},{8,9},{9,8},{10,11... | collective-permute-start | bytes 2211848 | tf_op jit(solution)/shard_map/ppermute | solution.py:28
  582.7 18.8 %collective-permute-start.69 = (bf16[80,2304]{1,0:T(8,128)(2,1)}, bf16[80,2304]{1,0:T(8,128)(2,1)}, u32[]{:S(2)}, u32[]{:S(2)}) collective-permute-start(bf16[80,2304]{1,0:T(8,128)(2,1)} %get-tuple-element.270), channel_id=1, source_target_pairs={{0,24},{8,0},{16,8},{24,16},{1,25},{9,1},{17,9},{25,17},{2,26},{10... | collective-permute-start | bytes 1105928 | tf_op jit(solution)/shard_map/ppermute | solution.py:33
  629.9 18.7 %collective-permute-start.71 = (bf16[80,2304]{1,0:T(8,128)(2,1)S(1)}, bf16[80,2304]{1,0:T(8,128)(2,1)S(1)}, u32[]{:S(2)}, u32[]{:S(2)}) collective-permute-start(bf16[80,2304]{1,0:T(8,128)(2,1)S(1)} %get-tuple-element.268), channel_id=1, source_target_pairs={{0,24},{8,0},{16,8},{24,16},{1,25},{9,1},{17,9},{25,17},{2,26},{10... | collective-permute-start | bytes 1105928 | tf_op jit(solution)/shard_map/ppermute | solution.py:33
  695.4 58.8 %all-to-all-start.5 = ((bf16[8,72,1152]{2,1,0:T(8,128)(2,1)}), bf16[8,72,1152]{2,1,0:T(8,128)(2,1)}, u32[]{:S(2)}, u32[]{:S(2)}) async-start(bf16[8,72,1152]{2,1,0:T(8,128)(2,1)} %bitcast.353), calls=%async_computation.6 | async-start | bytes 2654208 | tf_op jit(solution)/shard_map/all_to_all | solution.py:187
  760.0 37.4 %all-to-all-start.6 = ((bf16[8,72,1152]{2,1,0:T(8,128)(2,1)}), bf16[8,72,1152]{2,1,0:T(8,128)(2,1)}, u32[]{:S(2)}, u32[]{:S(2)}) async-start(bf16[8,72,1152]{2,1,0:T(8,128)(2,1)} %bitcast.354), calls=%async_computation.9 | async-start | bytes 2654208 | tf_op jit(solution)/shard_map/all_to_all | solution.py:187
  764.8 68.7 %reduce-scatter.12.cloned.1.call-start = ((), (), s32[]{:S(2)}) async-start(), calls=%async_computation.23 | async-start | bytes 1474560 | tf_op jit(solution)/shard_map/reduce_scatter | solution.py:196
  768.9 19.3 %collective-permute-start.87 = (bf16[1280,256]{1,0:T(8,128)(2,1)S(1)}, bf16[1280,256]{1,0:T(8,128)(2,1)}, u32[]{:S(2)}, u32[]{:S(2)}) collective-permute-start(bf16[1280,256]{1,0:T(8,128)(2,1)S(1)} %get-tuple-element.230), channel_id=1, source_target_pairs={{0,2},{2,0},{1,3},{3,1},{4,6},{6,4},{5,7},{7,5},{8,10},{10,8},{9,1... | collective-permute-start | bytes 1966088 | tf_op jit(solution)/shard_map/ppermute | solution.py:33
  797.4 37.1 %all-to-all-start.7 = ((bf16[8,72,1152]{2,1,0:T(8,128)(2,1)}), bf16[8,72,1152]{2,1,0:T(8,128)(2,1)}, u32[]{:S(2)}, u32[]{:S(2)}) async-start(bf16[8,72,1152]{2,1,0:T(8,128)(2,1)} %bitcast.355), calls=%async_computation.10 | async-start | bytes 2654208 | tf_op jit(solution)/shard_map/all_to_all | solution.py:187
  806.6 19.9 %collective-permute-start.89 = (bf16[1280,256]{1,0:T(8,128)(2,1)S(1)}, bf16[1280,256]{1,0:T(8,128)(2,1)S(1)}, u32[]{:S(2)}, u32[]{:S(2)}) collective-permute-start(bf16[1280,256]{1,0:T(8,128)(2,1)S(1)} %copy-done.67), channel_id=1, source_target_pairs={{0,2},{2,0},{1,3},{3,1},{4,6},{6,4},{5,7},{7,5},{8,10},{10,8},{9,1... | collective-permute-start | bytes 1966088 | tf_op jit(solution)/shard_map/ppermute | solution.py:33
  810.5 21.6 %collective-permute-start.88 = (bf16[1280,256]{1,0:T(8,128)(2,1)S(1)}, bf16[1280,256]{1,0:T(8,128)(2,1)S(1)}, u32[]{:S(2)}, u32[]{:S(2)}) collective-permute-start(bf16[1280,256]{1,0:T(8,128)(2,1)S(1)} %copy-done.68), channel_id=1, source_target_pairs={{0,4},{4,0},{1,5},{5,1},{2,6},{6,2},{3,7},{7,3},{8,12},{12,8},{9,1... | collective-permute-start | bytes 1966088 | tf_op jit(solution)/shard_map/ppermute | solution.py:33
  854.8 20.8 %all-to-all-start.8 = ((bf16[8,72,256]{2,1,0:T(8,128)(2,1)}), bf16[8,72,256]{2,1,0:T(8,128)(2,1)}, u32[]{:S(2)}, u32[]{:S(2)}) async-start(bf16[8,72,256]{2,1,0:T(8,128)(2,1)} %bitcast.74), calls=%async_computation.12 | async-start | bytes 589824 | tf_op jit(solution)/shard_map/all_to_all | solution.py:187
  858.9 67.0 %reduce-scatter.14.cloned.1.call-start = ((), (), s32[]{:S(2)}) async-start(), calls=%async_computation.24 | async-start | bytes 2949120 | tf_op jit(solution)/shard_map/reduce_scatter | solution.py:196
  862.6 23.0 %collective-permute-start.92 = (bf16[160,2304]{1,0:T(8,128)(2,1)}, bf16[160,2304]{1,0:T(8,128)(2,1)}, u32[]{:S(2)}, u32[]{:S(2)}) collective-permute-start(bf16[160,2304]{1,0:T(8,128)(2,1)} %slice.959), channel_id=1, source_target_pairs={{0,1},{1,0},{2,3},{3,2},{4,5},{5,4},{6,7},{7,6},{8,9},{9,8},{10,11... | collective-permute-start | bytes 2211848 | tf_op jit(solution)/shard_map/ppermute | solution.py:28
  866.8 18.8 %collective-permute-start.95 = (bf16[80,2304]{1,0:T(8,128)(2,1)}, bf16[80,2304]{1,0:T(8,128)(2,1)}, u32[]{:S(2)}, u32[]{:S(2)}) collective-permute-start(bf16[80,2304]{1,0:T(8,128)(2,1)} %get-tuple-element.266), channel_id=1, source_target_pairs={{0,24},{8,0},{16,8},{24,16},{1,25},{9,1},{17,9},{25,17},{2,26},{10... | collective-permute-start | bytes 1105928 | tf_op jit(solution)/shard_map/ppermute | solution.py:33
  875.6 21.2 %collective-permute-start.91 = (bf16[160,2304]{1,0:T(8,128)(2,1)}, bf16[160,2304]{1,0:T(8,128)(2,1)S(1)}, u32[]{:S(2)}, u32[]{:S(2)}) collective-permute-start(bf16[160,2304]{1,0:T(8,128)(2,1)} %slice.957), channel_id=1, source_target_pairs={{0,1},{1,0},{2,3},{3,2},{4,5},{5,4},{6,7},{7,6},{8,9},{9,8},{10,11... | collective-permute-start | bytes 2211848 | tf_op jit(solution)/shard_map/ppermute | solution.py:28
  896.6 19.1 %collective-permute-start.90 = (bf16[160,2304]{1,0:T(8,128)(2,1)S(1)}, bf16[160,2304]{1,0:T(8,128)(2,1)S(1)}, u32[]{:S(2)}, u32[]{:S(2)}) collective-permute-start(bf16[160,2304]{1,0:T(8,128)(2,1)S(1)} %slice.955), channel_id=1, source_target_pairs={{0,1},{1,0},{2,3},{3,2},{4,5},{5,4},{6,7},{7,6},{8,9},{9,8},{10,11... | collective-permute-start | bytes 2211848 | tf_op jit(solution)/shard_map/ppermute | solution.py:28
  925.9 20.4 %all-to-all-start.9 = ((bf16[8,72,512]{2,1,0:T(8,128)(2,1)}), bf16[8,72,512]{2,1,0:T(8,128)(2,1)S(1)}, u32[]{:S(2)}, u32[]{:S(2)}) async-start(bf16[8,72,512]{2,1,0:T(8,128)(2,1)} %bitcast.384), calls=%async_computation.14 | async-start | bytes 1179648 | tf_op jit(solution)/shard_map/all_to_all | solution.py:187
  (227 other events, 2487.4 us)
Sparse Core Ops, SparseCore 0:
  46.7 36.7 all-gather.5
  151.2 38.8 all-gather.7
  194.1 63.1 all-gather.11
  259.0 61.9 all-gather.9
  322.7 61.9 all-gather.13
  539.2 60.5 reduce-scatter.5
  602.8 62.0 reduce-scatter.7
  668.0 61.9 reduce-scatter.9
  776.6 37.7 reduce-scatter.11
  870.9 44.0 reduce-scatter.13

commit v2 on v1

v2 whole, which is shorter than its diff:
```python
import jax
import jax.numpy as jnp
from jax import lax
from jax.experimental import pallas as pl
from jax.experimental.pallas import tpu as pltpu
from jax.sharding import Mesh
from jax.sharding import PartitionSpec as P

HEADS = 8
KV_HEADS = 4
HEAD = 256
WINDOW = 4096
CAP = 10.0
EPS = 1e-06
SCALE = HEAD**-0.5
BLOCK = 256

RING = 4
AXES = ("z", "b", "y", "c")
GROUP = ("z", "c")
COPIES = ("b", "y")

bf16 = jnp.bfloat16
f32 = jnp.float32


def swapped(value, axis):
    return lax.ppermute(value, axis, [(0, 1), (1, 0)])


def rotated(value, axis, steps):
    count = lax.axis_size(axis)
    return lax.ppermute(value, axis, [(i, (i + steps) % count) for i in range(count)])


def copies_apart():
    return [(k, j) for k in range(lax.axis_size("b")) for j in range(lax.axis_size("y"))]


def moved_on(value, k, j, back=False):
    if k == 0 and j == 0:
        return value
    count_b, count_y = lax.axis_size("b"), lax.axis_size("y")
    pairs = [
        (b * count_y + y, (b + k) % count_b * count_y + (y + j) % count_y)
        for b in range(count_b)
        for y in range(count_y)
    ]
    return lax.ppermute(value, COPIES, [(t, f) if back else (f, t) for f, t in pairs])


def join(*values):
    return lax.optimization_barrier(values)


def dot_nn(left, right):
    return lax.dot_general(left, right, (((1,), (0,)), ((), ())), preferred_element_type=f32)


def dot_nt(left, right):
    return lax.dot_general(left, right, (((1,), (1,)), ((), ())), preferred_element_type=f32)


def dot_tn(left, right):
    return lax.dot_general(left, right, (((0,), (0,)), ((), ())), preferred_element_type=f32)


def moved(values, first, second):
    rest = values.shape[1] // (first * second)
    starts = [(i * second + j) * rest for j in range(second) for i in range(first)]
    return jnp.concatenate([values[:, s : s + rest] for s in starts], axis=1)


def copies_first(values, normed=False):
    rows, width = values.shape
    copies = lax.axis_size("b") * lax.axis_size("y")

    def kernel(in_ref, out_ref, *normed_refs):
        here = moved(in_ref[...].astype(f32), RING, copies)
        out_ref[...] = here.astype(out_ref.dtype)
        if normed:
            inverse = lax.rsqrt(jnp.mean(here * here, axis=1, keepdims=True) + EPS)
            normed_refs[0][...] = (here * inverse).astype(bf16)
            normed_refs[1][...] = inverse

    out_shape = [jax.ShapeDtypeStruct((rows, width), values.dtype)]
    if normed:
        out_shape.append(jax.ShapeDtypeStruct((rows, width), bf16))
        out_shape.append(jax.ShapeDtypeStruct((rows, 1), f32))
    result = pl.pallas_call(
        kernel,
        out_shape=out_shape,
        compiler_params=pltpu.CompilerParams(vmem_limit_bytes=24 << 20),
        cost_estimate=pl.CostEstimate(
            flops=rows * width, bytes_accessed=8 * rows * width, transcendentals=0
        ),
        name="copies_first",
    )(values)
    return result if normed else result[0]


def copies_back(values):
    rows, width = values.shape
    copies = lax.axis_size("b") * lax.axis_size("y")

    def kernel(in_ref, out_ref):
        out_ref[...] = moved(in_ref[...].astype(f32), copies, RING).astype(out_ref.dtype)

    return pl.pallas_call(
        kernel,
        out_shape=jax.ShapeDtypeStruct((rows, width), values.dtype),
        compiler_params=pltpu.CompilerParams(vmem_limit_bytes=24 << 20),
        cost_estimate=pl.CostEstimate(
            flops=rows * width, bytes_accessed=8 * rows * width, transcendentals=0
        ),
        name="copies_back",
    )(values)


def round_ring(value):
    pairs = [(2 * i, (i + 1) % RING * 2) for i in range(RING)]
    pairs += [(2 * i + 1, (i - 1) % RING * 2 + 1) for i in range(RING)]
    return lax.ppermute(value, GROUP, pairs)


def gather_tokens(own, work=None, beside=(None, None, None)):
    here = own
    chunks, results = [jnp.concatenate([own, swapped(own, "c")], axis=0)], []
    beside = list(beside)
    for step in range(RING):
        results.append(work(step, chunks[step]) if work else ())
        if step == RING - 1:
            return chunks, results, beside
        here = round_ring(here)
        extra = beside[step] or ()
        if results[step] or extra:
            here, results[step], beside[step] = join(here, results[step], extra)
        chunks.append(jnp.concatenate([here, swapped(here, "c")], axis=0))


def relative_places():
    place = None
    for axis in AXES:
        count = lax.axis_size(axis)
        at = (lax.axis_index(axis) - jnp.arange(count, dtype=jnp.int32)) % count
        place = at if place is None else (place[:, None] * count + at[None, :]).reshape(-1)
    return place


def gather_small(value):
    for axis in AXES[::-1]:
        parts = [value] + [rotated(value, axis, k) for k in range(1, lax.axis_size(axis))]
        value = jnp.concatenate(parts, axis=0)
    place = relative_places()
    chosen = place[None, :] == jnp.arange(place.shape[0], dtype=jnp.int32)[:, None]
    return dot_nn(chosen.astype(value.dtype), value)


def scatter_small(value):
    place = relative_places()
    chosen = place[:, None] == jnp.arange(place.shape[0], dtype=jnp.int32)[None, :]
    value = jnp.dot(
        chosen.astype(f32), value, precision=lax.Precision.HIGHEST, preferred_element_type=f32
    )
    for axis in AXES:
        count = lax.axis_size(axis)
        parts = value.reshape(count, -1, value.shape[1])
        total = parts[0]
        for k in range(1, count):
            total = total + rotated(parts[k], axis, -k)
        value = total
    return value[0]


def scatter_tokens(chunks, beside=(None, None, None)):
    rows = chunks[0].shape[0] // 2
    carried = None
    beside = list(beside)
    for step in range(RING):
        chunk = chunks[(step + 1) % RING]
        here = chunk[:rows].astype(f32) + swapped(chunk[rows:], "c").astype(f32)
        if carried is not None:
            here = here + carried.astype(f32)
        if step == RING - 1:
            return here, beside
        carried = round_ring(here.astype(bf16))
        if callable(beside[step]):
            beside[step] = beside[step](beside[step - 1])
        if beside[step] is not None:
            carried, *beside[step] = join(carried, *beside[step])


def exchange(blocks):
    return lax.all_to_all(blocks, GROUP, split_axis=0, concat_axis=0, tiled=True)


def gather_rows(blocks):
    parts, rows, cols = blocks.shape
    return lax.all_gather(blocks.reshape(parts * rows, cols), COPIES, axis=0, tiled=True)


def scatter_rows(grad):
    total = lax.psum_scatter(grad, COPIES, scatter_dimension=0, tiled=True)
    return total.reshape(8, -1, grad.shape[1])


def split_cols(weight):
    rows, cols = weight.shape
    return weight.reshape(rows, 8, cols // 8).transpose(1, 0, 2)


def join_cols(blocks):
    parts, rows, cols = blocks.shape
    return blocks.transpose(1, 0, 2).reshape(rows, parts * cols)


def attention_forward(q, kv_mine, kv_other, meta, run):
    tokens = q.shape[0]
    keys = kv_mine.shape[0]
    block = 2 * run
    q_runs = tokens // run
    steps = tokens // block

    def kernel(meta_ref, q_ref, mine_ref, other_ref, o_ref, lse_ref, acc_ref, sum_ref):
        i = pl.program_id(0)
        core = meta_ref[0]
        q_lows = [meta_ref[1 + 2 * i], meta_ref[2 + 2 * i]]
        acc_ref[...] = jnp.zeros_like(acc_ref)
        sum_ref[...] = jnp.zeros_like(sum_ref)
        lane = lax.broadcasted_iota(jnp.int32, (1, block), 1)
        row = lax.broadcasted_iota(jnp.int32, (block, 1), 0)
        q_pos = row + jnp.where(row < run, q_lows[0], q_lows[1] - run)

        def step(j, carry):
            one = meta_ref[1 + q_runs + 2 * j]
            two = meta_ref[2 + q_runs + 2 * j]

            used = [
                (q_low + run > low) & (q_low - (low + run) < WINDOW)
                for q_low in q_lows
                for low in (one, two)
            ]

            @pl.when(used[0] | used[1] | used[2] | used[3])
            def _():
                place = pl.ds(pl.multiple_of(j * block, block), block)
                mine, other = mine_ref[place, :], other_ref[place, :]
                key = jnp.where(core == 0, mine, other)
                value = jnp.where(core == 0, other, mine)
                scores = dot_nt(q_ref[...], key)
                turned = jnp.tanh(scores * (SCALE / CAP))
                k_pos = lane + jnp.where(lane < run, one, two - run)
                away = q_pos - k_pos
                weight = jnp.where((away >= 0) & (away < WINDOW), jnp.exp(turned * CAP), 0.0)
                sum_ref[...] += jnp.sum(weight, axis=1, keepdims=True)
                acc_ref[...] += dot_nn(weight.astype(bf16), value)

            return carry

        lax.fori_loop(0, keys // block, step, 0)
        total = sum_ref[...]
        o_ref[...] = acc_ref[...] / total
        lse_ref[...] = jnp.log(total)

    return pl.pallas_call(
        kernel,
        grid=(steps,),
        in_specs=[
            pl.BlockSpec(memory_space=pltpu.SMEM),
            pl.BlockSpec((block, HEAD), lambda i: (i, 0)),
            pl.BlockSpec(memory_space=pltpu.VMEM),
            pl.BlockSpec(memory_space=pltpu.VMEM),
        ],
        out_specs=[
            pl.BlockSpec((block, HEAD), lambda i: (i, 0)),
            pl.BlockSpec((block, 1), lambda i: (i, 0)),
        ],
        out_shape=[
            jax.ShapeDtypeStruct((tokens, HEAD), f32),
            jax.ShapeDtypeStruct((tokens, 1), f32),
        ],
        scratch_shapes=[pltpu.VMEM((block, HEAD), f32), pltpu.VMEM((block, 1), f32)],
        compiler_params=pltpu.CompilerParams(vmem_limit_bytes=4 * kv_mine.size + (12 << 20)),
        cost_estimate=pl.CostEstimate(
            flops=4 * tokens * keys * HEAD,
            bytes_accessed=4 * kv_mine.size + 8 * tokens * HEAD,
            transcendentals=2 * tokens * keys,
        ),
        name="attention_forward",
    )(meta, q, kv_mine, kv_other)


def attention_backward(q, d_out, kv_mine, kv_other, meta, lse, delta, run):
    tokens = q.shape[0]
    keys = kv_mine.shape[0]
    q_block = 2 * run
    block_k = 2 * run
    steps = tokens // q_block
    key_steps = keys // block_k
    q_runs, last = tokens // run, keys // run - 1

    def kernel(
        meta_ref, q_ref, d_ref, mine_ref, other_ref, lse_ref, delta_ref,
        dq_ref, d_mine_ref, d_other_ref, key_acc, value_acc, key_ref, value_ref,
    ):
        j = pl.program_id(0)
        core = meta_ref[0]
        at = j * block_k
        one = at // run
        two = jnp.minimum((at + block_k - 1) // run, last)
        one_pos = meta_ref[1 + q_runs + one] + at - one * run
        two_pos = meta_ref[1 + q_runs + two] + at - two * run
        turn_at = jnp.minimum((one + 1) * run - at, block_k)
        row = lax.broadcasted_iota(jnp.int32, (block_k, 1), 0)
        k_pos = row + jnp.where(row < turn_at, one_pos, two_pos)
        k_runs = [(one_pos, turn_at), (two_pos + turn_at, block_k - turn_at)]

        @pl.when(j == 0)
        def _():
            dq_ref[...] = jnp.zeros_like(dq_ref)

        key_acc[...] = jnp.zeros_like(key_acc)
        value_acc[...] = jnp.zeros_like(value_acc)
        key_ref[...] = jnp.where(core == 0, mine_ref[...], other_ref[...])
        value_ref[...] = jnp.where(core == 0, other_ref[...], mine_ref[...])
        for i in range(steps):
            q_runs_here = []
            first = i * q_block
            while first < (i + 1) * q_block:
                number = first // run
                stop = min((number + 1) * run, (i + 1) * q_block)
                q_runs_here.append((first, stop, meta_ref[1 + number] - number * run))
                first = stop
            used = None
            for first, stop, q_shift in q_runs_here:
                for low, size in k_runs:
                    here = (q_shift + stop > low) & (q_shift + first - (low + size) < WINDOW)
                    here = here & (size > 0)
                    used = here if used is None else used | here

            @pl.when(used)
            def _(i=i, q_runs_here=q_runs_here):
                place = pl.ds(i * q_block, q_block)
                key = key_ref[...]
                value = value_ref[...]
                query = q_ref[place, :]
                d_here = d_ref[place, :]
                turned = jnp.tanh(dot_nt(key, query) * (SCALE / CAP))
                lane = lax.broadcasted_iota(jnp.int32, (1, q_block), 1) + i * q_block
                q_pos = lane + q_runs_here[-1][2]
                for first, stop, q_shift in q_runs_here[-2::-1]:
                    q_pos = jnp.where(lane < stop, lane + q_shift, q_pos)
                away = q_pos - k_pos
                soft = jnp.where(
                    (away >= 0) & (away < WINDOW),
                    jnp.exp(turned * CAP - lse_ref[:, place]),
                    0.0,
                )
                d_prob = dot_nt(value, d_here)
                d_raw = soft * (d_prob - delta_ref[:, place]) * (1.0 - turned * turned)
                d_raw = d_raw.astype(bf16)
                value_acc[...] += dot_nn(soft.astype(bf16), d_here)
                key_acc[...] += dot_nn(d_raw, query)
                dq_ref[place, :] += dot_tn(d_raw, key)

        d_key, d_value = (key_acc[...] * SCALE).astype(bf16), value_acc[...].astype(bf16)
        d_mine_ref[...] = jnp.where(core == 0, d_key, d_value)
        d_other_ref[...] = jnp.where(core == 0, d_value, d_key)

        @pl.when(j == key_steps - 1)
        def _():
            dq_ref[...] = dq_ref[...] * SCALE

    whole = pl.BlockSpec(memory_space=pltpu.VMEM)
    block = pl.BlockSpec((block_k, HEAD), lambda j: (j, 0))
    return pl.pallas_call(
        kernel,
        grid=(key_steps,),
        in_specs=[
            pl.BlockSpec(memory_space=pltpu.SMEM),
            whole,
            whole,
            block,
            block,
            whole,
            whole,
        ],
        out_specs=[whole, block, block],
        out_shape=[
            jax.ShapeDtypeStruct((tokens, HEAD), f32),
            jax.ShapeDtypeStruct((keys, HEAD), bf16),
            jax.ShapeDtypeStruct((keys, HEAD), bf16),
        ],
        scratch_shapes=[
            pltpu.VMEM((block_k, HEAD), f32),
            pltpu.VMEM((block_k, HEAD), f32),
            pltpu.VMEM((block_k, HEAD), bf16),
            pltpu.VMEM((block_k, HEAD), bf16),
        ],
        compiler_params=pltpu.CompilerParams(vmem_limit_bytes=24 << 20),
        cost_estimate=pl.CostEstimate(
            flops=10 * tokens * keys * HEAD,
            bytes_accessed=8 * kv_mine.size + 8 * tokens * HEAD,
            transcendentals=2 * tokens * keys,
        ),
        name="attention_backward",
    )(meta, q, d_out, kv_mine, kv_other, lse, delta)


def rotated_halves(values, cosine, sine):
    half = HEAD // 2
    a, b = values[:, :half], values[:, half:]
    return jnp.concatenate([a * cosine - b * sine, b * cosine + a * sine], axis=1)


BACK = [0] + list(range(RING - 1, 0, -1))


def call_on_rows(kernel, name, out_shape, *operands):
    size = sum(x.size * x.dtype.itemsize for x in operands)
    return pl.pallas_call(
        kernel,
        in_specs=[pl.BlockSpec(memory_space=pltpu.SMEM)]
        + [pl.BlockSpec(memory_space=pltpu.VMEM)] * (len(operands) - 1),
        out_shape=out_shape,
        compiler_params=pltpu.CompilerParams(vmem_limit_bytes=24 << 20),
        cost_estimate=pl.CostEstimate(flops=size, bytes_accessed=2 * size, transcendentals=0),
        name=name,
    )(*operands)


def to_blocks(chunks, core, tables=None):
    tok, width = chunks[0].shape[0] // 2, chunks[0].shape[1]
    heads = width // HEAD

    def kernel(core_ref, *refs):
        first = core_ref[0] == 0
        outs = refs[-heads:]
        for d in range(RING):
            for e in range(2):
                one = refs[BACK[d] if e else d][e * tok : (e + 1) * tok, :]
                two = refs[BACK[d] if e else d][(1 - e) * tok : (2 - e) * tok, :]
                here = jnp.where(first, one, two)
                place = pl.ds((2 * d + e) * tok, tok)
                for h in range(heads):
                    part = here[:, h * HEAD : (h + 1) * HEAD]
                    if tables is not None:
                        cosine, sine = refs[RING][place, :], refs[RING + 1][place, :]
                        turned = rotated_halves(part, cosine, sine)
                        part = jnp.where(first, turned, part) if h else turned
                    outs[h][place, :] = part.astype(bf16)

    shape = jax.ShapeDtypeStruct((2 * RING * tok, HEAD), bf16)
    return call_on_rows(kernel, "to_blocks", [shape] * heads, core, *chunks, *(tables or ()))


def to_chunks(values, core, tables=None, keyed=False):
    tok = values.shape[0] // (2 * RING)

    def kernel(core_ref, *refs):
        first = core_ref[0] == 0
        for s in range(RING):
            for p in range(2):
                parts = []
                for d, e in ((BACK[s] if p else s, p), (s if p else BACK[s], 1 - p)):
                    place = pl.ds((2 * d + e) * tok, tok)
                    part = refs[0][place, :]
                    if tables is not None:
                        cosine, sine = refs[1][place, :], refs[2][place, :]
                        turned = rotated_halves(part, cosine, -sine)
                        part = jnp.where(first, turned, part) if keyed else turned
                    parts.append(part)
                here = jnp.where(first, parts[0], parts[1])
                refs[-1][pl.ds((2 * s + p) * tok, tok), :] = here.astype(bf16)

    shape = jax.ShapeDtypeStruct(values.shape, bf16)
    return call_on_rows(kernel, "to_chunks", shape, core, values, *(tables or ()))


def mean(values):
    return jnp.mean(values, axis=1, keepdims=True)


def gelu_parts(u):
    k = 0.7978845608028654
    t = jnp.tanh(k * (u + 0.044715 * u * u * u))
    value = 0.5 * u * (1.0 + t)
    slope = 0.5 * (1.0 + t) + 0.5 * u * (1.0 - t * t) * k * (1.0 + 3 * 0.044715 * u * u)
    return value, slope


def body(
    inputs,
    cotangent,
    w_query,
    w_key,
    w_value,
    w_out_t,
    w_gate,
    w_up,
    w_down_t,
    gain_attn_in,
    gain_attn_out,
    gain_mlp_in,
    gain_mlp_out,
):
    tok, width = inputs.shape
    rows = w_query.shape[0]
    count_b, count_y = lax.axis_size("b"), lax.axis_size("y")
    z, b, y, c = [lax.axis_index(name) for name in AXES]

    g_attn = gain_attn_in.astype(f32)[:, None]
    g_mlp = gain_mlp_in.astype(f32)[:, None]

    def scaled(weight, gain):
        return (weight.astype(f32) * gain).astype(bf16)

    pairs = jnp.stack(
        [w_key.reshape(rows, KV_HEADS, HEAD), w_value.reshape(rows, KV_HEADS, HEAD)], axis=2
    ).reshape(rows, 8, HEAD)
    qkv_pack = jnp.concatenate([w_query.reshape(rows, 8, HEAD), pairs], axis=2)
    qkv_pack = (qkv_pack.astype(f32) * g_attn[:, :, None]).astype(bf16)
    qkv_pack = jnp.concatenate([qkv_pack, w_out_t.reshape(rows, 8, HEAD)], axis=2)
    qkv_pack = qkv_pack.transpose(1, 0, 2)
    x, normed_x, r1 = copies_first(inputs, normed=True)
    x = x.astype(f32)
    gate_pack = split_cols(scaled(w_gate, g_mlp))
    up_pack = split_cols(scaled(w_up, g_mlp))
    down_pack = split_cols(w_down_t)
    qkv_w = gather_rows(exchange(qkv_pack))
    qkv_w, out_w = qkv_w[:, : 2 * HEAD], qkv_w[:, 2 * HEAD :]
    gains = jnp.concatenate([gain_attn_out, gain_mlp_out])[None]
    gains = gather_small(gains)
    x1, _, (_, _, (gate_pack,)) = gather_tokens(normed_x, None, (None, None, (gate_pack,)))
    gate_mine = exchange(gate_pack)
    qkv = [dot_nn(part, qkv_w) for part in x1]
    run = 2 * tok

    def starts(places_b, places_y):
        blocks = (z - jnp.arange(RING, dtype=jnp.int32)) % RING
        place = (blocks * count_b + places_b[:, None, None]) * count_y + places_y[:, None]
        return place.reshape(-1) * run

    q_starts = starts(b[None], y[None])
    k_starts = starts(
        (b - jnp.arange(count_b, dtype=jnp.int32)) % count_b,
        (y - jnp.arange(count_y, dtype=jnp.int32)) % count_y,
    )
    meta = jnp.concatenate([c.astype(jnp.int32)[None], q_starts, k_starts])

    core = c.astype(jnp.int32)[None]
    q_pos = (q_starts[:, None] + jnp.arange(run, dtype=jnp.int32)).reshape(-1)
    frequency = 10000.0 ** (-jnp.arange(HEAD // 2, dtype=f32) * 2.0 / HEAD)
    angles = q_pos.astype(f32)[:, None] * frequency[None, :]
    tables = (jnp.cos(angles), jnp.sin(angles))

    q, own_kv = to_blocks(qkv, core, tables)
    kv_mine = jnp.concatenate([moved_on(own_kv, k, j) for k, j in copies_apart()], axis=0)
    kv_mine, gate_mine, up_pack, gains = join(kv_mine, gate_mine, up_pack, gains)
    ff_cols = w_gate.shape[1] // 8
    gate_w = gather_rows(gate_mine)
    up_mine = exchange(up_pack)
    kv_other = swapped(kv_mine, "c")
    attended, lse = attention_forward(q, kv_mine, kv_other, meta, run)
    attended, up_mine, down_pack = join(attended, up_mine, down_pack)
    up_w = gather_rows(up_mine)
    down_mine = exchange(down_pack)
    g_attn_out = moved(gains[:, :rows].reshape(1, width), RING, count_b * count_y)
    g_mlp_out = moved(gains[:, rows:].reshape(1, width), RING, count_b * count_y)
    attended_b = to_chunks(attended, core)
    size = 2 * tok

    def cut(values):
        return [values[i * size : (i + 1) * size] for i in range(RING)]

    projected, ((gate_w,), (down_mine,), _) = scatter_tokens(
        [dot_nt(part, out_w).astype(bf16) for part in cut(attended_b)],
        ((gate_w,), (down_mine,), None),
    )
    down_w = gather_rows(down_mine)
    r2 = lax.rsqrt(mean(projected * projected) + EPS)
    hidden = x + projected * r2 * g_attn_out

    r3 = lax.rsqrt(mean(hidden * hidden) + EPS)
    def mlp_forward(i, part):
        gate = dot_nn(part, gate_w).astype(bf16)
        up = dot_nn(part, up_w).astype(bf16)
        return gate, up, (gelu_parts(gate.astype(f32))[0] * up.astype(f32)).astype(bf16)

    x2, mlp, _ = gather_tokens((hidden * r3).astype(bf16), mlp_forward)
    gate, up, mixed = zip(*mlp)
    *x1, hidden = join(*x1, hidden)
    x1, x2, all_mixed = [jnp.concatenate(parts, axis=0) for parts in (x1, x2, mixed)]
    reduced, ((x2,), (x1, all_mixed), _) = scatter_tokens(
        [dot_nt(part, down_w).astype(bf16) for part in mixed], ((x2,), (x1, all_mixed), None)
    )
    r4 = lax.rsqrt(mean(reduced * reduced) + EPS)

    top = copies_first(cotangent).astype(f32)
    lifted = top * g_mlp_out
    d_reduced = r4 * lifted - reduced * (r4 * r4 * r4 * mean(lifted * reduced))
    def mlp_backward(i, part):
        d_mixed = dot_nn(part, down_w)
        gelu, slope = gelu_parts(gate[i].astype(f32))
        d_gate = (d_mixed * up[i].astype(f32) * slope).astype(bf16)
        d_up = (d_mixed * gelu).astype(bf16)
        return d_gate, d_up, (dot_nt(d_gate, gate_w) + dot_nt(d_up, up_w)).astype(bf16)

    x3, mlp, _ = gather_tokens(d_reduced.astype(bf16), mlp_backward)
    d_gate, d_up, dn3 = zip(*mlp)
    x3 = jnp.concatenate(x3, axis=0)
    down_part = dot_tn(x3, all_mixed).astype(bf16)
    gate_part = dot_tn(x2, jnp.concatenate(d_gate, axis=0)).astype(bf16)
    up_part = dot_tn(x2, jnp.concatenate(d_up, axis=0)).astype(bf16)
    dn3, ((down_part,), (gate_part,), (up_part,)) = scatter_tokens(
        dn3, ((down_part,), (gate_part,), (up_part,))
    )
    down_rows, gate_rows, up_rows = [scatter_rows(p) for p in (down_part, gate_part, up_part)]
    d_hidden = top + r3 * dn3 - hidden * (r3 * r3 * r3 * mean(dn3 * hidden))
    lifted = d_hidden * g_attn_out
    d_projected = r2 * lifted - projected * (r2 * r2 * r2 * mean(lifted * projected))
    d_projected, d_hidden, reduced = join(d_projected.astype(bf16), d_hidden, reduced)
    output = copies_back((hidden + reduced * r4 * g_mlp_out).astype(bf16))
    d_gain_mlp_out = jnp.sum(top * reduced * r4, axis=0, keepdims=True)
    d_gain_attn_out = jnp.sum(d_hidden * projected * r2, axis=0, keepdims=True)
    d_gains = jnp.concatenate(
        [
            moved(d_gain_attn_out, count_b * count_y, RING).reshape(-1, rows),
            moved(d_gain_mlp_out, count_b * count_y, RING).reshape(-1, rows),
        ],
        axis=1,
    )
    d_gains = scatter_small(d_gains)
    x4, d_attended, ((output,), _, _) = gather_tokens(
        d_projected, lambda i, part: (dot_nn(part, out_w).astype(bf16),), ((output,), None, None)
    )
    (d_attended,) = to_blocks([part[0] for part in d_attended], core)
    delta = jnp.sum(d_attended.astype(f32) * attended, axis=1)
    delta, down_rows, gate_rows, d_gains = join(delta, down_rows, gate_rows, d_gains)
    down_sum = exchange(down_rows)
    d_query, d_mine, d_other = attention_backward(
        q, d_attended, kv_mine, kv_other, meta, lse.reshape(1, -1), delta[None], run
    )
    d_query, d_mine, d_other, down_sum, gate_rows = join(
        d_query, d_mine, d_other, down_sum, gate_rows
    )
    gate_sum = exchange(gate_rows)
    d_mine = (d_mine.astype(f32) + swapped(d_other, "c").astype(f32)).astype(bf16)
    d_parts = d_mine.reshape(count_b * count_y, -1, HEAD)
    d_own = sum(
        moved_on(part, k, j, back=True).astype(f32) for part, (k, j) in zip(d_parts, copies_apart())
    )
    d_own, d_query, *x4, gate_sum, up_rows = join(d_own, d_query, *x4, gate_sum, up_rows)
    up_sum = exchange(up_rows)
    d_q = to_chunks(d_query, core, tables)
    d_k = to_chunks(d_own, core, tables, keyed=True)
    d_qkv = jnp.concatenate([d_q, d_k], axis=1)
    q_part = dot_tn(x1, d_q)
    out_part = dot_tn(jnp.concatenate(x4, axis=0), attended_b)
    q_part = jnp.concatenate([q_part, out_part], axis=1).astype(bf16)
    kv_part = dot_tn(x1, d_k).astype(bf16)
    d_qkv, q_part, kv_part = join(d_qkv, q_part, kv_part)
    q_rows, kv_rows = scatter_rows(q_part), scatter_rows(kv_part)
    dn1, (_, (up_sum, _), (q_sum, kv_rows)) = scatter_tokens(
        [dot_nt(part, qkv_w).astype(bf16) for part in cut(d_qkv)],
        (None, (up_sum, q_rows), lambda before: (exchange(before[1]), kv_rows)),
    )
    kv_sum = exchange(kv_rows)
    down_sum, gate_sum, up_sum, q_sum, kv_sum = [
        part.astype(f32) for part in (down_sum, gate_sum, up_sum, q_sum, kv_sum)
    ]
    q_sum, out_sum = join_cols(q_sum[:, :, :HEAD]), join_cols(q_sum[:, :, HEAD:])
    kv_sum = kv_sum.reshape(KV_HEADS, 2, rows, HEAD)
    d_source = r1 * dn1 - x * (r1 * r1 * r1 * mean(dn1 * x))
    input_grad = copies_back((d_hidden + d_source).astype(bf16))

    k_sum, v_sum = join_cols(kv_sum[:, 0]), join_cols(kv_sum[:, 1])
    gate_sum, up_sum = join_cols(gate_sum), join_cols(up_sum)

    def row_term(weight, grad):
        return jnp.sum(weight.astype(f32) * grad, axis=1)

    d_gain_attn_in = (
        row_term(w_query, q_sum) + row_term(w_key, k_sum) + row_term(w_value, v_sum)
    )
    d_gain_mlp_in = row_term(w_gate, gate_sum) + row_term(w_up, up_sum)
    return (
        output,
        input_grad,
        q_sum * g_attn,
        k_sum * g_attn,
        v_sum * g_attn,
        out_sum,
        gate_sum * g_mlp,
        up_sum * g_mlp,
        join_cols(down_sum),
        d_gain_attn_in,
        d_gains[:rows],
        d_gain_mlp_in,
        d_gains[rows:],
    )


def solution(mesh):
    ctx, fsdp = mesh.devices.shape
    laid = Mesh(mesh.devices.reshape(RING, ctx // RING, fsdp // 2, 2), AXES)
    rows = P(AXES, None)
    line = P(AXES)
    return jax.shard_map(
        body,
        mesh=laid,
        in_specs=(rows,) * 9 + (line,) * 4,
        out_specs=(rows,) * 9 + (line,) * 4,
        check_vma=False,
    )
```

time: 974 us -> 904 us (0.928)
  starting transfers between devices: 186 us -> 126 us
  Pallas kernels: 68.7 us -> 54.6 us
  matrix products: 157 us -> 171 us
    ppermute x0 -> x30, waiting for transfers between devices: none -> 283 us  [the longest x24 243 us: round_ring(): return lax.ppermute(value, GROUP, pairs)]
    ppermute x66 -> x12, waiting for transfers between devices: 264 us -> 5.31 us  [rotated(): lax.ppermute(value, axis, [(i, (i + steps) % count) for i in range(count)])]
    ppermute x66 -> x12, starting transfers between devices: 136 us -> 23.1 us  [rotated(): lax.ppermute(value, axis, [(i, (i + steps) % count) for i in range(count)])]
    ppermute x0 -> x30, starting transfers between devices: none -> 41.8 us  [the longest x24 34.7 us: round_ring(): return lax.ppermute(value, GROUP, pairs)]
    all_gather x5 -> x4, waiting for transfers between devices: 15.5 us -> 0.01 us  [gather_rows(): lax.all_gather(blocks.reshape(parts * rows, cols), COPIES, axis=0, tiled=...]
    ppermute x34, starting transfers between devices: 5.92 us -> 18.2 us  [swapped(): return lax.ppermute(value, axis, [(0, 1), (1, 0)])]
    another operation x22 -> x0, other arithmetic: 12.3 us -> none
    pallas_call x1, Pallas kernels: 42.6 us -> 32.2 us  [attention_backward(): pl.pallas_call(kernel, grid=(key_steps,), in_specs=[pl.BlockSpec(memory_s...]
  transfers between devices with their start and end apart: 120 -> 94, of which waited for: 63 -> 44; matrix products, arithmetic and copies ran while one was open for 29% -> 31% of each run, Pallas kernels for 7% -> 6%
where the time goes in v2:
time: 904 us; the launch traced here: 893 us
  waiting for transfers between devices  362 us (40%)
  matrix products  171 us (19%)
  starting transfers between devices  126 us (14%)
  local copies, waits for them, and re-layouts  84.8 us (9%)
  other arithmetic  77.5 us (9%)
  Pallas kernels  54.6 us (6%)
  between operations  16.6 us (2%)
    ppermute x24, waiting for transfers between devices, round_ring(): return lax.ppermute(value, GROUP, pairs)  243 us
    dot_general x21, matrix products, dot_nn(): lax.dot_general(left, right, (((1,), (0,)), ((), ())), preferred_element_...  67.1 us
    dot_general x20, matrix products, dot_nt(): lax.dot_general(left, right, (((1,), (1,)), ((), ())), preferred_element_...  57 us
    all_to_all x9, waiting for transfers between devices, exchange(): lax.all_to_all(blocks, GROUP, split_axis=0, concat_axis=0, tiled=True)  56.2 us
    unnamed x300, local copies, waits for them, and re-layouts  49.8 us
    dot_general x6, matrix products, dot_tn(): lax.dot_general(left, right, (((0,), (0,)), ((), ())), preferred_element_...  46.5 us
    all_to_all x9, starting transfers between devices, exchange(): lax.all_to_all(blocks, GROUP, split_axis=0, concat_axis=0, tiled=True)  42.7 us
    ppermute x6, waiting for transfers between devices, moved_on(): lax.ppermute(value, COPIES, [(t, f) if back else (f, t) for f, t in pairs])  39.9 us
  transfers between devices with their start and end apart: 94, of which 44 were waited for; matrix products, arithmetic and copies ran while one was open for 31% of the time, Pallas kernels for 6%

profile of v2, /device:TPU:0, one launch (start us, length us, event | category | flops | bytes accessed | tf_op | source)
XLA Modules:
  0.0 892.6 jit_solution(12098651084970258373)
XLA Ops:
  11.8 6.5 all-to-all-start
  22.7 22.8 %all-to-all-done = bf16[8,72,768]{2,1,0:T(8,128)(2,1)S(1)} async-done(((bf16[8,72,768]{2,1,0:T(8,128)(2,1)}), bf16[8,72,768]{2,1,0:T(8,128)(2,1)S(1)}, u32[]{:S(2)}, u32[]{:S(2)}) %all-to-all-start) | async-done | bytes 884768 | tf_op jit(solution)/shard_map/all_to_all | solution.py:194
  60.9 14.1 %collective-permute-done.3 = bf16[160,2304]{1,0:T(8,128)(2,1)} collective-permute-done((bf16[160,2304]{1,0:T(8,128)(2,1)}, bf16[160,2304]{1,0:T(8,128)(2,1)}, u32[]{:S(2)}, u32[]{:S(2)}) %collective-permute-start.3) | collective-permute-done | bytes 737312 | tf_op jit(solution)/shard_map/ppermute | solution.py:123
  80.8 12.7 %collective-permute-done.5 = bf16[160,2304]{1,0:T(8,128)(2,1)} collective-permute-done((bf16[160,2304]{1,0:T(8,128)(2,1)}, bf16[160,2304]{1,0:T(8,128)(2,1)}, u32[]{:S(2)}, u32[]{:S(2)}) %collective-permute-start.5) | collective-permute-done | bytes 737312 | tf_op jit(solution)/shard_map/ppermute | solution.py:123
  123.8 9.5 %collective-permute-start.13 = (bf16[8,144]{1,0:T(8,128)(2,1)S(1)}, bf16[8,144]{1,0:T(8,128)(2,1)S(1)}, u32[]{:S(2)}, u32[]{:S(2)}) collective-permute-start(bf16[8,144]{1,0:T(8,128)(2,1)S(1)} %pad_maximum_fusion.9), channel_id=1, source_target_pairs={{0,8},{8,16},{16,24},{24,0},{1,9},{9,17},{17,25},{25,1},{2,10},{10... | collective-permute-start | bytes 6920 | tf_op jit(solution)/shard_map/ppermute | solution.py:33
  136.2 11.1 %collective-permute-done.8 = bf16[1280,256]{1,0:T(8,128)(2,1)S(1)} collective-permute-done((bf16[1280,256]{1,0:T(8,128)(2,1)S(1)}, bf16[1280,256]{1,0:T(8,128)(2,1)S(1)}, u32[]{:S(2)}, u32[]{:S(2)}) %collective-permute-start.8) | collective-permute-done | bytes 655392 | tf_op jit(solution)/shard_map/ppermute | solution.py:49
  163.2 17.9 %attention_forward.1 = (f32[1280,256]{1,0:T(8,128)S(1)}, f32[1280,1]{1,0:T(8,128)S(1)}) custom-call(s32[21]{0:T(128)S(1)} %pad_add_fusion.meta_ref, bf16[1280,256]{1,0:T(8,128)(2,1)S(1)} %copy-done.27, bf16[5120,256]{1,0:T(8,128)(2,1)S(1)} %copy-done.11, bf16[5120,256]{1,0:T(8,128)(2,1)} %collective-permute-done.16.other_ref), custom_call_target="tpu_custom_call" | custom-call | flops 6710886400 | bytes 7864320 | tf_op jit(solution)/shard_map/attention_forward/pallas_call | solution.py:265
  182.0 8.9 all-to-all-done.2
  208.6 12.1 %collective-permute-done.21 = bf16[160,2304]{1,0:T(8,128)(2,1)} collective-permute-done((bf16[160,2304]{1,0:T(8,128)(2,1)}, bf16[160,2304]{1,0:T(8,128)(2,1)}, u32[]{:S(2)}, u32[]{:S(2)}) %collective-permute-start.21) | collective-permute-done | bytes 737312 | tf_op jit(solution)/shard_map/ppermute | solution.py:123
  230.2 18.5 %all-to-all-done.3 = bf16[8,72,1152]{2,1,0:T(8,128)(2,1)} async-done(((bf16[8,72,1152]{2,1,0:T(8,128)(2,1)}), bf16[8,72,1152]{2,1,0:T(8,128)(2,1)}, u32[]{:S(2)}, u32[]{:S(2)}) %all-to-all-start.3) | async-done | bytes 1327136 | tf_op jit(solution)/shard_map/all_to_all | solution.py:194
  248.8 6.0 collective-permute-done.22
  257.5 5.9 collective-permute-start.23
  263.8 12.7 %collective-permute-done.23 = bf16[160,2304]{1,0:T(8,128)(2,1)} collective-permute-done((bf16[160,2304]{1,0:T(8,128)(2,1)}, bf16[160,2304]{1,0:T(8,128)(2,1)}, u32[]{:S(2)}, u32[]{:S(2)}) %collective-permute-start.23) | collective-permute-done | bytes 737312 | tf_op jit(solution)/shard_map/ppermute | solution.py:123
  286.0 4.7 convolution_convert_fusion.23
  290.7 6.6 fusion.82
  297.3 6.9 collective-permute-done.24
  312.9 11.5 %collective-permute-done.27 = bf16[160,2304]{1,0:T(8,128)(2,1)S(1)} collective-permute-done((bf16[160,2304]{1,0:T(8,128)(2,1)S(1)}, bf16[160,2304]{1,0:T(8,128)(2,1)S(1)}, u32[]{:S(2)}, u32[]{:S(2)}) %collective-permute-start.27) | collective-permute-done | bytes 737312 | tf_op jit(solution)/shard_map/ppermute | solution.py:123
  332.9 11.2 %collective-permute-done.29 = bf16[160,2304]{1,0:T(8,128)(2,1)S(1)} collective-permute-done((bf16[160,2304]{1,0:T(8,128)(2,1)S(1)}, bf16[160,2304]{1,0:T(8,128)(2,1)S(1)}, u32[]{:S(2)}, u32[]{:S(2)}) %collective-permute-start.29) | collective-permute-done | bytes 737312 | tf_op jit(solution)/shard_map/ppermute | solution.py:123
  344.1 4.8 pad_maximum_fusion
  356.6 5.3 convolution_convert_fusion.18
  373.9 10.1 %collective-permute-done.35 = bf16[160,2304]{1,0:T(8,128)(2,1)S(1)} collective-permute-done((bf16[160,2304]{1,0:T(8,128)(2,1)S(1)}, bf16[160,2304]{1,0:T(8,128)(2,1)S(1)}, u32[]{:S(2)}, u32[]{:S(2)}) %collective-permute-start.35) | collective-permute-done | bytes 737312 | tf_op jit(solution)/shard_map/ppermute | solution.py:123
  384.4 6.5 pad_maximum_fusion.1
  394.7 8.3 collective-permute-done.36
  404.1 18.4 %collective-permute-done.37 = bf16[160,2304]{1,0:T(8,128)(2,1)} collective-permute-done((bf16[160,2304]{1,0:T(8,128)(2,1)S(1)}, bf16[160,2304]{1,0:T(8,128)(2,1)}, u32[]{:S(2)}, u32[]{:S(2)}) %collective-permute-start.37) | collective-permute-done | bytes 737312 | tf_op jit(solution)/shard_map/ppermute | solution.py:123
  427.9 5.6 fusion.64
  441.5 4.9 collective-permute-done.38
  459.3 6.6 collective-permute-done.41
  477.3 8.5 collective-permute-done.43
  488.9 9.7 %convolution_convert_fusion.2 = bf16[2304,1152]{1,0:T(8,128)(2,1)} fusion(bf16[1280,2304]{1,0:T(8,128)(2,1)S(1)} %constant_dynamic-update-slice_fusion.22, bf16[1280,1152]{1,0:T(8,128)(2,1)S(1)} %copy-done.55), kind=kOutput, calls=%fused_computation.2 | convolution fusion | flops 6797426688 | bytes 14155776 | tf_op jit(solution)/shard_map/dot_general | solution.py:65
  498.6 7.9 collective-permute-done.49
  512.7 6.3 multiply_convert_fusion
  519.8 11.6 %convolution_convert_fusion.1 = bf16[2304,1152]{1,0:T(8,128)(2,1)} fusion(bf16[1280,2304]{1,0:T(8,128)(2,1)} %get-tuple-element.156, bf16[320,1152]{1,0:T(8,128)(2,1)S(1)} %get-tuple-element.232, bf16[320,1152]{1,0:T(8,128)(2,1)S(1)} %copy-done.99, bf16[320,1152]{1,0:T(8,128)(2,1)S(1)} %copy-done.97, bf16[320,1152]{1,0:T(8,128)(2,1)S(1)} %copy-done.95), kind=kOutput, calls=%fused_computation.1 | convolution fusion | flops 6809223168 | bytes 14155776 | tf_op jit(solution)/shard_map/dot_general | solution.py:65
  532.0 5.0 fusion.198
  537.1 4.7 fusion.11
  548.2 11.9 %convolution_convert_fusion = bf16[2304,1152]{1,0:T(8,128)(2,1)} fusion(bf16[1280,2304]{1,0:T(8,128)(2,1)} %get-tuple-element.156, bf16[320,1152]{1,0:T(8,128)(2,1)S(1)} %copy-done.108, bf16[320,1152]{1,0:T(8,128)(2,1)S(1)} %copy-done.107, bf16[320,1152]{1,0:T(8,128)(2,1)S(1)} %copy-done.105, bf16[320,1152]{1,0:T(8,128)(2,1)S(1)} %copy-done.103), kind=kOutput, calls=%fused_computation | convolution fusion | flops 6809223168 | bytes 14155776 | tf_op jit(solution)/shard_map/dot_general | solution.py:65
  560.1 7.2 collective-permute-done.51
  583.8 9.4 %collective-permute-done.52 = bf16[160,2304]{1,0:T(8,128)(2,1)} collective-permute-done((bf16[160,2304]{1,0:T(8,128)(2,1)S(1)}, bf16[160,2304]{1,0:T(8,128)(2,1)}, u32[]{:S(2)}, u32[]{:S(2)}) %collective-permute-start.52) | collective-permute-done | bytes 737312 | tf_op jit(solution)/shard_map/ppermute | solution.py:123
  604.2 13.1 %collective-permute-done.54 = bf16[160,2304]{1,0:T(8,128)(2,1)S(1)} collective-permute-done((bf16[160,2304]{1,0:T(8,128)(2,1)}, bf16[160,2304]{1,0:T(8,128)(2,1)S(1)}, u32[]{:S(2)}, u32[]{:S(2)}) %collective-permute-start.54) | collective-permute-done | bytes 737312 | tf_op jit(solution)/shard_map/ppermute | solution.py:123
  626.6 15.2 %collective-permute-done.56 = bf16[160,2304]{1,0:T(8,128)(2,1)S(1)} collective-permute-done((bf16[160,2304]{1,0:T(8,128)(2,1)S(1)}, bf16[160,2304]{1,0:T(8,128)(2,1)S(1)}, u32[]{:S(2)}, u32[]{:S(2)}) %collective-permute-start.56) | collective-permute-done | bytes 737312 | tf_op jit(solution)/shard_map/ppermute | solution.py:123
  648.8 4.7 all-to-all-start.4
  656.0 32.2 %attention_backward.1 = (f32[1280,256]{1,0:T(8,128)S(1)}, bf16[5120,256]{1,0:T(8,128)(2,1)S(1)}, bf16[5120,256]{1,0:T(8,128)(2,1)S(1)}) custom-call(s32[21]{0:T(128)S(1)} %copy-done.24, bf16[1280,256]{1,0:T(8,128)(2,1)S(1)} %copy-done.28, bf16[1280,256]{1,0:T(8,128)(2,1)S(1)} %to_blocks.3.d_ref, bf16[5120,256]{1,0:T(8,128)(2,1)S(1)} %copy-done.12, ...), custom_call_target="tpu_custom_call" | custom-call | flops 16777216000 | bytes 13107200 | tf_op jit(solution)/shard_map/attention_backward/pallas_call | solution.py:376
  703.6 27.5 %collective-permute-done.66 = bf16[1280,256]{1,0:T(8,128)(2,1)S(1)} collective-permute-done((bf16[1280,256]{1,0:T(8,128)(2,1)S(1)}, bf16[1280,256]{1,0:T(8,128)(2,1)S(1)}, u32[]{:S(2)}, u32[]{:S(2)}) %collective-permute-start.66) | collective-permute-done | bytes 655392 | tf_op jit(solution)/shard_map/ppermute | solution.py:49
  735.4 5.4 convolution_convert_fusion.15
  777.5 27.0 %collective-permute-done.73 = bf16[160,2304]{1,0:T(8,128)(2,1)S(1)} collective-permute-done((bf16[160,2304]{1,0:T(8,128)(2,1)S(1)}, bf16[160,2304]{1,0:T(8,128)(2,1)S(1)}, u32[]{:S(2)}, u32[]{:S(2)}) %collective-permute-start.73) | collective-permute-done | bytes 737312 | tf_op jit(solution)/shard_map/ppermute | solution.py:123
  805.6 12.6 %collective-permute-start.74 = (bf16[160,2304]{1,0:T(8,128)(2,1)}, bf16[160,2304]{1,0:T(8,128)(2,1)}, u32[]{:S(2)}, u32[]{:S(2)}) collective-permute-start(bf16[160,2304]{1,0:T(8,128)(2,1)} %add_convert_fusion.2), channel_id=1, source_target_pairs={{0,8},{8,16},{16,24},{24,0},{1,25},{9,1},{17,9},{25,17},{2,10},{10... | collective-permute-start | bytes 2211848 | tf_op jit(solution)/shard_map/ppermute | solution.py:123
  827.5 5.7 all-to-all-start.7
  848.6 15.0 %collective-permute-done.75 = bf16[160,2304]{1,0:T(8,128)(2,1)S(1)} collective-permute-done((bf16[160,2304]{1,0:T(8,128)(2,1)}, bf16[160,2304]{1,0:T(8,128)(2,1)S(1)}, u32[]{:S(2)}, u32[]{:S(2)}) %collective-permute-start.75) | collective-permute-done | bytes 737312 | tf_op jit(solution)/shard_map/ppermute | solution.py:123
  877.3 5.9 all-to-all-done.8
  (668 shorter events, 359.3 us)
Async XLA Ops:
  11.8 33.8 %all-to-all-start = ((bf16[8,72,768]{2,1,0:T(8,128)(2,1)}), bf16[8,72,768]{2,1,0:T(8,128)(2,1)S(1)}, u32[]{:S(2)}, u32[]{:S(2)}) async-start(bf16[8,72,768]{2,1,0:T(8,128)(2,1)} %copy.57), calls=%async_computation | async-start | bytes 1769472 | tf_op jit(solution)/shard_map/all_to_all | solution.py:194
  18.2 86.8 %all-gather.5.cloned.1.call-start = ((), (), s32[]{:S(2)}) async-start(), calls=%async_computation.14 | async-start | bytes 4423680 | tf_op jit(solution)/shard_map/all_gather | solution.py:199
  18.9 34.9 %collective-permute-start.1 = (bf16[160,2304]{1,0:T(8,128)(2,1)S(1)}, bf16[160,2304]{1,0:T(8,128)(2,1)}, u32[]{:S(2)}, u32[]{:S(2)}) collective-permute-start(bf16[160,2304]{1,0:T(8,128)(2,1)S(1)} %get-tuple-element.112), channel_id=1, source_target_pairs={{0,8},{8,16},{16,24},{24,0},{1,25},{9,1},{17,9},{25,17},{2,10},{10... | collective-permute-start | bytes 2211848 | tf_op jit(solution)/shard_map/ppermute | solution.py:123
  20.9 56.1 %collective-permute-start = (bf16[160,2304]{1,0:T(8,128)(2,1)S(1)}, bf16[160,2304]{1,0:T(8,128)(2,1)}, u32[]{:S(2)}, u32[]{:S(2)}) collective-permute-start(bf16[160,2304]{1,0:T(8,128)(2,1)S(1)} %get-tuple-element.112), channel_id=1, source_target_pairs={{0,1},{1,0},{2,3},{3,2},{4,5},{5,4},{6,7},{7,6},{8,9},{9,8},{10,11... | collective-permute-start | bytes 2211848 | tf_op jit(solution)/shard_map/ppermute | solution.py:28
  22.7 33.0 %collective-permute-start.10 = (bf16[1,144]{1,0:T(2,128)(2,1)S(1)}, bf16[1,144]{1,0:T(2,128)(2,1)S(1)}, u32[]{:S(2)}, u32[]{:S(2)}) collective-permute-start(bf16[1,144]{1,0:T(2,128)(2,1)S(1)} %broadcast_in_dim.11), channel_id=1, source_target_pairs={{0,1},{1,0},{2,3},{3,2},{4,5},{5,4},{6,7},{7,6},{8,9},{9,8},{10,11... | collective-permute-start | bytes 872 | tf_op jit(solution)/shard_map/ppermute | solution.py:33
  53.8 21.2 %collective-permute-start.3 = (bf16[160,2304]{1,0:T(8,128)(2,1)}, bf16[160,2304]{1,0:T(8,128)(2,1)}, u32[]{:S(2)}, u32[]{:S(2)}) collective-permute-start(bf16[160,2304]{1,0:T(8,128)(2,1)} %collective-permute-done.1), channel_id=1, source_target_pairs={{0,8},{8,16},{16,24},{24,0},{1,25},{9,1},{17,9},{25,17},{2,10},{10... | collective-permute-start | bytes 2211848 | tf_op jit(solution)/shard_map/ppermute | solution.py:123
  59.4 59.3 %collective-permute-start.12 = (bf16[4,144]{1,0:T(4,128)(2,1)S(1)}, bf16[4,144]{1,0:T(4,128)(2,1)S(1)}, u32[]{:S(2)}, u32[]{:S(2)}) collective-permute-start(bf16[4,144]{1,0:T(4,128)(2,1)S(1)} %pad_maximum_fusion.10), channel_id=1, source_target_pairs={{0,4},{4,0},{1,5},{5,1},{2,6},{6,2},{3,7},{7,3},{8,12},{12,8},{9,1... | collective-permute-start | bytes 3464 | tf_op jit(solution)/shard_map/ppermute | solution.py:33
  60.9 32.6 %collective-permute-start.2 = (bf16[160,2304]{1,0:T(8,128)(2,1)}, bf16[160,2304]{1,0:T(8,128)(2,1)S(1)}, u32[]{:S(2)}, u32[]{:S(2)}) collective-permute-start(bf16[160,2304]{1,0:T(8,128)(2,1)} %collective-permute-done.1), channel_id=1, source_target_pairs={{0,1},{1,0},{2,3},{3,2},{4,5},{5,4},{6,7},{7,6},{8,9},{9,8},{10,11... | collective-permute-start | bytes 2211848 | tf_op jit(solution)/shard_map/ppermute | solution.py:28
  78.2 23.8 %collective-permute-start.4 = (bf16[160,2304]{1,0:T(8,128)(2,1)}, bf16[160,2304]{1,0:T(8,128)(2,1)S(1)}, u32[]{:S(2)}, u32[]{:S(2)}) collective-permute-start(bf16[160,2304]{1,0:T(8,128)(2,1)} %collective-permute-done.3), channel_id=1, source_target_pairs={{0,1},{1,0},{2,3},{3,2},{4,5},{5,4},{6,7},{7,6},{8,9},{9,8},{10,11... | collective-permute-start | bytes 2211848 | tf_op jit(solution)/shard_map/ppermute | solution.py:28
  95.7 54.5 %all-to-all-start.1 = ((bf16[8,72,1152]{2,1,0:T(8,128)(2,1)}), bf16[8,72,1152]{2,1,0:T(8,128)(2,1)}, u32[]{:S(2)}, u32[]{:S(2)}) async-start(bf16[8,72,1152]{2,1,0:T(8,128)(2,1)} %copy.58), calls=%async_computation.1 | async-start | bytes 2654208 | tf_op jit(solution)/shard_map/all_to_all | solution.py:194
  99.9 120.8 %all-gather.7.cloned.1.call-start = ((), (), s32[]{:S(2)}) async-start(), calls=%async_computation.15 | async-start | bytes 6635520 | tf_op jit(solution)/shard_map/all_gather | solution.py:199
  115.2 21.0 %collective-permute-start.9 = (bf16[1280,256]{1,0:T(8,128)(2,1)S(1)}, bf16[1280,256]{1,0:T(8,128)(2,1)S(1)}, u32[]{:S(2)}, u32[]{:S(2)}) collective-permute-start(bf16[1280,256]{1,0:T(8,128)(2,1)S(1)} %get-tuple-element.115), channel_id=1, source_target_pairs={{0,6},{2,4},{4,2},{6,0},{1,7},{3,5},{5,3},{7,1},{8,14},{10,12},{12... | collective-permute-start | bytes 1966088 | tf_op jit(solution)/shard_map/ppermute | solution.py:49
  117.7 29.6 %collective-permute-start.8 = (bf16[1280,256]{1,0:T(8,128)(2,1)S(1)}, bf16[1280,256]{1,0:T(8,128)(2,1)S(1)}, u32[]{:S(2)}, u32[]{:S(2)}) collective-permute-start(bf16[1280,256]{1,0:T(8,128)(2,1)S(1)} %get-tuple-element.115), channel_id=1, source_target_pairs={{0,4},{2,6},{4,0},{6,2},{1,5},{3,7},{5,1},{7,3},{8,12},{10,14},{12... | collective-permute-start | bytes 1966088 | tf_op jit(solution)/shard_map/ppermute | solution.py:49
  118.2 30.0 %collective-permute-start.7 = (bf16[1280,256]{1,0:T(8,128)(2,1)S(1)}, bf16[1280,256]{1,0:T(8,128)(2,1)}, u32[]{:S(2)}, u32[]{:S(2)}) collective-permute-start(bf16[1280,256]{1,0:T(8,128)(2,1)S(1)} %get-tuple-element.115), channel_id=1, source_target_pairs={{0,2},{2,0},{4,6},{6,4},{1,3},{3,1},{5,7},{7,5},{8,10},{10,8},{12,... | collective-permute-start | bytes 1966088 | tf_op jit(solution)/shard_map/ppermute | solution.py:49
  153.6 37.3 %all-to-all-start.2 = ((bf16[8,72,1152]{2,1,0:T(8,128)(2,1)}), bf16[8,72,1152]{2,1,0:T(8,128)(2,1)}, u32[]{:S(2)}, u32[]{:S(2)}) async-start(bf16[8,72,1152]{2,1,0:T(8,128)(2,1)} %copy.59), calls=%async_computation.2 | async-start | bytes 2654208 | tf_op jit(solution)/shard_map/all_to_all | solution.py:194
  158.3 127.7 %all-gather.9.cloned.1.call-start = ((), (), s32[]{:S(2)}) async-start(), calls=%async_computation.16 | async-start | bytes 6635520 | tf_op jit(solution)/shard_map/all_gather | solution.py:199
  199.1 21.6 %collective-permute-start.21 = (bf16[160,2304]{1,0:T(8,128)(2,1)}, bf16[160,2304]{1,0:T(8,128)(2,1)}, u32[]{:S(2)}, u32[]{:S(2)}) collective-permute-start(bf16[160,2304]{1,0:T(8,128)(2,1)} %add_convert_fusion.13), channel_id=1, source_target_pairs={{0,8},{8,16},{16,24},{24,0},{1,25},{9,1},{17,9},{25,17},{2,10},{10... | collective-permute-start | bytes 2211848 | tf_op jit(solution)/shard_map/ppermute | solution.py:123
  204.3 44.5 %all-to-all-start.3 = ((bf16[8,72,1152]{2,1,0:T(8,128)(2,1)}), bf16[8,72,1152]{2,1,0:T(8,128)(2,1)}, u32[]{:S(2)}, u32[]{:S(2)}) async-start(bf16[8,72,1152]{2,1,0:T(8,128)(2,1)} %copy.60), calls=%async_computation.3 | async-start | bytes 2654208 | tf_op jit(solution)/shard_map/all_to_all | solution.py:194
  208.5 142.8 %all-gather.11.cloned.1.call-start = ((), (), s32[]{:S(2)}) async-start(), calls=%async_computation.17 | async-start | bytes 6635520 | tf_op jit(solution)/shard_map/all_gather | solution.py:199
  223.4 31.4 %collective-permute-start.22 = (bf16[160,2304]{1,0:T(8,128)(2,1)}, bf16[160,2304]{1,0:T(8,128)(2,1)}, u32[]{:S(2)}, u32[]{:S(2)}) collective-permute-start(bf16[160,2304]{1,0:T(8,128)(2,1)} %add_convert_fusion.12), channel_id=1, source_target_pairs={{0,8},{8,16},{16,24},{24,0},{1,25},{9,1},{17,9},{25,17},{2,10},{10... | collective-permute-start | bytes 2211848 | tf_op jit(solution)/shard_map/ppermute | solution.py:123
  226.8 28.0 %collective-permute-start.18 = (bf16[160,2304]{1,0:T(8,128)(2,1)}, bf16[160,2304]{1,0:T(8,128)(2,1)}, u32[]{:S(2)}, u32[]{:S(2)}) collective-permute-start(bf16[160,2304]{1,0:T(8,128)(2,1)} %slice.517), channel_id=1, source_target_pairs={{0,1},{1,0},{2,3},{3,2},{4,5},{5,4},{6,7},{7,6},{8,9},{9,8},{10,11... | collective-permute-start | bytes 2211848 | tf_op jit(solution)/shard_map/ppermute | solution.py:28
  229.7 34.1 %collective-permute-start.17 = (bf16[160,2304]{1,0:T(8,128)(2,1)}, bf16[160,2304]{1,0:T(8,128)(2,1)}, u32[]{:S(2)}, u32[]{:S(2)}) collective-permute-start(bf16[160,2304]{1,0:T(8,128)(2,1)} %slice.514), channel_id=1, source_target_pairs={{0,1},{1,0},{2,3},{3,2},{4,5},{5,4},{6,7},{7,6},{8,9},{9,8},{10,11... | collective-permute-start | bytes 2211848 | tf_op jit(solution)/shard_map/ppermute | solution.py:28
  284.2 364.6 %reduce-scatter.8.cloned.1.call-start = ((), (), s32[]{:S(2)}) async-start(), calls=%async_computation.18 | async-start | bytes 6635520 | tf_op jit(solution)/shard_map/reduce_scatter | solution.py:203
  284.2 20.0 %collective-permute-start.24 = (bf16[160,2304]{1,0:T(8,128)(2,1)S(1)}, bf16[160,2304]{1,0:T(8,128)(2,1)S(1)}, u32[]{:S(2)}, u32[]{:S(2)}) collective-permute-start(bf16[160,2304]{1,0:T(8,128)(2,1)S(1)} %get-tuple-element.221), channel_id=1, source_target_pairs={{0,8},{8,16},{16,24},{24,0},{1,25},{9,1},{17,9},{25,17},{2,10},{10... | collective-permute-start | bytes 2211848 | tf_op jit(solution)/shard_map/ppermute | solution.py:123
  371.6 31.4 %collective-permute-start.32 = (bf16[160,2304]{1,0:T(8,128)(2,1)S(1)}, bf16[160,2304]{1,0:T(8,128)(2,1)S(1)}, u32[]{:S(2)}, u32[]{:S(2)}) collective-permute-start(bf16[160,2304]{1,0:T(8,128)(2,1)S(1)} %slice.543), channel_id=1, source_target_pairs={{0,1},{1,0},{2,3},{3,2},{4,5},{5,4},{6,7},{7,6},{8,9},{9,8},{10,11... | collective-permute-start | bytes 2211848 | tf_op jit(solution)/shard_map/ppermute | solution.py:28
  425.7 20.7 %collective-permute-start.38 = (bf16[160,2304]{1,0:T(8,128)(2,1)S(1)}, bf16[160,2304]{1,0:T(8,128)(2,1)S(1)}, u32[]{:S(2)}, u32[]{:S(2)}) collective-permute-start(bf16[160,2304]{1,0:T(8,128)(2,1)S(1)} %get-tuple-element.218), channel_id=1, source_target_pairs={{0,8},{8,16},{16,24},{24,0},{1,25},{9,1},{17,9},{25,17},{2,10},{10... | collective-permute-start | bytes 2211848 | tf_op jit(solution)/shard_map/ppermute | solution.py:123
  506.5 142.2 %reduce-scatter.10.cloned.1.call-start = ((), (), s32[]{:S(2)}) async-start(), calls=%async_computation.19 | async-start | bytes 6635520 | tf_op jit(solution)/shard_map/reduce_scatter | solution.py:203
  532.0 200.8 %reduce-scatter.12.cloned.1.call-start = ((), (), s32[]{:S(2)}) async-start(), calls=%async_computation.20 | async-start | bytes 6635520 | tf_op jit(solution)/shard_map/reduce_scatter | solution.py:203
  544.6 22.8 %collective-permute-start.40 = (bf16[160,2304]{1,0:T(8,128)(2,1)}, bf16[160,2304]{1,0:T(8,128)(2,1)S(1)}, u32[]{:S(2)}, u32[]{:S(2)}) collective-permute-start(bf16[160,2304]{1,0:T(8,128)(2,1)} %slice.443), channel_id=1, source_target_pairs={{0,1},{1,0},{2,3},{3,2},{4,5},{5,4},{6,7},{7,6},{8,9},{9,8},{10,11... | collective-permute-start | bytes 2211848 | tf_op jit(solution)/shard_map/ppermute | solution.py:28
  593.5 23.9 %collective-permute-start.59 = (f32[8,144]{1,0:T(8,128)S(1)}, f32[8,144]{1,0:T(8,128)S(1)}, u32[]{:S(2)}, u32[]{:S(2)}) collective-permute-start(f32[8,144]{1,0:T(8,128)S(1)} %get-tuple-element.263), channel_id=1, source_target_pairs={{0,24},{8,0},{16,8},{24,16},{1,25},{9,1},{17,9},{25,17},{2,26},{10... | collective-permute-start | bytes 13832 | tf_op jit(solution)/shard_map/ppermute | solution.py:33
  596.2 21.2 %collective-permute-start.61 = (f32[8,144]{1,0:T(8,128)S(1)}, f32[8,144]{1,0:T(8,128)S(1)}, u32[]{:S(2)}, u32[]{:S(2)}) collective-permute-start(f32[8,144]{1,0:T(8,128)S(1)} %get-tuple-element.264), channel_id=1, source_target_pairs={{0,8},{8,16},{16,24},{24,0},{1,9},{9,17},{17,25},{25,1},{2,10},{10... | collective-permute-start | bytes 13832 | tf_op jit(solution)/shard_map/ppermute | solution.py:33
  596.2 21.2 %collective-permute-start.60 = (f32[8,144]{1,0:T(8,128)S(1)}, f32[8,144]{1,0:T(8,128)S(1)}, u32[]{:S(2)}, u32[]{:S(2)}) collective-permute-start(f32[8,144]{1,0:T(8,128)S(1)} %get-tuple-element.265), channel_id=1, source_target_pairs={{0,16},{8,24},{16,0},{24,8},{1,17},{9,25},{17,1},{25,9},{2,18},{10... | collective-permute-start | bytes 13832 | tf_op jit(solution)/shard_map/ppermute | solution.py:33
  596.8 20.6 %collective-permute-start.54 = (bf16[160,2304]{1,0:T(8,128)(2,1)}, bf16[160,2304]{1,0:T(8,128)(2,1)S(1)}, u32[]{:S(2)}, u32[]{:S(2)}) collective-permute-start(bf16[160,2304]{1,0:T(8,128)(2,1)} %collective-permute-done.52), channel_id=1, source_target_pairs={{0,8},{8,16},{16,24},{24,0},{1,25},{9,1},{17,9},{25,17},{2,10},{10... | collective-permute-start | bytes 2211848 | tf_op jit(solution)/shard_map/ppermute | solution.py:123
  621.2 20.6 %collective-permute-start.63 = (f32[2,144]{1,0:T(2,128)S(1)}, f32[2,144]{1,0:T(2,128)S(1)}, u32[]{:S(2)}, u32[]{:S(2)}) collective-permute-start(f32[2,144]{1,0:T(2,128)S(1)} %slice.605), channel_id=1, source_target_pairs={{0,2},{2,0},{1,3},{3,1},{4,6},{6,4},{5,7},{7,5},{8,10},{10,8},{9,1... | collective-permute-start | bytes 3464 | tf_op jit(solution)/shard_map/ppermute | solution.py:33
  648.8 43.4 %all-to-all-start.4 = ((bf16[8,72,1152]{2,1,0:T(8,128)(2,1)}), bf16[8,72,1152]{2,1,0:T(8,128)(2,1)}, u32[]{:S(2)}, u32[]{:S(2)}) async-start(bf16[8,72,1152]{2,1,0:T(8,128)(2,1)} %bitcast.137), calls=%async_computation.6 | async-start | bytes 2654208 | tf_op jit(solution)/shard_map/all_to_all | solution.py:194
  692.6 40.1 %all-to-all-start.5 = ((bf16[8,72,1152]{2,1,0:T(8,128)(2,1)}), bf16[8,72,1152]{2,1,0:T(8,128)(2,1)}, u32[]{:S(2)}, u32[]{:S(2)}) async-start(bf16[8,72,1152]{2,1,0:T(8,128)(2,1)} %bitcast.136), calls=%async_computation.7 | async-start | bytes 2654208 | tf_op jit(solution)/shard_map/all_to_all | solution.py:194
  697.0 130.5 %reduce-scatter.16.cloned.1.call-start = ((), (), s32[]{:S(2)}) async-start(), calls=%async_computation.22 | async-start | bytes 2949120 | tf_op jit(solution)/shard_map/reduce_scatter | solution.py:203
  700.0 31.1 %collective-permute-start.66 = (bf16[1280,256]{1,0:T(8,128)(2,1)S(1)}, bf16[1280,256]{1,0:T(8,128)(2,1)S(1)}, u32[]{:S(2)}, u32[]{:S(2)}) collective-permute-start(bf16[1280,256]{1,0:T(8,128)(2,1)S(1)} %get-tuple-element.228), channel_id=1, source_target_pairs={{2,0},{0,2},{6,4},{4,6},{3,1},{1,3},{7,5},{5,7},{10,8},{8,10},{14,... | collective-permute-start | bytes 1966088 | tf_op jit(solution)/shard_map/ppermute | solution.py:49
  701.0 30.2 %collective-permute-start.68 = (bf16[1280,256]{1,0:T(8,128)(2,1)S(1)}, bf16[1280,256]{1,0:T(8,128)(2,1)S(1)}, u32[]{:S(2)}, u32[]{:S(2)}) collective-permute-start(bf16[1280,256]{1,0:T(8,128)(2,1)S(1)} %get-tuple-element.229), channel_id=1, source_target_pairs={{6,0},{4,2},{2,4},{0,6},{7,1},{5,3},{3,5},{1,7},{14,8},{12,10},{10... | collective-permute-start | bytes 1966088 | tf_op jit(solution)/shard_map/ppermute | solution.py:49
  703.1 29.3 %collective-permute-start.67 = (bf16[1280,256]{1,0:T(8,128)(2,1)S(1)}, bf16[1280,256]{1,0:T(8,128)(2,1)S(1)}, u32[]{:S(2)}, u32[]{:S(2)}) collective-permute-start(bf16[1280,256]{1,0:T(8,128)(2,1)S(1)} %get-tuple-element.230), channel_id=1, source_target_pairs={{4,0},{6,2},{0,4},{2,6},{5,1},{7,3},{1,5},{3,7},{12,8},{14,10},{8,... | collective-permute-start | bytes 1966088 | tf_op jit(solution)/shard_map/ppermute | solution.py:49
  757.7 69.8 %all-to-all-start.6 = ((bf16[8,72,1152]{2,1,0:T(8,128)(2,1)}), bf16[8,72,1152]{2,1,0:T(8,128)(2,1)S(1)}, u32[]{:S(2)}, u32[]{:S(2)}) async-start(bf16[8,72,1152]{2,1,0:T(8,128)(2,1)} %bitcast.138), calls=%async_computation.9 | async-start | bytes 2654208 | tf_op jit(solution)/shard_map/all_to_all | solution.py:194
  762.2 86.4 %reduce-scatter.14.cloned.1.call-start = ((), (), s32[]{:S(2)}) async-start(), calls=%async_computation.21 | async-start | bytes 1474560 | tf_op jit(solution)/shard_map/reduce_scatter | solution.py:203
  766.9 37.6 %collective-permute-start.73 = (bf16[160,2304]{1,0:T(8,128)(2,1)S(1)}, bf16[160,2304]{1,0:T(8,128)(2,1)S(1)}, u32[]{:S(2)}, u32[]{:S(2)}) collective-permute-start(bf16[160,2304]{1,0:T(8,128)(2,1)S(1)} %add_convert_fusion.3), channel_id=1, source_target_pairs={{0,8},{8,16},{16,24},{24,0},{1,25},{9,1},{17,9},{25,17},{2,10},{10... | collective-permute-start | bytes 2211848 | tf_op jit(solution)/shard_map/ppermute | solution.py:123
  775.4 57.8 %collective-permute-start.70 = (bf16[160,2304]{1,0:T(8,128)(2,1)}, bf16[160,2304]{1,0:T(8,128)(2,1)}, u32[]{:S(2)}, u32[]{:S(2)}) collective-permute-start(bf16[160,2304]{1,0:T(8,128)(2,1)} %slice.611), channel_id=1, source_target_pairs={{0,1},{1,0},{2,3},{3,2},{4,5},{5,4},{6,7},{7,6},{8,9},{9,8},{10,11... | collective-permute-start | bytes 2211848 | tf_op jit(solution)/shard_map/ppermute | solution.py:28
  805.6 21.9 %collective-permute-start.74 = (bf16[160,2304]{1,0:T(8,128)(2,1)}, bf16[160,2304]{1,0:T(8,128)(2,1)}, u32[]{:S(2)}, u32[]{:S(2)}) collective-permute-start(bf16[160,2304]{1,0:T(8,128)(2,1)} %add_convert_fusion.2), channel_id=1, source_target_pairs={{0,8},{8,16},{16,24},{24,0},{1,25},{9,1},{17,9},{25,17},{2,10},{10... | collective-permute-start | bytes 2211848 | tf_op jit(solution)/shard_map/ppermute | solution.py:123
  820.2 44.3 %collective-permute-start.69 = (bf16[160,2304]{1,0:T(8,128)(2,1)}, bf16[160,2304]{1,0:T(8,128)(2,1)}, u32[]{:S(2)}, u32[]{:S(2)}) collective-permute-start(bf16[160,2304]{1,0:T(8,128)(2,1)} %slice.609), channel_id=1, source_target_pairs={{0,1},{1,0},{2,3},{3,2},{4,5},{5,4},{6,7},{7,6},{8,9},{9,8},{10,11... | collective-permute-start | bytes 2211848 | tf_op jit(solution)/shard_map/ppermute | solution.py:28
  827.5 36.1 %all-to-all-start.7 = ((bf16[8,72,512]{2,1,0:T(8,128)(2,1)}), bf16[8,72,512]{2,1,0:T(8,128)(2,1)}, u32[]{:S(2)}, u32[]{:S(2)}) async-start(bf16[8,72,512]{2,1,0:T(8,128)(2,1)} %bitcast.147), calls=%async_computation.10 | async-start | bytes 1179648 | tf_op jit(solution)/shard_map/all_to_all | solution.py:194
  835.9 27.7 %collective-permute-start.75 = (bf16[160,2304]{1,0:T(8,128)(2,1)}, bf16[160,2304]{1,0:T(8,128)(2,1)S(1)}, u32[]{:S(2)}, u32[]{:S(2)}) collective-permute-start(bf16[160,2304]{1,0:T(8,128)(2,1)} %add_convert_fusion.1), channel_id=1, source_target_pairs={{0,8},{8,16},{16,24},{24,0},{1,25},{9,1},{17,9},{25,17},{2,10},{10... | collective-permute-start | bytes 2211848 | tf_op jit(solution)/shard_map/ppermute | solution.py:123
  (181 other events, 1893.2 us)
Sparse Core Ops, SparseCore 0:
  46.6 46.8 all-gather.4
  150.3 62.1 all-gather.6
  214.4 61.9 all-gather.8
  284.3 60.9 all-gather.10
  506.6 61.0 reduce-scatter.7
  570.6 62.0 reduce-scatter.9
  635.7 61.9 reduce-scatter.11
  753.6 37.4 reduce-scatter.15
  820.3 28.2 reduce-scatter.13

commit v3 on v2

--- a/solution.py
+++ b/solution.py
@@ -557,7 +557,6 @@
     q, own_kv = to_blocks(qkv, core, tables)
     kv_mine = jnp.concatenate([moved_on(own_kv, k, j) for k, j in copies_apart()], axis=0)
     kv_mine, gate_mine, up_pack, gains = join(kv_mine, gate_mine, up_pack, gains)
-    ff_cols = w_gate.shape[1] // 8
     gate_w = gather_rows(gate_mine)
     up_mine = exchange(up_pack)
     kv_other = swapped(kv_mine, "c")
@@ -657,19 +656,19 @@
     d_qkv = jnp.concatenate([d_q, d_k], axis=1)
     q_part = dot_tn(x1, d_q)
     out_part = dot_tn(jnp.concatenate(x4, axis=0), attended_b)
-    q_part = jnp.concatenate([q_part, out_part], axis=1).astype(bf16)
-    kv_part = dot_tn(x1, d_k).astype(bf16)
-    d_qkv, q_part, kv_part = join(d_qkv, q_part, kv_part)
-    q_rows, kv_rows = scatter_rows(q_part), scatter_rows(kv_part)
-    dn1, (_, (up_sum, _), (q_sum, kv_rows)) = scatter_tokens(
+    kv_part = dot_tn(x1, d_k)
+    attn_part = jnp.concatenate([q_part, out_part, kv_part], axis=1).astype(bf16)
+    d_qkv, attn_part = join(d_qkv, attn_part)
+    attn_rows = scatter_rows(attn_part)
+    dn1, (_, (up_sum, _), (attn_sum,)) = scatter_tokens(
         [dot_nt(part, qkv_w).astype(bf16) for part in cut(d_qkv)],
-        (None, (up_sum, q_rows), lambda before: (exchange(before[1]), kv_rows)),
-    )
-    kv_sum = exchange(kv_rows)
-    down_sum, gate_sum, up_sum, q_sum, kv_sum = [
-        part.astype(f32) for part in (down_sum, gate_sum, up_sum, q_sum, kv_sum)
+        (None, (up_sum, attn_rows), lambda before: (exchange(before[1]),)),
+    )
+    down_sum, gate_sum, up_sum, attn_sum = [
+        part.astype(f32) for part in (down_sum, gate_sum, up_sum, attn_sum)
     ]
-    q_sum, out_sum = join_cols(q_sum[:, :, :HEAD]), join_cols(q_sum[:, :, HEAD:])
+    q_sum, out_sum, kv_sum = [attn_sum[:, :, i * HEAD : (i + 1) * HEAD] for i in range(3)]
+    q_sum, out_sum = join_cols(q_sum), join_cols(out_sum)
     kv_sum = kv_sum.reshape(KV_HEADS, 2, rows, HEAD)
     d_source = r1 * dn1 - x * (r1 * r1 * r1 * mean(dn1 * x))
     input_grad = copies_back((d_hidden + d_source).astype(bf16))

time: 904 us -> 897 us (level)
    ppermute x24, waiting for transfers between devices: 243 us -> 253 us  [round_ring(): return lax.ppermute(value, GROUP, pairs)]
    all_to_all x9 -> x8, waiting for transfers between devices: 56.2 us -> 50.3 us  [exchange(): lax.all_to_all(blocks, GROUP, split_axis=0, concat_axis=0, tiled=True)]
    all_to_all x9 -> x8, starting transfers between devices: 42.7 us -> 39.2 us  [exchange(): lax.all_to_all(blocks, GROUP, split_axis=0, concat_axis=0, tiled=True)]
    unnamed x300 -> x297, local copies, waits for them, and re-layouts: 49.8 us -> 51.2 us
  transfers between devices with their start and end apart: 94 -> 92, of which waited for: 44 -> 42; matrix products, arithmetic and copies ran while one was open for 31% -> 30% of each run, Pallas kernels for 6% -> 6%
where the time goes in v3:
time: 897 us; the launch traced here: 885 us
  waiting for transfers between devices  361 us (40%)
  matrix products  167 us (19%)
  starting transfers between devices  123 us (14%)
  local copies, waits for them, and re-layouts  86.3 us (10%)
  other arithmetic  75.6 us (8%)
  Pallas kernels  54.6 us (6%)
  between operations  16.9 us (2%)
    ppermute x24, waiting for transfers between devices, round_ring(): return lax.ppermute(value, GROUP, pairs)  253 us
    dot_general x21, matrix products, dot_nn(): lax.dot_general(left, right, (((1,), (0,)), ((), ())), preferred_element_...  67.1 us
    dot_general x20, matrix products, dot_nt(): lax.dot_general(left, right, (((1,), (1,)), ((), ())), preferred_element_...  56.9 us
    unnamed x297, local copies, waits for them, and re-layouts  51.2 us
    all_to_all x8, waiting for transfers between devices, exchange(): lax.all_to_all(blocks, GROUP, split_axis=0, concat_axis=0, tiled=True)  50.3 us
    dot_general x6, matrix products, dot_tn(): lax.dot_general(left, right, (((0,), (0,)), ((), ())), preferred_element_...  43.3 us
    ppermute x6, waiting for transfers between devices, moved_on(): lax.ppermute(value, COPIES, [(t, f) if back else (f, t) for f, t in pairs])  39.9 us
    all_to_all x8, starting transfers between devices, exchange(): lax.all_to_all(blocks, GROUP, split_axis=0, concat_axis=0, tiled=True)  39.2 us
  transfers between devices with their start and end apart: 92, of which 42 were waited for; matrix products, arithmetic and copies ran while one was open for 30% of the time, Pallas kernels for 6%

profile of v3, /device:TPU:0, one launch (start us, length us, event | category | flops | bytes accessed | tf_op | source)
XLA Modules:
  0.0 884.7 jit_solution(6761664352803540347)
XLA Ops:
  11.8 6.5 all-to-all-start
  22.7 22.8 %all-to-all-done = bf16[8,72,768]{2,1,0:T(8,128)(2,1)S(1)} async-done(((bf16[8,72,768]{2,1,0:T(8,128)(2,1)}), bf16[8,72,768]{2,1,0:T(8,128)(2,1)S(1)}, u32[]{:S(2)}, u32[]{:S(2)}) %all-to-all-start) | async-done | bytes 884768 | tf_op jit(solution)/shard_map/all_to_all | solution.py:194
  60.9 14.1 %collective-permute-done.3 = bf16[160,2304]{1,0:T(8,128)(2,1)} collective-permute-done((bf16[160,2304]{1,0:T(8,128)(2,1)}, bf16[160,2304]{1,0:T(8,128)(2,1)}, u32[]{:S(2)}, u32[]{:S(2)}) %collective-permute-start.3) | collective-permute-done | bytes 737312 | tf_op jit(solution)/shard_map/ppermute | solution.py:123
  80.8 12.7 %collective-permute-done.5 = bf16[160,2304]{1,0:T(8,128)(2,1)} collective-permute-done((bf16[160,2304]{1,0:T(8,128)(2,1)}, bf16[160,2304]{1,0:T(8,128)(2,1)}, u32[]{:S(2)}, u32[]{:S(2)}) %collective-permute-start.5) | collective-permute-done | bytes 737312 | tf_op jit(solution)/shard_map/ppermute | solution.py:123
  123.8 9.5 %collective-permute-start.13 = (bf16[8,144]{1,0:T(8,128)(2,1)S(1)}, bf16[8,144]{1,0:T(8,128)(2,1)S(1)}, u32[]{:S(2)}, u32[]{:S(2)}) collective-permute-start(bf16[8,144]{1,0:T(8,128)(2,1)S(1)} %pad_maximum_fusion.9), channel_id=1, source_target_pairs={{0,8},{8,16},{16,24},{24,0},{1,9},{9,17},{17,25},{25,1},{2,10},{10... | collective-permute-start | bytes 6920 | tf_op jit(solution)/shard_map/ppermute | solution.py:33
  136.2 11.1 %collective-permute-done.8 = bf16[1280,256]{1,0:T(8,128)(2,1)S(1)} collective-permute-done((bf16[1280,256]{1,0:T(8,128)(2,1)S(1)}, bf16[1280,256]{1,0:T(8,128)(2,1)S(1)}, u32[]{:S(2)}, u32[]{:S(2)}) %collective-permute-start.8) | collective-permute-done | bytes 655392 | tf_op jit(solution)/shard_map/ppermute | solution.py:49
  153.6 4.6 all-to-all-start.2
  163.2 17.9 %attention_forward.1 = (f32[1280,256]{1,0:T(8,128)S(1)}, f32[1280,1]{1,0:T(8,128)S(1)}) custom-call(s32[21]{0:T(128)S(1)} %pad_add_fusion.meta_ref, bf16[1280,256]{1,0:T(8,128)(2,1)S(1)} %copy-done.25, bf16[5120,256]{1,0:T(8,128)(2,1)S(1)} %copy-done.11, bf16[5120,256]{1,0:T(8,128)(2,1)} %collective-permute-done.16.other_ref), custom_call_target="tpu_custom_call" | custom-call | flops 6710886400 | bytes 7864320 | tf_op jit(solution)/shard_map/attention_forward/pallas_call | solution.py:265
  182.0 8.9 %all-to-all-done.2 = bf16[8,72,1152]{2,1,0:T(8,128)(2,1)} async-done(((bf16[8,72,1152]{2,1,0:T(8,128)(2,1)}), bf16[8,72,1152]{2,1,0:T(8,128)(2,1)}, u32[]{:S(2)}, u32[]{:S(2)}) %all-to-all-start.2) | async-done | bytes 1327136 | tf_op jit(solution)/shard_map/all_to_all | solution.py:194
  208.6 12.1 %collective-permute-done.21 = bf16[160,2304]{1,0:T(8,128)(2,1)} collective-permute-done((bf16[160,2304]{1,0:T(8,128)(2,1)}, bf16[160,2304]{1,0:T(8,128)(2,1)}, u32[]{:S(2)}, u32[]{:S(2)}) %collective-permute-start.21) | collective-permute-done | bytes 737312 | tf_op jit(solution)/shard_map/ppermute | solution.py:123
  230.2 18.5 %all-to-all-done.3 = bf16[8,72,1152]{2,1,0:T(8,128)(2,1)} async-done(((bf16[8,72,1152]{2,1,0:T(8,128)(2,1)}), bf16[8,72,1152]{2,1,0:T(8,128)(2,1)}, u32[]{:S(2)}, u32[]{:S(2)}) %all-to-all-start.3) | async-done | bytes 1327136 | tf_op jit(solution)/shard_map/all_to_all | solution.py:194
  248.7 6.0 collective-permute-done.22
  257.5 5.9 collective-permute-start.23
  263.8 12.7 %collective-permute-done.23 = bf16[160,2304]{1,0:T(8,128)(2,1)} collective-permute-done((bf16[160,2304]{1,0:T(8,128)(2,1)}, bf16[160,2304]{1,0:T(8,128)(2,1)}, u32[]{:S(2)}, u32[]{:S(2)}) %collective-permute-start.23) | collective-permute-done | bytes 737312 | tf_op jit(solution)/shard_map/ppermute | solution.py:123
  286.0 4.7 convolution_convert_fusion.23
  290.7 6.6 fusion.82
  297.3 6.9 collective-permute-done.24
  312.9 11.5 %collective-permute-done.27 = bf16[160,2304]{1,0:T(8,128)(2,1)S(1)} collective-permute-done((bf16[160,2304]{1,0:T(8,128)(2,1)S(1)}, bf16[160,2304]{1,0:T(8,128)(2,1)S(1)}, u32[]{:S(2)}, u32[]{:S(2)}) %collective-permute-start.27) | collective-permute-done | bytes 737312 | tf_op jit(solution)/shard_map/ppermute | solution.py:123
  332.9 11.2 %collective-permute-done.29 = bf16[160,2304]{1,0:T(8,128)(2,1)S(1)} collective-permute-done((bf16[160,2304]{1,0:T(8,128)(2,1)S(1)}, bf16[160,2304]{1,0:T(8,128)(2,1)S(1)}, u32[]{:S(2)}, u32[]{:S(2)}) %collective-permute-start.29) | collective-permute-done | bytes 737312 | tf_op jit(solution)/shard_map/ppermute | solution.py:123
  344.1 4.8 pad_maximum_fusion
  356.6 5.3 convolution_convert_fusion.18
  373.9 10.1 %collective-permute-done.35 = bf16[160,2304]{1,0:T(8,128)(2,1)S(1)} collective-permute-done((bf16[160,2304]{1,0:T(8,128)(2,1)S(1)}, bf16[160,2304]{1,0:T(8,128)(2,1)S(1)}, u32[]{:S(2)}, u32[]{:S(2)}) %collective-permute-start.35) | collective-permute-done | bytes 737312 | tf_op jit(solution)/shard_map/ppermute | solution.py:123
  384.4 6.5 pad_maximum_fusion.2
  394.7 8.3 collective-permute-done.36
  404.1 18.4 %collective-permute-done.37 = bf16[160,2304]{1,0:T(8,128)(2,1)} collective-permute-done((bf16[160,2304]{1,0:T(8,128)(2,1)S(1)}, bf16[160,2304]{1,0:T(8,128)(2,1)}, u32[]{:S(2)}, u32[]{:S(2)}) %collective-permute-start.37) | collective-permute-done | bytes 737312 | tf_op jit(solution)/shard_map/ppermute | solution.py:123
  427.9 5.6 fusion.64
  441.5 4.9 collective-permute-done.38
  459.2 6.6 collective-permute-done.41
  477.3 8.5 collective-permute-done.43
  488.9 9.7 %convolution_convert_fusion.2 = bf16[2304,1152]{1,0:T(8,128)(2,1)} fusion(bf16[1280,2304]{1,0:T(8,128)(2,1)S(1)} %constant_dynamic-update-slice_fusion.22, bf16[1280,1152]{1,0:T(8,128)(2,1)S(1)} %copy-done.52), kind=kOutput, calls=%fused_computation.2 | convolution fusion | flops 6797426688 | bytes 14155776 | tf_op jit(solution)/shard_map/dot_general | solution.py:65
  498.6 7.9 collective-permute-done.49
  512.7 6.3 multiply_convert_fusion
  519.8 11.6 %convolution_convert_fusion.1 = bf16[2304,1152]{1,0:T(8,128)(2,1)} fusion(bf16[1280,2304]{1,0:T(8,128)(2,1)} %get-tuple-element.154, bf16[320,1152]{1,0:T(8,128)(2,1)S(1)} %get-tuple-element.228, bf16[320,1152]{1,0:T(8,128)(2,1)S(1)} %copy-done.97, bf16[320,1152]{1,0:T(8,128)(2,1)S(1)} %copy-done.95, bf16[320,1152]{1,0:T(8,128)(2,1)S(1)} %copy-done.93), kind=kOutput, calls=%fused_computation.1 | convolution fusion | flops 6809223168 | bytes 14155776 | tf_op jit(solution)/shard_map/dot_general | solution.py:65
  532.0 5.0 fusion.197
  537.0 4.7 fusion.11
  548.2 11.9 %convolution_convert_fusion = bf16[2304,1152]{1,0:T(8,128)(2,1)} fusion(bf16[1280,2304]{1,0:T(8,128)(2,1)} %get-tuple-element.154, bf16[320,1152]{1,0:T(8,128)(2,1)S(1)} %copy-done.106, bf16[320,1152]{1,0:T(8,128)(2,1)S(1)} %copy-done.105, bf16[320,1152]{1,0:T(8,128)(2,1)S(1)} %copy-done.103, bf16[320,1152]{1,0:T(8,128)(2,1)S(1)} %copy-done.101), kind=kOutput, calls=%fused_computation | convolution fusion | flops 6809223168 | bytes 14155776 | tf_op jit(solution)/shard_map/dot_general | solution.py:65
  560.1 7.3 collective-permute-done.51
  583.8 9.4 %collective-permute-done.52 = bf16[160,2304]{1,0:T(8,128)(2,1)} collective-permute-done((bf16[160,2304]{1,0:T(8,128)(2,1)S(1)}, bf16[160,2304]{1,0:T(8,128)(2,1)}, u32[]{:S(2)}, u32[]{:S(2)}) %collective-permute-start.52) | collective-permute-done | bytes 737312 | tf_op jit(solution)/shard_map/ppermute | solution.py:123
  604.2 13.2 %collective-permute-done.54 = bf16[160,2304]{1,0:T(8,128)(2,1)S(1)} collective-permute-done((bf16[160,2304]{1,0:T(8,128)(2,1)}, bf16[160,2304]{1,0:T(8,128)(2,1)S(1)}, u32[]{:S(2)}, u32[]{:S(2)}) %collective-permute-start.54) | collective-permute-done | bytes 737312 | tf_op jit(solution)/shard_map/ppermute | solution.py:123
  626.6 15.2 %collective-permute-done.56 = bf16[160,2304]{1,0:T(8,128)(2,1)S(1)} collective-permute-done((bf16[160,2304]{1,0:T(8,128)(2,1)S(1)}, bf16[160,2304]{1,0:T(8,128)(2,1)S(1)}, u32[]{:S(2)}, u32[]{:S(2)}) %collective-permute-start.56) | collective-permute-done | bytes 737312 | tf_op jit(solution)/shard_map/ppermute | solution.py:123
  655.8 32.2 %attention_backward.1 = (f32[1280,256]{1,0:T(8,128)S(1)}, bf16[5120,256]{1,0:T(8,128)(2,1)S(1)}, bf16[5120,256]{1,0:T(8,128)(2,1)S(1)}) custom-call(s32[21]{0:T(128)S(1)} %copy-done.22, bf16[1280,256]{1,0:T(8,128)(2,1)S(1)} %copy-done.26, bf16[1280,256]{1,0:T(8,128)(2,1)S(1)} %to_blocks.3.d_ref, bf16[5120,256]{1,0:T(8,128)(2,1)S(1)} %copy-done.12, ...), custom_call_target="tpu_custom_call" | custom-call | flops 16777216000 | bytes 13107200 | tf_op jit(solution)/shard_map/attention_backward/pallas_call | solution.py:376
  703.4 27.5 %collective-permute-done.66 = bf16[1280,256]{1,0:T(8,128)(2,1)S(1)} collective-permute-done((bf16[1280,256]{1,0:T(8,128)(2,1)S(1)}, bf16[1280,256]{1,0:T(8,128)(2,1)S(1)}, u32[]{:S(2)}, u32[]{:S(2)}) %collective-permute-start.66) | collective-permute-done | bytes 655392 | tf_op jit(solution)/shard_map/ppermute | solution.py:49
  748.2 5.8 copy.70
  758.1 4.6 all-to-all-start.6
  778.0 27.0 %collective-permute-done.73 = bf16[160,2304]{1,0:T(8,128)(2,1)S(1)} collective-permute-done((bf16[160,2304]{1,0:T(8,128)(2,1)S(1)}, bf16[160,2304]{1,0:T(8,128)(2,1)S(1)}, u32[]{:S(2)}, u32[]{:S(2)}) %collective-permute-start.73) | collective-permute-done | bytes 737312 | tf_op jit(solution)/shard_map/ppermute | solution.py:123
  805.3 12.5 %collective-permute-start.74 = (bf16[160,2304]{1,0:T(8,128)(2,1)S(1)}, bf16[160,2304]{1,0:T(8,128)(2,1)}, u32[]{:S(2)}, u32[]{:S(2)}) collective-permute-start(bf16[160,2304]{1,0:T(8,128)(2,1)S(1)} %add_convert_fusion.2), channel_id=1, source_target_pairs={{0,8},{8,16},{16,24},{24,0},{1,25},{9,1},{17,9},{25,17},{2,10},{10... | collective-permute-start | bytes 2211848 | tf_op jit(solution)/shard_map/ppermute | solution.py:123
  826.8 6.0 all-to-all-start.7
  843.2 24.8 %collective-permute-done.75 = bf16[160,2304]{1,0:T(8,128)(2,1)} collective-permute-done((bf16[160,2304]{1,0:T(8,128)(2,1)S(1)}, bf16[160,2304]{1,0:T(8,128)(2,1)}, u32[]{:S(2)}, u32[]{:S(2)}) %collective-permute-start.75) | collective-permute-done | bytes 737312 | tf_op jit(solution)/shard_map/ppermute | solution.py:123
  (663 shorter events, 342.0 us)
Async XLA Ops:
  11.8 33.8 %all-to-all-start = ((bf16[8,72,768]{2,1,0:T(8,128)(2,1)}), bf16[8,72,768]{2,1,0:T(8,128)(2,1)S(1)}, u32[]{:S(2)}, u32[]{:S(2)}) async-start(bf16[8,72,768]{2,1,0:T(8,128)(2,1)} %copy.57), calls=%async_computation | async-start | bytes 1769472 | tf_op jit(solution)/shard_map/all_to_all | solution.py:194
  18.2 86.8 %all-gather.5.cloned.1.call-start = ((), (), s32[]{:S(2)}) async-start(), calls=%async_computation.12 | async-start | bytes 4423680 | tf_op jit(solution)/shard_map/all_gather | solution.py:199
  18.9 34.9 %collective-permute-start.1 = (bf16[160,2304]{1,0:T(8,128)(2,1)S(1)}, bf16[160,2304]{1,0:T(8,128)(2,1)}, u32[]{:S(2)}, u32[]{:S(2)}) collective-permute-start(bf16[160,2304]{1,0:T(8,128)(2,1)S(1)} %get-tuple-element.110), channel_id=1, source_target_pairs={{0,8},{8,16},{16,24},{24,0},{1,25},{9,1},{17,9},{25,17},{2,10},{10... | collective-permute-start | bytes 2211848 | tf_op jit(solution)/shard_map/ppermute | solution.py:123
  20.9 56.1 %collective-permute-start = (bf16[160,2304]{1,0:T(8,128)(2,1)S(1)}, bf16[160,2304]{1,0:T(8,128)(2,1)}, u32[]{:S(2)}, u32[]{:S(2)}) collective-permute-start(bf16[160,2304]{1,0:T(8,128)(2,1)S(1)} %get-tuple-element.110), channel_id=1, source_target_pairs={{0,1},{1,0},{2,3},{3,2},{4,5},{5,4},{6,7},{7,6},{8,9},{9,8},{10,11... | collective-permute-start | bytes 2211848 | tf_op jit(solution)/shard_map/ppermute | solution.py:28
  22.7 33.0 %collective-permute-start.10 = (bf16[1,144]{1,0:T(2,128)(2,1)S(1)}, bf16[1,144]{1,0:T(2,128)(2,1)S(1)}, u32[]{:S(2)}, u32[]{:S(2)}) collective-permute-start(bf16[1,144]{1,0:T(2,128)(2,1)S(1)} %broadcast_in_dim.11), channel_id=1, source_target_pairs={{0,1},{1,0},{2,3},{3,2},{4,5},{5,4},{6,7},{7,6},{8,9},{9,8},{10,11... | collective-permute-start | bytes 872 | tf_op jit(solution)/shard_map/ppermute | solution.py:33
  53.8 21.2 %collective-permute-start.3 = (bf16[160,2304]{1,0:T(8,128)(2,1)}, bf16[160,2304]{1,0:T(8,128)(2,1)}, u32[]{:S(2)}, u32[]{:S(2)}) collective-permute-start(bf16[160,2304]{1,0:T(8,128)(2,1)} %collective-permute-done.1), channel_id=1, source_target_pairs={{0,8},{8,16},{16,24},{24,0},{1,25},{9,1},{17,9},{25,17},{2,10},{10... | collective-permute-start | bytes 2211848 | tf_op jit(solution)/shard_map/ppermute | solution.py:123
  59.4 59.3 %collective-permute-start.12 = (bf16[4,144]{1,0:T(4,128)(2,1)S(1)}, bf16[4,144]{1,0:T(4,128)(2,1)S(1)}, u32[]{:S(2)}, u32[]{:S(2)}) collective-permute-start(bf16[4,144]{1,0:T(4,128)(2,1)S(1)} %pad_maximum_fusion.10), channel_id=1, source_target_pairs={{0,4},{4,0},{1,5},{5,1},{2,6},{6,2},{3,7},{7,3},{8,12},{12,8},{9,1... | collective-permute-start | bytes 3464 | tf_op jit(solution)/shard_map/ppermute | solution.py:33
  60.9 32.6 %collective-permute-start.2 = (bf16[160,2304]{1,0:T(8,128)(2,1)}, bf16[160,2304]{1,0:T(8,128)(2,1)S(1)}, u32[]{:S(2)}, u32[]{:S(2)}) collective-permute-start(bf16[160,2304]{1,0:T(8,128)(2,1)} %collective-permute-done.1), channel_id=1, source_target_pairs={{0,1},{1,0},{2,3},{3,2},{4,5},{5,4},{6,7},{7,6},{8,9},{9,8},{10,11... | collective-permute-start | bytes 2211848 | tf_op jit(solution)/shard_map/ppermute | solution.py:28
  78.2 23.8 %collective-permute-start.4 = (bf16[160,2304]{1,0:T(8,128)(2,1)}, bf16[160,2304]{1,0:T(8,128)(2,1)S(1)}, u32[]{:S(2)}, u32[]{:S(2)}) collective-permute-start(bf16[160,2304]{1,0:T(8,128)(2,1)} %collective-permute-done.3), channel_id=1, source_target_pairs={{0,1},{1,0},{2,3},{3,2},{4,5},{5,4},{6,7},{7,6},{8,9},{9,8},{10,11... | collective-permute-start | bytes 2211848 | tf_op jit(solution)/shard_map/ppermute | solution.py:28
  95.7 54.5 %all-to-all-start.1 = ((bf16[8,72,1152]{2,1,0:T(8,128)(2,1)}), bf16[8,72,1152]{2,1,0:T(8,128)(2,1)}, u32[]{:S(2)}, u32[]{:S(2)}) async-start(bf16[8,72,1152]{2,1,0:T(8,128)(2,1)} %copy.58), calls=%async_computation.1 | async-start | bytes 2654208 | tf_op jit(solution)/shard_map/all_to_all | solution.py:194
  99.9 120.7 %all-gather.7.cloned.1.call-start = ((), (), s32[]{:S(2)}) async-start(), calls=%async_computation.13 | async-start | bytes 6635520 | tf_op jit(solution)/shard_map/all_gather | solution.py:199
  115.2 21.0 %collective-permute-start.9 = (bf16[1280,256]{1,0:T(8,128)(2,1)S(1)}, bf16[1280,256]{1,0:T(8,128)(2,1)S(1)}, u32[]{:S(2)}, u32[]{:S(2)}) collective-permute-start(bf16[1280,256]{1,0:T(8,128)(2,1)S(1)} %get-tuple-element.113), channel_id=1, source_target_pairs={{0,6},{2,4},{4,2},{6,0},{1,7},{3,5},{5,3},{7,1},{8,14},{10,12},{12... | collective-permute-start | bytes 1966088 | tf_op jit(solution)/shard_map/ppermute | solution.py:49
  117.7 29.6 %collective-permute-start.8 = (bf16[1280,256]{1,0:T(8,128)(2,1)S(1)}, bf16[1280,256]{1,0:T(8,128)(2,1)S(1)}, u32[]{:S(2)}, u32[]{:S(2)}) collective-permute-start(bf16[1280,256]{1,0:T(8,128)(2,1)S(1)} %get-tuple-element.113), channel_id=1, source_target_pairs={{0,4},{2,6},{4,0},{6,2},{1,5},{3,7},{5,1},{7,3},{8,12},{10,14},{12... | collective-permute-start | bytes 1966088 | tf_op jit(solution)/shard_map/ppermute | solution.py:49
  118.2 30.0 %collective-permute-start.7 = (bf16[1280,256]{1,0:T(8,128)(2,1)S(1)}, bf16[1280,256]{1,0:T(8,128)(2,1)}, u32[]{:S(2)}, u32[]{:S(2)}) collective-permute-start(bf16[1280,256]{1,0:T(8,128)(2,1)S(1)} %get-tuple-element.113), channel_id=1, source_target_pairs={{0,2},{2,0},{4,6},{6,4},{1,3},{3,1},{5,7},{7,5},{8,10},{10,8},{12,... | collective-permute-start | bytes 1966088 | tf_op jit(solution)/shard_map/ppermute | solution.py:49
  153.6 37.3 %all-to-all-start.2 = ((bf16[8,72,1152]{2,1,0:T(8,128)(2,1)}), bf16[8,72,1152]{2,1,0:T(8,128)(2,1)}, u32[]{:S(2)}, u32[]{:S(2)}) async-start(bf16[8,72,1152]{2,1,0:T(8,128)(2,1)} %copy.59), calls=%async_computation.2 | async-start | bytes 2654208 | tf_op jit(solution)/shard_map/all_to_all | solution.py:194
  158.2 127.7 %all-gather.9.cloned.1.call-start = ((), (), s32[]{:S(2)}) async-start(), calls=%async_computation.14 | async-start | bytes 6635520 | tf_op jit(solution)/shard_map/all_gather | solution.py:199
  199.1 21.6 %collective-permute-start.21 = (bf16[160,2304]{1,0:T(8,128)(2,1)}, bf16[160,2304]{1,0:T(8,128)(2,1)}, u32[]{:S(2)}, u32[]{:S(2)}) collective-permute-start(bf16[160,2304]{1,0:T(8,128)(2,1)} %add_convert_fusion.13), channel_id=1, source_target_pairs={{0,8},{8,16},{16,24},{24,0},{1,25},{9,1},{17,9},{25,17},{2,10},{10... | collective-permute-start | bytes 2211848 | tf_op jit(solution)/shard_map/ppermute | solution.py:123
  204.2 44.5 %all-to-all-start.3 = ((bf16[8,72,1152]{2,1,0:T(8,128)(2,1)}), bf16[8,72,1152]{2,1,0:T(8,128)(2,1)}, u32[]{:S(2)}, u32[]{:S(2)}) async-start(bf16[8,72,1152]{2,1,0:T(8,128)(2,1)} %copy.60), calls=%async_computation.3 | async-start | bytes 2654208 | tf_op jit(solution)/shard_map/all_to_all | solution.py:194
  208.5 142.8 %all-gather.11.cloned.1.call-start = ((), (), s32[]{:S(2)}) async-start(), calls=%async_computation.15 | async-start | bytes 6635520 | tf_op jit(solution)/shard_map/all_gather | solution.py:199
  223.3 31.4 %collective-permute-start.22 = (bf16[160,2304]{1,0:T(8,128)(2,1)}, bf16[160,2304]{1,0:T(8,128)(2,1)}, u32[]{:S(2)}, u32[]{:S(2)}) collective-permute-start(bf16[160,2304]{1,0:T(8,128)(2,1)} %add_convert_fusion.12), channel_id=1, source_target_pairs={{0,8},{8,16},{16,24},{24,0},{1,25},{9,1},{17,9},{25,17},{2,10},{10... | collective-permute-start | bytes 2211848 | tf_op jit(solution)/shard_map/ppermute | solution.py:123
  226.8 28.0 %collective-permute-start.18 = (bf16[160,2304]{1,0:T(8,128)(2,1)}, bf16[160,2304]{1,0:T(8,128)(2,1)}, u32[]{:S(2)}, u32[]{:S(2)}) collective-permute-start(bf16[160,2304]{1,0:T(8,128)(2,1)} %slice.521), channel_id=1, source_target_pairs={{0,1},{1,0},{2,3},{3,2},{4,5},{5,4},{6,7},{7,6},{8,9},{9,8},{10,11... | collective-permute-start | bytes 2211848 | tf_op jit(solution)/shard_map/ppermute | solution.py:28
  229.7 34.1 %collective-permute-start.17 = (bf16[160,2304]{1,0:T(8,128)(2,1)}, bf16[160,2304]{1,0:T(8,128)(2,1)}, u32[]{:S(2)}, u32[]{:S(2)}) collective-permute-start(bf16[160,2304]{1,0:T(8,128)(2,1)} %slice.518), channel_id=1, source_target_pairs={{0,1},{1,0},{2,3},{3,2},{4,5},{5,4},{6,7},{7,6},{8,9},{9,8},{10,11... | collective-permute-start | bytes 2211848 | tf_op jit(solution)/shard_map/ppermute | solution.py:28
  284.1 364.6 %reduce-scatter.7.cloned.1.call-start = ((), (), s32[]{:S(2)}) async-start(), calls=%async_computation.16 | async-start | bytes 6635520 | tf_op jit(solution)/shard_map/reduce_scatter | solution.py:203
  284.2 20.0 %collective-permute-start.24 = (bf16[160,2304]{1,0:T(8,128)(2,1)S(1)}, bf16[160,2304]{1,0:T(8,128)(2,1)S(1)}, u32[]{:S(2)}, u32[]{:S(2)}) collective-permute-start(bf16[160,2304]{1,0:T(8,128)(2,1)S(1)} %get-tuple-element.217), channel_id=1, source_target_pairs={{0,8},{8,16},{16,24},{24,0},{1,25},{9,1},{17,9},{25,17},{2,10},{10... | collective-permute-start | bytes 2211848 | tf_op jit(solution)/shard_map/ppermute | solution.py:123
  364.1 19.9 %collective-permute-start.33 = (bf16[160,2304]{1,0:T(8,128)(2,1)S(1)}, bf16[160,2304]{1,0:T(8,128)(2,1)S(1)}, u32[]{:S(2)}, u32[]{:S(2)}) collective-permute-start(bf16[160,2304]{1,0:T(8,128)(2,1)S(1)} %slice.549), channel_id=1, source_target_pairs={{0,1},{1,0},{2,3},{3,2},{4,5},{5,4},{6,7},{7,6},{8,9},{9,8},{10,11... | collective-permute-start | bytes 2211848 | tf_op jit(solution)/shard_map/ppermute | solution.py:28
  371.6 31.4 %collective-permute-start.32 = (bf16[160,2304]{1,0:T(8,128)(2,1)S(1)}, bf16[160,2304]{1,0:T(8,128)(2,1)S(1)}, u32[]{:S(2)}, u32[]{:S(2)}) collective-permute-start(bf16[160,2304]{1,0:T(8,128)(2,1)S(1)} %slice.547), channel_id=1, source_target_pairs={{0,1},{1,0},{2,3},{3,2},{4,5},{5,4},{6,7},{7,6},{8,9},{9,8},{10,11... | collective-permute-start | bytes 2211848 | tf_op jit(solution)/shard_map/ppermute | solution.py:28
  425.7 20.7 %collective-permute-start.38 = (bf16[160,2304]{1,0:T(8,128)(2,1)S(1)}, bf16[160,2304]{1,0:T(8,128)(2,1)S(1)}, u32[]{:S(2)}, u32[]{:S(2)}) collective-permute-start(bf16[160,2304]{1,0:T(8,128)(2,1)S(1)} %get-tuple-element.214), channel_id=1, source_target_pairs={{0,8},{8,16},{16,24},{24,0},{1,25},{9,1},{17,9},{25,17},{2,10},{10... | collective-permute-start | bytes 2211848 | tf_op jit(solution)/shard_map/ppermute | solution.py:123
  506.5 142.2 %reduce-scatter.9.cloned.1.call-start = ((), (), s32[]{:S(2)}) async-start(), calls=%async_computation.17 | async-start | bytes 6635520 | tf_op jit(solution)/shard_map/reduce_scatter | solution.py:203
  531.9 200.6 %reduce-scatter.11.cloned.1.call-start = ((), (), s32[]{:S(2)}) async-start(), calls=%async_computation.18 | async-start | bytes 6635520 | tf_op jit(solution)/shard_map/reduce_scatter | solution.py:203
  544.5 22.8 %collective-permute-start.40 = (bf16[160,2304]{1,0:T(8,128)(2,1)}, bf16[160,2304]{1,0:T(8,128)(2,1)S(1)}, u32[]{:S(2)}, u32[]{:S(2)}) collective-permute-start(bf16[160,2304]{1,0:T(8,128)(2,1)} %slice.446), channel_id=1, source_target_pairs={{0,1},{1,0},{2,3},{3,2},{4,5},{5,4},{6,7},{7,6},{8,9},{9,8},{10,11... | collective-permute-start | bytes 2211848 | tf_op jit(solution)/shard_map/ppermute | solution.py:28
  593.4 23.9 %collective-permute-start.59 = (f32[8,144]{1,0:T(8,128)S(1)}, f32[8,144]{1,0:T(8,128)S(1)}, u32[]{:S(2)}, u32[]{:S(2)}) collective-permute-start(f32[8,144]{1,0:T(8,128)S(1)} %get-tuple-element.259), channel_id=1, source_target_pairs={{0,24},{8,0},{16,8},{24,16},{1,25},{9,1},{17,9},{25,17},{2,26},{10... | collective-permute-start | bytes 13832 | tf_op jit(solution)/shard_map/ppermute | solution.py:33
  596.1 21.2 %collective-permute-start.61 = (f32[8,144]{1,0:T(8,128)S(1)}, f32[8,144]{1,0:T(8,128)S(1)}, u32[]{:S(2)}, u32[]{:S(2)}) collective-permute-start(f32[8,144]{1,0:T(8,128)S(1)} %get-tuple-element.260), channel_id=1, source_target_pairs={{0,8},{8,16},{16,24},{24,0},{1,9},{9,17},{17,25},{25,1},{2,10},{10... | collective-permute-start | bytes 13832 | tf_op jit(solution)/shard_map/ppermute | solution.py:33
  596.1 21.2 %collective-permute-start.60 = (f32[8,144]{1,0:T(8,128)S(1)}, f32[8,144]{1,0:T(8,128)S(1)}, u32[]{:S(2)}, u32[]{:S(2)}) collective-permute-start(f32[8,144]{1,0:T(8,128)S(1)} %get-tuple-element.261), channel_id=1, source_target_pairs={{0,16},{8,24},{16,0},{24,8},{1,17},{9,25},{17,1},{25,9},{2,18},{10... | collective-permute-start | bytes 13832 | tf_op jit(solution)/shard_map/ppermute | solution.py:33
  596.8 20.6 %collective-permute-start.54 = (bf16[160,2304]{1,0:T(8,128)(2,1)}, bf16[160,2304]{1,0:T(8,128)(2,1)S(1)}, u32[]{:S(2)}, u32[]{:S(2)}) collective-permute-start(bf16[160,2304]{1,0:T(8,128)(2,1)} %collective-permute-done.52), channel_id=1, source_target_pairs={{0,8},{8,16},{16,24},{24,0},{1,25},{9,1},{17,9},{25,17},{2,10},{10... | collective-permute-start | bytes 2211848 | tf_op jit(solution)/shard_map/ppermute | solution.py:123
  621.1 20.6 %collective-permute-start.63 = (f32[2,144]{1,0:T(2,128)S(1)}, f32[2,144]{1,0:T(2,128)S(1)}, u32[]{:S(2)}, u32[]{:S(2)}) collective-permute-start(f32[2,144]{1,0:T(2,128)S(1)} %slice.609), channel_id=1, source_target_pairs={{0,2},{2,0},{1,3},{3,1},{4,6},{6,4},{5,7},{7,5},{8,10},{10,8},{9,1... | collective-permute-start | bytes 3464 | tf_op jit(solution)/shard_map/ppermute | solution.py:33
  648.8 43.2 %all-to-all-start.4 = ((bf16[8,72,1152]{2,1,0:T(8,128)(2,1)}), bf16[8,72,1152]{2,1,0:T(8,128)(2,1)}, u32[]{:S(2)}, u32[]{:S(2)}) async-start(bf16[8,72,1152]{2,1,0:T(8,128)(2,1)} %bitcast.139), calls=%async_computation.6 | async-start | bytes 2654208 | tf_op jit(solution)/shard_map/all_to_all | solution.py:194
  692.4 40.1 %all-to-all-start.5 = ((bf16[8,72,1152]{2,1,0:T(8,128)(2,1)}), bf16[8,72,1152]{2,1,0:T(8,128)(2,1)}, u32[]{:S(2)}, u32[]{:S(2)}) async-start(bf16[8,72,1152]{2,1,0:T(8,128)(2,1)} %bitcast.138), calls=%async_computation.7 | async-start | bytes 2654208 | tf_op jit(solution)/shard_map/all_to_all | solution.py:194
  696.8 130.0 %reduce-scatter.13.cloned.1.call-start = ((), (), s32[]{:S(2)}) async-start(), calls=%async_computation.19 | async-start | bytes 4423680 | tf_op jit(solution)/shard_map/reduce_scatter | solution.py:203
  699.8 31.1 %collective-permute-start.66 = (bf16[1280,256]{1,0:T(8,128)(2,1)S(1)}, bf16[1280,256]{1,0:T(8,128)(2,1)S(1)}, u32[]{:S(2)}, u32[]{:S(2)}) collective-permute-start(bf16[1280,256]{1,0:T(8,128)(2,1)S(1)} %get-tuple-element.224), channel_id=1, source_target_pairs={{2,0},{0,2},{6,4},{4,6},{3,1},{1,3},{7,5},{5,7},{10,8},{8,10},{14,... | collective-permute-start | bytes 1966088 | tf_op jit(solution)/shard_map/ppermute | solution.py:49
  700.8 30.1 %collective-permute-start.68 = (bf16[1280,256]{1,0:T(8,128)(2,1)S(1)}, bf16[1280,256]{1,0:T(8,128)(2,1)S(1)}, u32[]{:S(2)}, u32[]{:S(2)}) collective-permute-start(bf16[1280,256]{1,0:T(8,128)(2,1)S(1)} %get-tuple-element.225), channel_id=1, source_target_pairs={{6,0},{4,2},{2,4},{0,6},{7,1},{5,3},{3,5},{1,7},{14,8},{12,10},{10... | collective-permute-start | bytes 1966088 | tf_op jit(solution)/shard_map/ppermute | solution.py:49
  702.8 29.3 %collective-permute-start.67 = (bf16[1280,256]{1,0:T(8,128)(2,1)S(1)}, bf16[1280,256]{1,0:T(8,128)(2,1)S(1)}, u32[]{:S(2)}, u32[]{:S(2)}) collective-permute-start(bf16[1280,256]{1,0:T(8,128)(2,1)S(1)} %get-tuple-element.226), channel_id=1, source_target_pairs={{4,0},{6,2},{0,4},{2,6},{5,1},{7,3},{1,5},{3,7},{12,8},{14,10},{8,... | collective-permute-start | bytes 1966088 | tf_op jit(solution)/shard_map/ppermute | solution.py:49
  758.1 68.7 %all-to-all-start.6 = ((bf16[8,72,1152]{2,1,0:T(8,128)(2,1)}), bf16[8,72,1152]{2,1,0:T(8,128)(2,1)S(1)}, u32[]{:S(2)}, u32[]{:S(2)}) async-start(bf16[8,72,1152]{2,1,0:T(8,128)(2,1)} %bitcast.140), calls=%async_computation.9 | async-start | bytes 2654208 | tf_op jit(solution)/shard_map/all_to_all | solution.py:194
  767.5 37.5 %collective-permute-start.73 = (bf16[160,2304]{1,0:T(8,128)(2,1)S(1)}, bf16[160,2304]{1,0:T(8,128)(2,1)S(1)}, u32[]{:S(2)}, u32[]{:S(2)}) collective-permute-start(bf16[160,2304]{1,0:T(8,128)(2,1)S(1)} %add_convert_fusion.3), channel_id=1, source_target_pairs={{0,8},{8,16},{16,24},{24,0},{1,25},{9,1},{17,9},{25,17},{2,10},{10... | collective-permute-start | bytes 2211848 | tf_op jit(solution)/shard_map/ppermute | solution.py:123
  776.2 56.6 %collective-permute-start.70 = (bf16[160,2304]{1,0:T(8,128)(2,1)}, bf16[160,2304]{1,0:T(8,128)(2,1)}, u32[]{:S(2)}, u32[]{:S(2)}) collective-permute-start(bf16[160,2304]{1,0:T(8,128)(2,1)} %slice.615), channel_id=1, source_target_pairs={{0,1},{1,0},{2,3},{3,2},{4,5},{5,4},{6,7},{7,6},{8,9},{9,8},{10,11... | collective-permute-start | bytes 2211848 | tf_op jit(solution)/shard_map/ppermute | solution.py:28
  805.3 21.5 %collective-permute-start.74 = (bf16[160,2304]{1,0:T(8,128)(2,1)S(1)}, bf16[160,2304]{1,0:T(8,128)(2,1)}, u32[]{:S(2)}, u32[]{:S(2)}) collective-permute-start(bf16[160,2304]{1,0:T(8,128)(2,1)S(1)} %add_convert_fusion.2), channel_id=1, source_target_pairs={{0,8},{8,16},{16,24},{24,0},{1,25},{9,1},{17,9},{25,17},{2,10},{10... | collective-permute-start | bytes 2211848 | tf_op jit(solution)/shard_map/ppermute | solution.py:123
  819.8 48.3 %collective-permute-start.69 = (bf16[160,2304]{1,0:T(8,128)(2,1)}, bf16[160,2304]{1,0:T(8,128)(2,1)}, u32[]{:S(2)}, u32[]{:S(2)}) collective-permute-start(bf16[160,2304]{1,0:T(8,128)(2,1)} %slice.613), channel_id=1, source_target_pairs={{0,1},{1,0},{2,3},{3,2},{4,5},{5,4},{6,7},{7,6},{8,9},{9,8},{10,11... | collective-permute-start | bytes 2211848 | tf_op jit(solution)/shard_map/ppermute | solution.py:28
  826.8 41.3 %all-to-all-start.7 = ((bf16[8,72,768]{2,1,0:T(8,128)(2,1)}), bf16[8,72,768]{2,1,0:T(8,128)(2,1)S(1)}, u32[]{:S(2)}, u32[]{:S(2)}) async-start(bf16[8,72,768]{2,1,0:T(8,128)(2,1)} %bitcast.147), calls=%async_computation.10 | async-start | bytes 1769472 | tf_op jit(solution)/shard_map/all_to_all | solution.py:194
  834.6 33.4 %collective-permute-start.75 = (bf16[160,2304]{1,0:T(8,128)(2,1)S(1)}, bf16[160,2304]{1,0:T(8,128)(2,1)}, u32[]{:S(2)}, u32[]{:S(2)}) collective-permute-start(bf16[160,2304]{1,0:T(8,128)(2,1)S(1)} %add_convert_fusion.1), channel_id=1, source_target_pairs={{0,8},{8,16},{16,24},{24,0},{1,25},{9,1},{17,9},{25,17},{2,10},{10... | collective-permute-start | bytes 2211848 | tf_op jit(solution)/shard_map/ppermute | solution.py:123
  (179 other events, 1894.8 us)
Sparse Core Ops, SparseCore 0:
  46.6 46.8 all-gather.4
  150.3 62.1 all-gather.6
  214.3 61.9 all-gather.8
  284.3 60.9 all-gather.10
  506.6 61.0 reduce-scatter.6
  570.6 62.0 reduce-scatter.8
  635.6 61.9 reduce-scatter.10
  754.1 47.4 reduce-scatter.12

commit v4 on v3

--- a/solution.py
+++ b/solution.py
@@ -172,7 +172,7 @@
     return value[0]
 
 
-def scatter_tokens(chunks, beside=(None, None, None)):
+def scatter_tokens(chunks, beside=(None, None, None), first=()):
     rows = chunks[0].shape[0] // 2
     carried = None
     beside = list(beside)
@@ -183,9 +183,11 @@
             here = here + carried.astype(f32)
         if step == RING - 1:
             return here, beside
+        if step == 0 and first:
+            here, *first = join(here, *first)
         carried = round_ring(here.astype(bf16))
         if callable(beside[step]):
-            beside[step] = beside[step](beside[step - 1])
+            beside[step] = beside[step](beside[step - 1] if step > 1 else first)
         if beside[step] is not None:
             carried, *beside[step] = join(carried, *beside[step])
 
@@ -654,15 +656,20 @@
     d_q = to_chunks(d_query, core, tables)
     d_k = to_chunks(d_own, core, tables, keyed=True)
     d_qkv = jnp.concatenate([d_q, d_k], axis=1)
-    q_part = dot_tn(x1, d_q)
-    out_part = dot_tn(jnp.concatenate(x4, axis=0), attended_b)
-    kv_part = dot_tn(x1, d_k)
-    attn_part = jnp.concatenate([q_part, out_part, kv_part], axis=1).astype(bf16)
-    d_qkv, attn_part = join(d_qkv, attn_part)
-    attn_rows = scatter_rows(attn_part)
+
+    def attention_rows(first):
+        q_side, k_side, *x4_parts = first
+        parts = [
+            dot_tn(x1, q_side),
+            dot_tn(jnp.concatenate(x4_parts, axis=0), attended_b),
+            dot_tn(x1, k_side),
+        ]
+        return up_sum, scatter_rows(jnp.concatenate(parts, axis=1).astype(bf16))
+
     dn1, (_, (up_sum, _), (attn_sum,)) = scatter_tokens(
         [dot_nt(part, qkv_w).astype(bf16) for part in cut(d_qkv)],
-        (None, (up_sum, attn_rows), lambda before: (exchange(before[1]),)),
+        (None, attention_rows, lambda before: (exchange(before[1]),)),
+        (d_q, d_k, *x4),
     )
     down_sum, gate_sum, up_sum, attn_sum = [
         part.astype(f32) for part in (down_sum, gate_sum, up_sum, attn_sum)

time: 897 us -> 895 us (level)
    unnamed x297 -> x301, local copies, waits for them, and re-layouts: 51.2 us -> 51.4 us
  transfers between devices with their start and end apart: 92 -> 92, of which waited for: 42 -> 43; matrix products, arithmetic and copies ran while one was open for 30% -> 30% of each run, Pallas kernels for 6% -> 6%
where the time goes in v4:
time: 895 us; the launch traced here: 883 us
  waiting for transfers between devices  365 us (41%)
  matrix products  163 us (18%)
  starting transfers between devices  123 us (14%)
  local copies, waits for them, and re-layouts  85.6 us (10%)
  other arithmetic  75 us (8%)
  Pallas kernels  54.6 us (6%)
  between operations  16.9 us (2%)
    ppermute x24, waiting for transfers between devices, round_ring(): return lax.ppermute(value, GROUP, pairs)  255 us
    dot_general x21, matrix products, dot_nn(): lax.dot_general(left, right, (((1,), (0,)), ((), ())), preferred_element_...  67.1 us
    dot_general x20, matrix products, dot_nt(): lax.dot_general(left, right, (((1,), (1,)), ((), ())), preferred_element_...  55.2 us
    unnamed x301, local copies, waits for them, and re-layouts  51.4 us
    all_to_all x8, waiting for transfers between devices, exchange(): lax.all_to_all(blocks, GROUP, split_axis=0, concat_axis=0, tiled=True)  50.2 us
    dot_general x6, matrix products, dot_tn(): lax.dot_general(left, right, (((0,), (0,)), ((), ())), preferred_element_...  40.1 us
    ppermute x6, waiting for transfers between devices, moved_on(): lax.ppermute(value, COPIES, [(t, f) if back else (f, t) for f, t in pairs])  39.9 us
    all_to_all x8, starting transfers between devices, exchange(): lax.all_to_all(blocks, GROUP, split_axis=0, concat_axis=0, tiled=True)  39.1 us
  transfers between devices with their start and end apart: 92, of which 43 were waited for; matrix products, arithmetic and copies ran while one was open for 30% of the time, Pallas kernels for 6%

profile of v4, /device:TPU:0, one launch (start us, length us, event | category | flops | bytes accessed | tf_op | source)
XLA Modules:
  0.0 882.6 jit_solution(5715304549612375392)
XLA Ops:
  11.8 6.5 all-to-all-start
  22.7 22.8 %all-to-all-done = bf16[8,72,768]{2,1,0:T(8,128)(2,1)S(1)} async-done(((bf16[8,72,768]{2,1,0:T(8,128)(2,1)}), bf16[8,72,768]{2,1,0:T(8,128)(2,1)S(1)}, u32[]{:S(2)}, u32[]{:S(2)}) %all-to-all-start) | async-done | bytes 884768 | tf_op jit(solution)/shard_map/all_to_all | solution.py:196
  60.9 14.1 %collective-permute-done.3 = bf16[160,2304]{1,0:T(8,128)(2,1)} collective-permute-done((bf16[160,2304]{1,0:T(8,128)(2,1)}, bf16[160,2304]{1,0:T(8,128)(2,1)}, u32[]{:S(2)}, u32[]{:S(2)}) %collective-permute-start.3) | collective-permute-done | bytes 737312 | tf_op jit(solution)/shard_map/ppermute | solution.py:123
  80.8 12.7 %collective-permute-done.5 = bf16[160,2304]{1,0:T(8,128)(2,1)} collective-permute-done((bf16[160,2304]{1,0:T(8,128)(2,1)}, bf16[160,2304]{1,0:T(8,128)(2,1)}, u32[]{:S(2)}, u32[]{:S(2)}) %collective-permute-start.5) | collective-permute-done | bytes 737312 | tf_op jit(solution)/shard_map/ppermute | solution.py:123
  123.8 9.5 %collective-permute-start.13 = (bf16[8,144]{1,0:T(8,128)(2,1)S(1)}, bf16[8,144]{1,0:T(8,128)(2,1)S(1)}, u32[]{:S(2)}, u32[]{:S(2)}) collective-permute-start(bf16[8,144]{1,0:T(8,128)(2,1)S(1)} %pad_maximum_fusion.10), channel_id=1, source_target_pairs={{0,8},{8,16},{16,24},{24,0},{1,9},{9,17},{17,25},{25,1},{2,10},{10... | collective-permute-start | bytes 6920 | tf_op jit(solution)/shard_map/ppermute | solution.py:33
  136.2 11.1 %collective-permute-done.8 = bf16[1280,256]{1,0:T(8,128)(2,1)S(1)} collective-permute-done((bf16[1280,256]{1,0:T(8,128)(2,1)S(1)}, bf16[1280,256]{1,0:T(8,128)(2,1)S(1)}, u32[]{:S(2)}, u32[]{:S(2)}) %collective-permute-start.8) | collective-permute-done | bytes 655392 | tf_op jit(solution)/shard_map/ppermute | solution.py:49
  153.6 4.6 all-to-all-start.2
  163.2 17.9 %attention_forward.1 = (f32[1280,256]{1,0:T(8,128)S(1)}, f32[1280,1]{1,0:T(8,128)S(1)}) custom-call(s32[21]{0:T(128)S(1)} %pad_add_fusion.meta_ref, bf16[1280,256]{1,0:T(8,128)(2,1)S(1)} %copy-done.27, bf16[5120,256]{1,0:T(8,128)(2,1)S(1)} %copy-done.11, bf16[5120,256]{1,0:T(8,128)(2,1)} %collective-permute-done.16.other_ref), custom_call_target="tpu_custom_call" | custom-call | flops 6710886400 | bytes 7864320 | tf_op jit(solution)/shard_map/attention_forward/pallas_call | solution.py:267
  182.0 8.9 %all-to-all-done.2 = bf16[8,72,1152]{2,1,0:T(8,128)(2,1)} async-done(((bf16[8,72,1152]{2,1,0:T(8,128)(2,1)}), bf16[8,72,1152]{2,1,0:T(8,128)(2,1)}, u32[]{:S(2)}, u32[]{:S(2)}) %all-to-all-start.2) | async-done | bytes 1327136 | tf_op jit(solution)/shard_map/all_to_all | solution.py:196
  208.6 12.1 %collective-permute-done.21 = bf16[160,2304]{1,0:T(8,128)(2,1)} collective-permute-done((bf16[160,2304]{1,0:T(8,128)(2,1)}, bf16[160,2304]{1,0:T(8,128)(2,1)}, u32[]{:S(2)}, u32[]{:S(2)}) %collective-permute-start.21) | collective-permute-done | bytes 737312 | tf_op jit(solution)/shard_map/ppermute | solution.py:123
  230.2 18.5 %all-to-all-done.3 = bf16[8,72,1152]{2,1,0:T(8,128)(2,1)} async-done(((bf16[8,72,1152]{2,1,0:T(8,128)(2,1)}), bf16[8,72,1152]{2,1,0:T(8,128)(2,1)}, u32[]{:S(2)}, u32[]{:S(2)}) %all-to-all-start.3) | async-done | bytes 1327136 | tf_op jit(solution)/shard_map/all_to_all | solution.py:196
  248.7 6.0 collective-permute-done.22
  257.5 5.9 collective-permute-start.23
  263.8 12.7 %collective-permute-done.23 = bf16[160,2304]{1,0:T(8,128)(2,1)} collective-permute-done((bf16[160,2304]{1,0:T(8,128)(2,1)}, bf16[160,2304]{1,0:T(8,128)(2,1)}, u32[]{:S(2)}, u32[]{:S(2)}) %collective-permute-start.23) | collective-permute-done | bytes 737312 | tf_op jit(solution)/shard_map/ppermute | solution.py:123
  286.0 4.7 convolution_convert_fusion.23
  290.7 6.6 fusion.82
  297.3 6.9 collective-permute-done.24
  312.9 11.5 %collective-permute-done.27 = bf16[160,2304]{1,0:T(8,128)(2,1)S(1)} collective-permute-done((bf16[160,2304]{1,0:T(8,128)(2,1)S(1)}, bf16[160,2304]{1,0:T(8,128)(2,1)S(1)}, u32[]{:S(2)}, u32[]{:S(2)}) %collective-permute-start.27) | collective-permute-done | bytes 737312 | tf_op jit(solution)/shard_map/ppermute | solution.py:123
  332.9 11.2 %collective-permute-done.29 = bf16[160,2304]{1,0:T(8,128)(2,1)S(1)} collective-permute-done((bf16[160,2304]{1,0:T(8,128)(2,1)S(1)}, bf16[160,2304]{1,0:T(8,128)(2,1)S(1)}, u32[]{:S(2)}, u32[]{:S(2)}) %collective-permute-start.29) | collective-permute-done | bytes 737312 | tf_op jit(solution)/shard_map/ppermute | solution.py:123
  344.1 4.7 pad_maximum_fusion
  351.2 4.6 convolution_convert_fusion.7
  356.5 5.3 convolution_convert_fusion.18
  373.8 10.1 %collective-permute-done.35 = bf16[160,2304]{1,0:T(8,128)(2,1)S(1)} collective-permute-done((bf16[160,2304]{1,0:T(8,128)(2,1)S(1)}, bf16[160,2304]{1,0:T(8,128)(2,1)S(1)}, u32[]{:S(2)}, u32[]{:S(2)}) %collective-permute-start.35) | collective-permute-done | bytes 737312 | tf_op jit(solution)/shard_map/ppermute | solution.py:123
  384.3 6.5 pad_maximum_fusion.2
  394.6 8.3 collective-permute-done.36
  404.0 18.4 %collective-permute-done.37 = bf16[160,2304]{1,0:T(8,128)(2,1)} collective-permute-done((bf16[160,2304]{1,0:T(8,128)(2,1)S(1)}, bf16[160,2304]{1,0:T(8,128)(2,1)}, u32[]{:S(2)}, u32[]{:S(2)}) %collective-permute-start.37) | collective-permute-done | bytes 737312 | tf_op jit(solution)/shard_map/ppermute | solution.py:123
  427.8 5.6 fusion.64
  441.4 4.9 collective-permute-done.38
  459.1 6.7 collective-permute-done.41
  477.2 8.5 collective-permute-done.43
  488.8 9.7 %convolution_convert_fusion.2 = bf16[2304,1152]{1,0:T(8,128)(2,1)} fusion(bf16[1280,2304]{1,0:T(8,128)(2,1)S(1)} %constant_dynamic-update-slice_fusion.22, bf16[1280,1152]{1,0:T(8,128)(2,1)S(1)} %copy-done.55), kind=kOutput, calls=%fused_computation.2 | convolution fusion | flops 6797426688 | bytes 14155776 | tf_op jit(solution)/shard_map/dot_general | solution.py:65
  498.5 7.9 collective-permute-done.49
  512.6 6.3 multiply_convert_fusion
  519.7 11.6 %convolution_convert_fusion.1 = bf16[2304,1152]{1,0:T(8,128)(2,1)} fusion(bf16[1280,2304]{1,0:T(8,128)(2,1)} %get-tuple-element.159, bf16[320,1152]{1,0:T(8,128)(2,1)S(1)} %get-tuple-element.238, bf16[320,1152]{1,0:T(8,128)(2,1)S(1)} %copy-done.99, bf16[320,1152]{1,0:T(8,128)(2,1)S(1)} %copy-done.97, bf16[320,1152]{1,0:T(8,128)(2,1)S(1)} %copy-done.95), kind=kOutput, calls=%fused_computation.1 | convolution fusion | flops 6809223168 | bytes 14155776 | tf_op jit(solution)/shard_map/dot_general | solution.py:65
  531.9 5.0 fusion.204
  536.9 4.7 fusion.11
  548.1 11.9 %convolution_convert_fusion = bf16[2304,1152]{1,0:T(8,128)(2,1)} fusion(bf16[1280,2304]{1,0:T(8,128)(2,1)} %get-tuple-element.159, bf16[320,1152]{1,0:T(8,128)(2,1)S(1)} %copy-done.108, bf16[320,1152]{1,0:T(8,128)(2,1)S(1)} %copy-done.107, bf16[320,1152]{1,0:T(8,128)(2,1)S(1)} %copy-done.105, bf16[320,1152]{1,0:T(8,128)(2,1)S(1)} %copy-done.103), kind=kOutput, calls=%fused_computation | convolution fusion | flops 6809223168 | bytes 14155776 | tf_op jit(solution)/shard_map/dot_general | solution.py:65
  560.1 7.2 collective-permute-done.51
  583.7 9.4 %collective-permute-done.52 = bf16[160,2304]{1,0:T(8,128)(2,1)} collective-permute-done((bf16[160,2304]{1,0:T(8,128)(2,1)S(1)}, bf16[160,2304]{1,0:T(8,128)(2,1)}, u32[]{:S(2)}, u32[]{:S(2)}) %collective-permute-start.52) | collective-permute-done | bytes 737312 | tf_op jit(solution)/shard_map/ppermute | solution.py:123
  604.1 13.1 %collective-permute-done.54 = bf16[160,2304]{1,0:T(8,128)(2,1)S(1)} collective-permute-done((bf16[160,2304]{1,0:T(8,128)(2,1)}, bf16[160,2304]{1,0:T(8,128)(2,1)S(1)}, u32[]{:S(2)}, u32[]{:S(2)}) %collective-permute-start.54) | collective-permute-done | bytes 737312 | tf_op jit(solution)/shard_map/ppermute | solution.py:123
  626.5 15.2 %collective-permute-done.56 = bf16[160,2304]{1,0:T(8,128)(2,1)S(1)} collective-permute-done((bf16[160,2304]{1,0:T(8,128)(2,1)S(1)}, bf16[160,2304]{1,0:T(8,128)(2,1)S(1)}, u32[]{:S(2)}, u32[]{:S(2)}) %collective-permute-start.56) | collective-permute-done | bytes 737312 | tf_op jit(solution)/shard_map/ppermute | solution.py:123
  655.7 32.2 %attention_backward.1 = (f32[1280,256]{1,0:T(8,128)S(1)}, bf16[5120,256]{1,0:T(8,128)(2,1)S(1)}, bf16[5120,256]{1,0:T(8,128)(2,1)S(1)}) custom-call(s32[21]{0:T(128)S(1)} %copy-done.24, bf16[1280,256]{1,0:T(8,128)(2,1)S(1)} %copy-done.28, bf16[1280,256]{1,0:T(8,128)(2,1)S(1)} %to_blocks.3.d_ref, bf16[5120,256]{1,0:T(8,128)(2,1)S(1)} %copy-done.12, ...), custom_call_target="tpu_custom_call" | custom-call | flops 16777216000 | bytes 13107200 | tf_op jit(solution)/shard_map/attention_backward/pallas_call | solution.py:378
  703.2 27.5 %collective-permute-done.66 = bf16[1280,256]{1,0:T(8,128)(2,1)S(1)} collective-permute-done((bf16[1280,256]{1,0:T(8,128)(2,1)S(1)}, bf16[1280,256]{1,0:T(8,128)(2,1)S(1)}, u32[]{:S(2)}, u32[]{:S(2)}) %collective-permute-start.66) | collective-permute-done | bytes 655392 | tf_op jit(solution)/shard_map/ppermute | solution.py:49
  749.7 5.8 copy.70
  774.2 28.7 %collective-permute-done.73 = bf16[160,2304]{1,0:T(8,128)(2,1)S(1)} collective-permute-done((bf16[160,2304]{1,0:T(8,128)(2,1)S(1)}, bf16[160,2304]{1,0:T(8,128)(2,1)S(1)}, u32[]{:S(2)}, u32[]{:S(2)}) %collective-permute-start.73) | collective-permute-done | bytes 737312 | tf_op jit(solution)/shard_map/ppermute | solution.py:123
  803.2 12.5 %collective-permute-start.74 = (bf16[160,2304]{1,0:T(8,128)(2,1)S(1)}, bf16[160,2304]{1,0:T(8,128)(2,1)}, u32[]{:S(2)}, u32[]{:S(2)}) collective-permute-start(bf16[160,2304]{1,0:T(8,128)(2,1)S(1)} %add_convert_fusion.2), channel_id=1, source_target_pairs={{0,8},{8,16},{16,24},{24,0},{1,25},{9,1},{17,9},{25,17},{2,10},{10... | collective-permute-start | bytes 2211848 | tf_op jit(solution)/shard_map/ppermute | solution.py:123
  824.6 6.0 all-to-all-start.7
  841.1 24.8 %collective-permute-done.75 = bf16[160,2304]{1,0:T(8,128)(2,1)} collective-permute-done((bf16[160,2304]{1,0:T(8,128)(2,1)S(1)}, bf16[160,2304]{1,0:T(8,128)(2,1)}, u32[]{:S(2)}, u32[]{:S(2)}) %collective-permute-start.75) | collective-permute-done | bytes 737312 | tf_op jit(solution)/shard_map/ppermute | solution.py:123
  (666 shorter events, 338.5 us)
Async XLA Ops:
  11.8 33.8 %all-to-all-start = ((bf16[8,72,768]{2,1,0:T(8,128)(2,1)}), bf16[8,72,768]{2,1,0:T(8,128)(2,1)S(1)}, u32[]{:S(2)}, u32[]{:S(2)}) async-start(bf16[8,72,768]{2,1,0:T(8,128)(2,1)} %copy.57), calls=%async_computation | async-start | bytes 1769472 | tf_op jit(solution)/shard_map/all_to_all | solution.py:196
  18.2 86.8 %all-gather.5.cloned.1.call-start = ((), (), s32[]{:S(2)}) async-start(), calls=%async_computation.12 | async-start | bytes 4423680 | tf_op jit(solution)/shard_map/all_gather | solution.py:201
  18.9 34.9 %collective-permute-start.1 = (bf16[160,2304]{1,0:T(8,128)(2,1)S(1)}, bf16[160,2304]{1,0:T(8,128)(2,1)}, u32[]{:S(2)}, u32[]{:S(2)}) collective-permute-start(bf16[160,2304]{1,0:T(8,128)(2,1)S(1)} %get-tuple-element.115), channel_id=1, source_target_pairs={{0,8},{8,16},{16,24},{24,0},{1,25},{9,1},{17,9},{25,17},{2,10},{10... | collective-permute-start | bytes 2211848 | tf_op jit(solution)/shard_map/ppermute | solution.py:123
  20.9 56.1 %collective-permute-start = (bf16[160,2304]{1,0:T(8,128)(2,1)S(1)}, bf16[160,2304]{1,0:T(8,128)(2,1)}, u32[]{:S(2)}, u32[]{:S(2)}) collective-permute-start(bf16[160,2304]{1,0:T(8,128)(2,1)S(1)} %get-tuple-element.115), channel_id=1, source_target_pairs={{0,1},{1,0},{2,3},{3,2},{4,5},{5,4},{6,7},{7,6},{8,9},{9,8},{10,11... | collective-permute-start | bytes 2211848 | tf_op jit(solution)/shard_map/ppermute | solution.py:28
  22.7 33.0 %collective-permute-start.10 = (bf16[1,144]{1,0:T(2,128)(2,1)S(1)}, bf16[1,144]{1,0:T(2,128)(2,1)S(1)}, u32[]{:S(2)}, u32[]{:S(2)}) collective-permute-start(bf16[1,144]{1,0:T(2,128)(2,1)S(1)} %broadcast_in_dim.11), channel_id=1, source_target_pairs={{0,1},{1,0},{2,3},{3,2},{4,5},{5,4},{6,7},{7,6},{8,9},{9,8},{10,11... | collective-permute-start | bytes 872 | tf_op jit(solution)/shard_map/ppermute | solution.py:33
  53.8 21.2 %collective-permute-start.3 = (bf16[160,2304]{1,0:T(8,128)(2,1)}, bf16[160,2304]{1,0:T(8,128)(2,1)}, u32[]{:S(2)}, u32[]{:S(2)}) collective-permute-start(bf16[160,2304]{1,0:T(8,128)(2,1)} %collective-permute-done.1), channel_id=1, source_target_pairs={{0,8},{8,16},{16,24},{24,0},{1,25},{9,1},{17,9},{25,17},{2,10},{10... | collective-permute-start | bytes 2211848 | tf_op jit(solution)/shard_map/ppermute | solution.py:123
  59.4 59.3 %collective-permute-start.12 = (bf16[4,144]{1,0:T(4,128)(2,1)S(1)}, bf16[4,144]{1,0:T(4,128)(2,1)S(1)}, u32[]{:S(2)}, u32[]{:S(2)}) collective-permute-start(bf16[4,144]{1,0:T(4,128)(2,1)S(1)} %pad_maximum_fusion.11), channel_id=1, source_target_pairs={{0,4},{4,0},{1,5},{5,1},{2,6},{6,2},{3,7},{7,3},{8,12},{12,8},{9,1... | collective-permute-start | bytes 3464 | tf_op jit(solution)/shard_map/ppermute | solution.py:33
  60.9 32.6 %collective-permute-start.2 = (bf16[160,2304]{1,0:T(8,128)(2,1)}, bf16[160,2304]{1,0:T(8,128)(2,1)S(1)}, u32[]{:S(2)}, u32[]{:S(2)}) collective-permute-start(bf16[160,2304]{1,0:T(8,128)(2,1)} %collective-permute-done.1), channel_id=1, source_target_pairs={{0,1},{1,0},{2,3},{3,2},{4,5},{5,4},{6,7},{7,6},{8,9},{9,8},{10,11... | collective-permute-start | bytes 2211848 | tf_op jit(solution)/shard_map/ppermute | solution.py:28
  78.2 23.8 %collective-permute-start.4 = (bf16[160,2304]{1,0:T(8,128)(2,1)}, bf16[160,2304]{1,0:T(8,128)(2,1)S(1)}, u32[]{:S(2)}, u32[]{:S(2)}) collective-permute-start(bf16[160,2304]{1,0:T(8,128)(2,1)} %collective-permute-done.3), channel_id=1, source_target_pairs={{0,1},{1,0},{2,3},{3,2},{4,5},{5,4},{6,7},{7,6},{8,9},{9,8},{10,11... | collective-permute-start | bytes 2211848 | tf_op jit(solution)/shard_map/ppermute | solution.py:28
  95.6 54.5 %all-to-all-start.1 = ((bf16[8,72,1152]{2,1,0:T(8,128)(2,1)}), bf16[8,72,1152]{2,1,0:T(8,128)(2,1)}, u32[]{:S(2)}, u32[]{:S(2)}) async-start(bf16[8,72,1152]{2,1,0:T(8,128)(2,1)} %copy.58), calls=%async_computation.1 | async-start | bytes 2654208 | tf_op jit(solution)/shard_map/all_to_all | solution.py:196
  99.9 120.7 %all-gather.7.cloned.1.call-start = ((), (), s32[]{:S(2)}) async-start(), calls=%async_computation.13 | async-start | bytes 6635520 | tf_op jit(solution)/shard_map/all_gather | solution.py:201
  115.2 21.0 %collective-permute-start.9 = (bf16[1280,256]{1,0:T(8,128)(2,1)S(1)}, bf16[1280,256]{1,0:T(8,128)(2,1)S(1)}, u32[]{:S(2)}, u32[]{:S(2)}) collective-permute-start(bf16[1280,256]{1,0:T(8,128)(2,1)S(1)} %get-tuple-element.118), channel_id=1, source_target_pairs={{0,6},{2,4},{4,2},{6,0},{1,7},{3,5},{5,3},{7,1},{8,14},{10,12},{12... | collective-permute-start | bytes 1966088 | tf_op jit(solution)/shard_map/ppermute | solution.py:49
  117.7 29.7 %collective-permute-start.8 = (bf16[1280,256]{1,0:T(8,128)(2,1)S(1)}, bf16[1280,256]{1,0:T(8,128)(2,1)S(1)}, u32[]{:S(2)}, u32[]{:S(2)}) collective-permute-start(bf16[1280,256]{1,0:T(8,128)(2,1)S(1)} %get-tuple-element.118), channel_id=1, source_target_pairs={{0,4},{2,6},{4,0},{6,2},{1,5},{3,7},{5,1},{7,3},{8,12},{10,14},{12... | collective-permute-start | bytes 1966088 | tf_op jit(solution)/shard_map/ppermute | solution.py:49
  118.2 30.0 %collective-permute-start.7 = (bf16[1280,256]{1,0:T(8,128)(2,1)S(1)}, bf16[1280,256]{1,0:T(8,128)(2,1)}, u32[]{:S(2)}, u32[]{:S(2)}) collective-permute-start(bf16[1280,256]{1,0:T(8,128)(2,1)S(1)} %get-tuple-element.118), channel_id=1, source_target_pairs={{0,2},{2,0},{4,6},{6,4},{1,3},{3,1},{5,7},{7,5},{8,10},{10,8},{12,... | collective-permute-start | bytes 1966088 | tf_op jit(solution)/shard_map/ppermute | solution.py:49
  153.6 37.3 %all-to-all-start.2 = ((bf16[8,72,1152]{2,1,0:T(8,128)(2,1)}), bf16[8,72,1152]{2,1,0:T(8,128)(2,1)}, u32[]{:S(2)}, u32[]{:S(2)}) async-start(bf16[8,72,1152]{2,1,0:T(8,128)(2,1)} %copy.59), calls=%async_computation.2 | async-start | bytes 2654208 | tf_op jit(solution)/shard_map/all_to_all | solution.py:196
  158.2 127.8 %all-gather.9.cloned.1.call-start = ((), (), s32[]{:S(2)}) async-start(), calls=%async_computation.14 | async-start | bytes 6635520 | tf_op jit(solution)/shard_map/all_gather | solution.py:201
  199.1 21.6 %collective-permute-start.21 = (bf16[160,2304]{1,0:T(8,128)(2,1)}, bf16[160,2304]{1,0:T(8,128)(2,1)}, u32[]{:S(2)}, u32[]{:S(2)}) collective-permute-start(bf16[160,2304]{1,0:T(8,128)(2,1)} %add_convert_fusion.12), channel_id=1, source_target_pairs={{0,8},{8,16},{16,24},{24,0},{1,25},{9,1},{17,9},{25,17},{2,10},{10... | collective-permute-start | bytes 2211848 | tf_op jit(solution)/shard_map/ppermute | solution.py:123
  204.2 44.5 %all-to-all-start.3 = ((bf16[8,72,1152]{2,1,0:T(8,128)(2,1)}), bf16[8,72,1152]{2,1,0:T(8,128)(2,1)}, u32[]{:S(2)}, u32[]{:S(2)}) async-start(bf16[8,72,1152]{2,1,0:T(8,128)(2,1)} %copy.60), calls=%async_computation.3 | async-start | bytes 2654208 | tf_op jit(solution)/shard_map/all_to_all | solution.py:196
  208.5 142.7 %all-gather.11.cloned.1.call-start = ((), (), s32[]{:S(2)}) async-start(), calls=%async_computation.15 | async-start | bytes 6635520 | tf_op jit(solution)/shard_map/all_gather | solution.py:201
  223.3 31.4 %collective-permute-start.22 = (bf16[160,2304]{1,0:T(8,128)(2,1)}, bf16[160,2304]{1,0:T(8,128)(2,1)}, u32[]{:S(2)}, u32[]{:S(2)}) collective-permute-start(bf16[160,2304]{1,0:T(8,128)(2,1)} %add_convert_fusion.11), channel_id=1, source_target_pairs={{0,8},{8,16},{16,24},{24,0},{1,25},{9,1},{17,9},{25,17},{2,10},{10... | collective-permute-start | bytes 2211848 | tf_op jit(solution)/shard_map/ppermute | solution.py:123
  226.8 27.9 %collective-permute-start.18 = (bf16[160,2304]{1,0:T(8,128)(2,1)}, bf16[160,2304]{1,0:T(8,128)(2,1)}, u32[]{:S(2)}, u32[]{:S(2)}) collective-permute-start(bf16[160,2304]{1,0:T(8,128)(2,1)} %slice.521), channel_id=1, source_target_pairs={{0,1},{1,0},{2,3},{3,2},{4,5},{5,4},{6,7},{7,6},{8,9},{9,8},{10,11... | collective-permute-start | bytes 2211848 | tf_op jit(solution)/shard_map/ppermute | solution.py:28
  229.7 34.1 %collective-permute-start.17 = (bf16[160,2304]{1,0:T(8,128)(2,1)}, bf16[160,2304]{1,0:T(8,128)(2,1)}, u32[]{:S(2)}, u32[]{:S(2)}) collective-permute-start(bf16[160,2304]{1,0:T(8,128)(2,1)} %slice.518), channel_id=1, source_target_pairs={{0,1},{1,0},{2,3},{3,2},{4,5},{5,4},{6,7},{7,6},{8,9},{9,8},{10,11... | collective-permute-start | bytes 2211848 | tf_op jit(solution)/shard_map/ppermute | solution.py:28
  284.2 364.4 %reduce-scatter.7.cloned.1.call-start = ((), (), s32[]{:S(2)}) async-start(), calls=%async_computation.16 | async-start | bytes 6635520 | tf_op jit(solution)/shard_map/reduce_scatter | solution.py:205
  284.2 20.0 %collective-permute-start.24 = (bf16[160,2304]{1,0:T(8,128)(2,1)S(1)}, bf16[160,2304]{1,0:T(8,128)(2,1)S(1)}, u32[]{:S(2)}, u32[]{:S(2)}) collective-permute-start(bf16[160,2304]{1,0:T(8,128)(2,1)S(1)} %get-tuple-element.227), channel_id=1, source_target_pairs={{0,8},{8,16},{16,24},{24,0},{1,25},{9,1},{17,9},{25,17},{2,10},{10... | collective-permute-start | bytes 2211848 | tf_op jit(solution)/shard_map/ppermute | solution.py:123
  364.0 19.9 %collective-permute-start.33 = (bf16[160,2304]{1,0:T(8,128)(2,1)S(1)}, bf16[160,2304]{1,0:T(8,128)(2,1)S(1)}, u32[]{:S(2)}, u32[]{:S(2)}) collective-permute-start(bf16[160,2304]{1,0:T(8,128)(2,1)S(1)} %slice.549), channel_id=1, source_target_pairs={{0,1},{1,0},{2,3},{3,2},{4,5},{5,4},{6,7},{7,6},{8,9},{9,8},{10,11... | collective-permute-start | bytes 2211848 | tf_op jit(solution)/shard_map/ppermute | solution.py:28
  371.5 31.4 %collective-permute-start.32 = (bf16[160,2304]{1,0:T(8,128)(2,1)S(1)}, bf16[160,2304]{1,0:T(8,128)(2,1)S(1)}, u32[]{:S(2)}, u32[]{:S(2)}) collective-permute-start(bf16[160,2304]{1,0:T(8,128)(2,1)S(1)} %slice.547), channel_id=1, source_target_pairs={{0,1},{1,0},{2,3},{3,2},{4,5},{5,4},{6,7},{7,6},{8,9},{9,8},{10,11... | collective-permute-start | bytes 2211848 | tf_op jit(solution)/shard_map/ppermute | solution.py:28
  425.6 20.7 %collective-permute-start.38 = (bf16[160,2304]{1,0:T(8,128)(2,1)S(1)}, bf16[160,2304]{1,0:T(8,128)(2,1)S(1)}, u32[]{:S(2)}, u32[]{:S(2)}) collective-permute-start(bf16[160,2304]{1,0:T(8,128)(2,1)S(1)} %get-tuple-element.224), channel_id=1, source_target_pairs={{0,8},{8,16},{16,24},{24,0},{1,25},{9,1},{17,9},{25,17},{2,10},{10... | collective-permute-start | bytes 2211848 | tf_op jit(solution)/shard_map/ppermute | solution.py:123
  506.4 142.2 %reduce-scatter.9.cloned.1.call-start = ((), (), s32[]{:S(2)}) async-start(), calls=%async_computation.17 | async-start | bytes 6635520 | tf_op jit(solution)/shard_map/reduce_scatter | solution.py:205
  531.8 200.5 %reduce-scatter.11.cloned.1.call-start = ((), (), s32[]{:S(2)}) async-start(), calls=%async_computation.18 | async-start | bytes 6635520 | tf_op jit(solution)/shard_map/reduce_scatter | solution.py:205
  544.5 22.8 %collective-permute-start.40 = (bf16[160,2304]{1,0:T(8,128)(2,1)}, bf16[160,2304]{1,0:T(8,128)(2,1)S(1)}, u32[]{:S(2)}, u32[]{:S(2)}) collective-permute-start(bf16[160,2304]{1,0:T(8,128)(2,1)} %slice.446), channel_id=1, source_target_pairs={{0,1},{1,0},{2,3},{3,2},{4,5},{5,4},{6,7},{7,6},{8,9},{9,8},{10,11... | collective-permute-start | bytes 2211848 | tf_op jit(solution)/shard_map/ppermute | solution.py:28
  593.4 23.9 %collective-permute-start.59 = (f32[8,144]{1,0:T(8,128)S(1)}, f32[8,144]{1,0:T(8,128)S(1)}, u32[]{:S(2)}, u32[]{:S(2)}) collective-permute-start(f32[8,144]{1,0:T(8,128)S(1)} %get-tuple-element.269), channel_id=1, source_target_pairs={{0,24},{8,0},{16,8},{24,16},{1,25},{9,1},{17,9},{25,17},{2,26},{10... | collective-permute-start | bytes 13832 | tf_op jit(solution)/shard_map/ppermute | solution.py:33
  596.1 21.2 %collective-permute-start.61 = (f32[8,144]{1,0:T(8,128)S(1)}, f32[8,144]{1,0:T(8,128)S(1)}, u32[]{:S(2)}, u32[]{:S(2)}) collective-permute-start(f32[8,144]{1,0:T(8,128)S(1)} %get-tuple-element.270), channel_id=1, source_target_pairs={{0,8},{8,16},{16,24},{24,0},{1,9},{9,17},{17,25},{25,1},{2,10},{10... | collective-permute-start | bytes 13832 | tf_op jit(solution)/shard_map/ppermute | solution.py:33
  596.1 21.2 %collective-permute-start.60 = (f32[8,144]{1,0:T(8,128)S(1)}, f32[8,144]{1,0:T(8,128)S(1)}, u32[]{:S(2)}, u32[]{:S(2)}) collective-permute-start(f32[8,144]{1,0:T(8,128)S(1)} %get-tuple-element.271), channel_id=1, source_target_pairs={{0,16},{8,24},{16,0},{24,8},{1,17},{9,25},{17,1},{25,9},{2,18},{10... | collective-permute-start | bytes 13832 | tf_op jit(solution)/shard_map/ppermute | solution.py:33
  596.7 20.6 %collective-permute-start.54 = (bf16[160,2304]{1,0:T(8,128)(2,1)}, bf16[160,2304]{1,0:T(8,128)(2,1)S(1)}, u32[]{:S(2)}, u32[]{:S(2)}) collective-permute-start(bf16[160,2304]{1,0:T(8,128)(2,1)} %collective-permute-done.52), channel_id=1, source_target_pairs={{0,8},{8,16},{16,24},{24,0},{1,25},{9,1},{17,9},{25,17},{2,10},{10... | collective-permute-start | bytes 2211848 | tf_op jit(solution)/shard_map/ppermute | solution.py:123
  621.1 20.6 %collective-permute-start.63 = (f32[2,144]{1,0:T(2,128)S(1)}, f32[2,144]{1,0:T(2,128)S(1)}, u32[]{:S(2)}, u32[]{:S(2)}) collective-permute-start(f32[2,144]{1,0:T(2,128)S(1)} %slice.609), channel_id=1, source_target_pairs={{0,2},{2,0},{1,3},{3,1},{4,6},{6,4},{5,7},{7,5},{8,10},{10,8},{9,1... | collective-permute-start | bytes 3464 | tf_op jit(solution)/shard_map/ppermute | solution.py:33
  648.6 43.2 %all-to-all-start.4 = ((bf16[8,72,1152]{2,1,0:T(8,128)(2,1)}), bf16[8,72,1152]{2,1,0:T(8,128)(2,1)}, u32[]{:S(2)}, u32[]{:S(2)}) async-start(bf16[8,72,1152]{2,1,0:T(8,128)(2,1)} %bitcast.139), calls=%async_computation.6 | async-start | bytes 2654208 | tf_op jit(solution)/shard_map/all_to_all | solution.py:196
  692.2 40.1 %all-to-all-start.5 = ((bf16[8,72,1152]{2,1,0:T(8,128)(2,1)}), bf16[8,72,1152]{2,1,0:T(8,128)(2,1)}, u32[]{:S(2)}, u32[]{:S(2)}) async-start(bf16[8,72,1152]{2,1,0:T(8,128)(2,1)} %bitcast.138), calls=%async_computation.7 | async-start | bytes 2654208 | tf_op jit(solution)/shard_map/all_to_all | solution.py:196
  696.6 128.0 %reduce-scatter.13.cloned.1.call-start = ((), (), s32[]{:S(2)}) async-start(), calls=%async_computation.19 | async-start | bytes 4423680 | tf_op jit(solution)/shard_map/reduce_scatter | solution.py:205
  699.7 31.1 %collective-permute-start.66 = (bf16[1280,256]{1,0:T(8,128)(2,1)S(1)}, bf16[1280,256]{1,0:T(8,128)(2,1)S(1)}, u32[]{:S(2)}, u32[]{:S(2)}) collective-permute-start(bf16[1280,256]{1,0:T(8,128)(2,1)S(1)} %get-tuple-element.234), channel_id=1, source_target_pairs={{2,0},{0,2},{6,4},{4,6},{3,1},{1,3},{7,5},{5,7},{10,8},{8,10},{14,... | collective-permute-start | bytes 1966088 | tf_op jit(solution)/shard_map/ppermute | solution.py:49
  700.7 30.1 %collective-permute-start.68 = (bf16[1280,256]{1,0:T(8,128)(2,1)S(1)}, bf16[1280,256]{1,0:T(8,128)(2,1)S(1)}, u32[]{:S(2)}, u32[]{:S(2)}) collective-permute-start(bf16[1280,256]{1,0:T(8,128)(2,1)S(1)} %get-tuple-element.235), channel_id=1, source_target_pairs={{6,0},{4,2},{2,4},{0,6},{7,1},{5,3},{3,5},{1,7},{14,8},{12,10},{10... | collective-permute-start | bytes 1966088 | tf_op jit(solution)/shard_map/ppermute | solution.py:49
  702.7 29.3 %collective-permute-start.67 = (bf16[1280,256]{1,0:T(8,128)(2,1)S(1)}, bf16[1280,256]{1,0:T(8,128)(2,1)S(1)}, u32[]{:S(2)}, u32[]{:S(2)}) collective-permute-start(bf16[1280,256]{1,0:T(8,128)(2,1)S(1)} %get-tuple-element.236), channel_id=1, source_target_pairs={{4,0},{6,2},{0,4},{2,6},{5,1},{7,3},{1,5},{3,7},{12,8},{14,10},{8,... | collective-permute-start | bytes 1966088 | tf_op jit(solution)/shard_map/ppermute | solution.py:49
  756.1 68.5 %all-to-all-start.6 = ((bf16[8,72,1152]{2,1,0:T(8,128)(2,1)}), bf16[8,72,1152]{2,1,0:T(8,128)(2,1)S(1)}, u32[]{:S(2)}, u32[]{:S(2)}) async-start(bf16[8,72,1152]{2,1,0:T(8,128)(2,1)} %bitcast.140), calls=%async_computation.9 | async-start | bytes 2654208 | tf_op jit(solution)/shard_map/all_to_all | solution.py:196
  764.0 38.8 %collective-permute-start.73 = (bf16[160,2304]{1,0:T(8,128)(2,1)S(1)}, bf16[160,2304]{1,0:T(8,128)(2,1)S(1)}, u32[]{:S(2)}, u32[]{:S(2)}) collective-permute-start(bf16[160,2304]{1,0:T(8,128)(2,1)S(1)} %copy-done.63), channel_id=1, source_target_pairs={{0,8},{8,16},{16,24},{24,0},{1,25},{9,1},{17,9},{25,17},{2,10},{10... | collective-permute-start | bytes 2211848 | tf_op jit(solution)/shard_map/ppermute | solution.py:123
  772.2 58.4 %collective-permute-start.70 = (bf16[160,2304]{1,0:T(8,128)(2,1)}, bf16[160,2304]{1,0:T(8,128)(2,1)}, u32[]{:S(2)}, u32[]{:S(2)}) collective-permute-start(bf16[160,2304]{1,0:T(8,128)(2,1)} %slice.619), channel_id=1, source_target_pairs={{0,1},{1,0},{2,3},{3,2},{4,5},{5,4},{6,7},{7,6},{8,9},{9,8},{10,11... | collective-permute-start | bytes 2211848 | tf_op jit(solution)/shard_map/ppermute | solution.py:28
  803.2 21.5 %collective-permute-start.74 = (bf16[160,2304]{1,0:T(8,128)(2,1)S(1)}, bf16[160,2304]{1,0:T(8,128)(2,1)}, u32[]{:S(2)}, u32[]{:S(2)}) collective-permute-start(bf16[160,2304]{1,0:T(8,128)(2,1)S(1)} %add_convert_fusion.2), channel_id=1, source_target_pairs={{0,8},{8,16},{16,24},{24,0},{1,25},{9,1},{17,9},{25,17},{2,10},{10... | collective-permute-start | bytes 2211848 | tf_op jit(solution)/shard_map/ppermute | solution.py:123
  817.6 48.3 %collective-permute-start.69 = (bf16[160,2304]{1,0:T(8,128)(2,1)}, bf16[160,2304]{1,0:T(8,128)(2,1)}, u32[]{:S(2)}, u32[]{:S(2)}) collective-permute-start(bf16[160,2304]{1,0:T(8,128)(2,1)} %slice.615), channel_id=1, source_target_pairs={{0,1},{1,0},{2,3},{3,2},{4,5},{5,4},{6,7},{7,6},{8,9},{9,8},{10,11... | collective-permute-start | bytes 2211848 | tf_op jit(solution)/shard_map/ppermute | solution.py:28
  824.6 41.3 %all-to-all-start.7 = ((bf16[8,72,768]{2,1,0:T(8,128)(2,1)}), bf16[8,72,768]{2,1,0:T(8,128)(2,1)S(1)}, u32[]{:S(2)}, u32[]{:S(2)}) async-start(bf16[8,72,768]{2,1,0:T(8,128)(2,1)} %bitcast.147), calls=%async_computation.10 | async-start | bytes 1769472 | tf_op jit(solution)/shard_map/all_to_all | solution.py:196
  832.5 33.4 %collective-permute-start.75 = (bf16[160,2304]{1,0:T(8,128)(2,1)S(1)}, bf16[160,2304]{1,0:T(8,128)(2,1)}, u32[]{:S(2)}, u32[]{:S(2)}) collective-permute-start(bf16[160,2304]{1,0:T(8,128)(2,1)S(1)} %add_convert_fusion.1), channel_id=1, source_target_pairs={{0,8},{8,16},{16,24},{24,0},{1,25},{9,1},{17,9},{25,17},{2,10},{10... | collective-permute-start | bytes 2211848 | tf_op jit(solution)/shard_map/ppermute | solution.py:123
  (181 other events, 1892.3 us)
Sparse Core Ops, SparseCore 0:
  46.6 46.9 all-gather.4
  150.3 62.1 all-gather.6
  214.3 61.9 all-gather.8
  284.3 60.9 all-gather.10
  506.5 61.0 reduce-scatter.6
  570.5 62.0 reduce-scatter.8
  635.5 61.9 reduce-scatter.10
  755.6 47.4 reduce-scatter.12
